TPU v7x, 128 devices: a whole 4x4x4 slice. The times are simulated.
128 devices in a mesh: blk: 16 (over y, z_lo, core), grp: 8 (over x, z_hi).
Axes of the slice: x: 4, y: 4, z: 4 (z_hi: 2, z_lo: 2; z = z_hi * 2 + z_lo), core: 2. Of those that a mesh axis runs over, the one named last changes fastest.
Arguments:
- image_embed: float32 [24576, 1152], P(('blk', 'grp')), may hold values from -0.3125 to 0.3125
- text_embed: float32 [24576, 1152], P(('blk', 'grp')), may hold values from -0.3125 to 0.3125
- scale_parameter: float32 [1], replicated, may hold values from 3 to 10
- logit_bias: float32 [1], replicated, may hold values from -5 to -2
Outputs:
- image_gradient_scaled: float32 [24576, 1152], P(('blk', 'grp'))
- text_gradient_scaled: float32 [24576, 1152], P(('blk', 'grp'))
- window_mean_loss: float32 [1], replicated
All inputs are finite; a program needn't handle non-finite values.
Results may differ from a plain program's by a relative error of at most 0.0004.
The roundings to bfloat16 on the way count: a program that leaves them out, or rounds other values in their place, can miss the bound.
Values may be sent and summed in bfloat16 or wider, within the bound.
No kernel may reach another device: no remote copies, remote signals or barrier semaphores. Data moves between devices by JAX's collectives and lax.ppermute only.
A program may use at most 128 MiB of HBM per device.

v0:
```python
import jax
import jax.numpy as jnp
from jax import lax
from jax.sharding import PartitionSpec as P

STEPS = 3


def shifted(value, axis, steps):
    count = lax.axis_size(axis)
    pairs = [(source, (source + steps) % count) for source in range(count)]
    return lax.ppermute(value, axis, pairs)


def local(image_embed, text_embed, scale_parameter, logit_bias):
    row_count = image_embed.shape[0]
    feature_width = image_embed.shape[1]
    group_size = lax.axis_size("grp")
    member = lax.axis_index("grp")
    block_rows = group_size * row_count
    inverse_temp = scale_parameter[0]
    bias_offset = logit_bias[0]
    image_b = image_embed.astype(jnp.bfloat16)
    text_b = text_embed.astype(jnp.bfloat16)
    own_start = member * row_count
    row_ids = lax.broadcasted_iota(jnp.int32, (row_count, block_rows), 0)
    col_ids = lax.broadcasted_iota(jnp.int32, (row_count, block_rows), 1)
    matches = (col_ids == row_ids + own_start).astype(jnp.float32)
    contract_last = (((1,), (1,)), ((), ()))
    contract_first = (((0,), (0,)), ((), ()))
    moving = lax.all_gather(text_b, "grp", axis=0, tiled=True)
    image_running_sum = jnp.zeros((row_count, feature_width), jnp.float32)
    loss_local = jnp.zeros((), jnp.float32)
    loop_state = image_running_sum
    for turn_index in range(STEPS):
        if turn_index > 0:
            moving = shifted(moving, "blk", 1)
        similarity_matrix = lax.dot_general(
            image_b, moving, contract_last, preferred_element_type=jnp.float32
        )
        pair_logits = inverse_temp * similarity_matrix + bias_offset
        if turn_index == 0:
            weights_full = jax.nn.sigmoid(pair_logits) - matches
            signed = pair_logits - 2.0 * matches * pair_logits
        else:
            weights_full = jax.nn.sigmoid(pair_logits)
            signed = pair_logits
        loss_local = loss_local + jnp.sum(jax.nn.softplus(signed))
        weights = weights_full.astype(jnp.bfloat16)
        image_running_sum = image_running_sum + jnp.dot(
            weights, moving, preferred_element_type=jnp.float32
        )
        grad_term = lax.dot_general(
            weights, image_b, contract_first, preferred_element_type=jnp.float32
        )
        if turn_index == 0:
            loop_state = grad_term
        else:
            loop_state = shifted(loop_state, "blk", 1) + grad_term
    loop_state = lax.psum_scatter(loop_state, "grp", scatter_dimension=0, tiled=True)
    loop_state = shifted(loop_state, "blk", 1 - STEPS)
    loss_total = lax.psum(loss_local, ("blk", "grp"))
    pair_count = row_count * group_size * lax.axis_size("blk") * STEPS * block_rows
    window_mean_loss = (loss_total / pair_count).reshape(1)
    return (inverse_temp * image_running_sum, inverse_temp * loop_state, window_mean_loss)


def solution(mesh):
    placed = (P(("blk", "grp"), None), P(("blk", "grp"), None), P(), P())
    return jax.shard_map(
        local,
        mesh=mesh,
        in_specs=placed,
        out_specs=(P(("blk", "grp"), None), P(("blk", "grp"), None), P()),
        check_vma=False,
    )
```

profile of v0, /device:TPU:0, one launch (start us, length us, event | category | flops | bytes accessed | tf_op | source)
XLA Modules:
  0.0 530.9 jit_solution(16266445797292095406)
XLA Ops:
  7.2 2.0 convert_element_type.19
  10.0 0.1 convert_element_type.18
  10.7 69.1 %all-gather.2.cloned.1.call-done = bf16[1536,1152]{1,0:T(8,128)(2,1)} async-done(((bf16[192,1152]{1,0:T(8,128)(2,1)}), bf16[1536,1152]{1,0:T(8,128)(2,1)}) %all-gather.2.cloned.1.call-update) | async-done | bytes 3538960 | tf_op jit(solution)/shard_map/all_gather | solution.py:31
  79.8 4.5 fusion.4
  84.3 1.5 fusion.8
  85.8 0.1 collective-permute-start.2
  85.9 0.4 copy-done.3
  86.3 0.3 collective-permute-start
  86.7 118.1 %collective-permute-done = bf16[1536,1152]{1,0:T(8,128)(2,1)S(1)} collective-permute-done((bf16[1536,1152]{1,0:T(8,128)(2,1)S(1)}, bf16[1536,1152]{1,0:T(8,128)(2,1)S(1)}, u32[]{:S(2)}, u32[]{:S(2)}) %collective-permute-start) | collective-permute-done | bytes 3538976 | tf_op jit(solution)/shard_map/ppermute | solution.py:12
  204.7 2.5 fusion.5
  207.2 1.5 convolution_add_fusion
  208.7 0.1 collective-permute-start.3
  208.8 0.1 collective-permute-start.1
  208.9 118.7 %collective-permute-done.1 = bf16[1536,1152]{1,0:T(8,128)(2,1)S(1)} collective-permute-done((bf16[1536,1152]{1,0:T(8,128)(2,1)S(1)}, bf16[1536,1152]{1,0:T(8,128)(2,1)S(1)}, u32[]{:S(2)}, u32[]{:S(2)}) %collective-permute-start.1) | collective-permute-done | bytes 3538976 | tf_op jit(solution)/shard_map/ppermute | solution.py:12
  327.6 2.4 fusion.6
  330.0 1.4 fusion.7
  331.5 6.6 %add.74 = f32[1536,1152]{1,0:T(8,128)} add(f32[1536,1152]{1,0:T(8,128)} %collective-permute-done.3, f32[1536,1152]{1,0:T(8,128)S(1)} %fusion.7) | non-fusion elementwise | flops 1769472 | bytes 21233664 | tf_op jit(solution)/shard_map/add | solution.py:59
  338.1 4.0 fusion.9
  344.2 94.6 %reduce-scatter.2.cloned.1.call-done = f32[192,1152]{1,0:T(8,128)} async-done(((f32[1536,1152]{1,0:T(8,128)}), f32[192,1152]{1,0:T(8,128)}) %reduce-scatter.2.cloned.1.call-update) | async-done | bytes 884752 | tf_op jit(solution)/shard_map/reduce_scatter | solution.py:60
  438.8 2.9 collective-permute-start.4
  441.6 4.1 convolution_add_fusion.2
  445.8 71.4 %psum.7 = f32[]{:T(128)} all-reduce(f32[]{:T(128)S(6)} %add.79), channel_id=1, replica_groups=mesh['blk'=16,'grp'=8] {'blk','grp'}, use_global_device_ids=true, to_apply=%region_4.5 | all-reduce | flops 1 | bytes 8 | tf_op jit(solution)/shard_map/psum | solution.py:62
  517.8 4.1 fusion
  521.9 1.0 broadcast_multiply_fusion
  (19 shorter events, 0.1 us)
Async XLA Ops:
  7.2 2.8 copy-start.2
  7.2 72.6 %all-gather.2.cloned.1.call-start = ((), (), s32[]{:S(2)}) async-start(), calls=%async_computation.1 | async-start | bytes 3981312 | tf_op jit(solution)/shard_map/all_gather | solution.py:31
  9.3 429.5 %reduce-scatter.2.cloned.1.call-start = ((), (), s32[]{:S(2)}) async-start(), calls=%async_computation.2 | async-start | bytes 7962624 | tf_op jit(solution)/shard_map/reduce_scatter | solution.py:60
  84.3 2.0 copy-start.3
  85.8 121.4 %collective-permute-start.2 = (f32[1536,1152]{1,0:T(8,128)S(1)}, f32[1536,1152]{1,0:T(8,128)S(1)}, u32[]{:S(2)}, u32[]{:S(2)}) collective-permute-start(f32[1536,1152]{1,0:T(8,128)S(1)} %fusion.8), channel_id=1, source_target_pairs={{0,8},{8,16},{16,24},{24,32},{32,40},{40,48},{48,56},{56,64},{64,7... | collective-permute-start | bytes 21233672 | tf_op jit(solution)/shard_map/ppermute | solution.py:12
  86.3 118.4 %collective-permute-start = (bf16[1536,1152]{1,0:T(8,128)(2,1)S(1)}, bf16[1536,1152]{1,0:T(8,128)(2,1)S(1)}, u32[]{:S(2)}, u32[]{:S(2)}) collective-permute-start(bf16[1536,1152]{1,0:T(8,128)(2,1)S(1)} %copy-done.3), channel_id=1, source_target_pairs={{0,8},{8,16},{16,24},{24,32},{32,40},{40,48},{48,56},{56,64},{64,7... | collective-permute-start | bytes 10616840 | tf_op jit(solution)/shard_map/ppermute | solution.py:12
  204.7 4.0 copy-start.4
  207.2 1.5 copy-start
  208.7 122.8 %collective-permute-start.3 = (f32[1536,1152]{1,0:T(8,128)S(1)}, f32[1536,1152]{1,0:T(8,128)}, u32[]{:S(2)}, u32[]{:S(2)}) collective-permute-start(f32[1536,1152]{1,0:T(8,128)S(1)} %convolution_add_fusion), channel_id=1, source_target_pairs={{0,8},{8,16},{16,24},{24,32},{32,40},{40,48},{48,56},{56,64},{64,7... | collective-permute-start | bytes 21233672 | tf_op jit(solution)/shard_map/ppermute | solution.py:12
  208.8 118.8 %collective-permute-start.1 = (bf16[1536,1152]{1,0:T(8,128)(2,1)S(1)}, bf16[1536,1152]{1,0:T(8,128)(2,1)S(1)}, u32[]{:S(2)}, u32[]{:S(2)}) collective-permute-start(bf16[1536,1152]{1,0:T(8,128)(2,1)S(1)} %collective-permute-done), channel_id=1, source_target_pairs={{0,8},{8,16},{16,24},{24,32},{32,40},{40,48},{48,56},{56,64},{64,7... | collective-permute-start | bytes 10616840 | tf_op jit(solution)/shard_map/ppermute | solution.py:12
  327.6 2.4 copy-start.5
  338.1 103.5 %copy-start.1 = (f32[192,1536]{1,0:T(8,128)S(1)}, f32[192,1536]{1,0:T(8,128)}, u32[]{:S(2)}) copy-start(f32[192,1536]{1,0:T(8,128)} %copy-done) | copy-start | bytes 3538948
  438.8 83.2 %collective-permute-start.4 = (f32[192,1152]{1,0:T(8,128)}, f32[192,1152]{1,0:T(8,128)S(1)}, u32[]{:S(2)}, u32[]{:S(2)}) collective-permute-start(f32[192,1152]{1,0:T(8,128)} %reduce-scatter.2.cloned.1.call-done), channel_id=1, source_target_pairs={{0,112},{8,120},{16,0},{24,8},{32,16},{40,24},{48,32},{56,40},{64,... | collective-permute-start | bytes 2654216 | tf_op jit(solution)/shard_map/ppermute | solution.py:12
Sparse Core Ops, SparseCore 0:
  10.9 68.8 all-gather.1
  338.3 100.4 reduce-scatter.1
where the time goes:
time: 532 us; the launch traced here: 531 us
  waiting for transfers between devices  401 us (75%)
  blocking collectives  71.4 us (13%)
  matrix products  26 us (5%)
  between operations  19.2 us (4%)
  other arithmetic  9.71 us (2%)
    ppermute x5, waiting for transfers between devices, shifted(): return lax.ppermute(value, axis, pairs)  237 us
    reduce_scatter x1, waiting for transfers between devices, local(): lax.psum_scatter(loop_state, 'grp', scatter_dimension=0, tiled=True)  94.6 us
    psum x1, blocking collectives, local(): loss_total = lax.psum(loss_local, ('blk', 'grp'))  71.4 us
    all_gather x1, waiting for transfers between devices, local(): moving = lax.all_gather(text_b, 'grp', axis=0, tiled=True)  69.1 us
    dot_general x3, matrix products, local(): jnp.dot(weights, moving, preferred_element_type=jnp.float32)  12.3 us
  transfers between devices with their start and end apart: 7, of which 4 were waited for; matrix products, arithmetic and copies ran while one was open for 4% of the time, Pallas kernels for 0%

commit v1 on v0

v1 whole, which is shorter than its diff:
```python
import jax
import jax.numpy as jnp
from jax import lax
from jax.sharding import PartitionSpec as P

AXES = ("blk", "grp")
NY, NX = 4, 4
SEND_SCALE = 64.0


def place(y, z, core, x):
    z = z % 4
    return (((y % NY) * 2 + z % 2) * 2 + core % 2) * 8 + (x % NX) * 2 + z // 2


def route(move):
    pairs = []
    for y in range(NY):
        for z in range(4):
            for core in range(2):
                for x in range(NX):
                    pairs.append((place(y, z, core, x), place(*move(y, z, core, x))))
    return pairs


def along_x(k):
    return route(lambda y, z, core, x: (y, z, core, x + k))


def along_z(k):
    return route(lambda y, z, core, x: (y, z + k, core, x))


def along_y(k):
    return route(lambda y, z, core, x: (y + k, z, core, x))


def next_column(k, flip_zh, flip_core):
    def move(y, z, core, x):
        zh, zl = z // 2, z % 2
        column = (y * 2 + zl + k) % 8
        return column // 2, (zh ^ flip_zh) * 2 + column % 2, core ^ flip_core, x

    return route(move)


OTHER_CORE = route(lambda y, z, core, x: (y, z, core + 1, x))


def send(value, pairs):
    return lax.ppermute(value, AXES, pairs)


def total_over_devices(value):
    value = value + send(value, OTHER_CORE)
    for axis in (along_x, along_z, along_y):
        value = value + send(value, axis(1)) + send(value, axis(2)) + send(value, axis(3))
    return value


def local(image_embed, text_embed, scale_parameter, logit_bias):
    n = image_embed.shape[0]
    scale = scale_parameter[0]
    bias = logit_bias[0]
    core = lax.axis_index("blk") % 2
    image_b = image_embed.astype(jnp.bfloat16)
    text_b = text_embed.astype(jnp.bfloat16)

    text_z = send(text_b, along_z(2))
    far_a = send(text_b, next_column(1, 0, 1))
    far_b = send(text_b, next_column(1, 1, 1))
    image_l = send(image_b, along_x(1))
    image_r = send(image_b, along_x(-1))
    image_f = send(image_b, along_x(2))
    images = jnp.concatenate([image_b, image_l, image_r, image_f])
    text_0 = jnp.concatenate([text_b, text_z])
    far = jnp.concatenate([far_a, far_b])
    text_2 = send(far, OTHER_CORE)
    text_1 = jnp.where(core == 0, far, send(text_0, OTHER_CORE))

    contract_last = (((1,), (1,)), ((), ()))
    contract_first = (((0,), (0,)), ((), ()))
    loss = jnp.zeros((), jnp.float32)
    weights = []
    sums = []
    for s, text in enumerate((text_0, text_1, text_2)):
        logits = scale * lax.dot_general(
            images, text, contract_last, preferred_element_type=jnp.float32
        ) + bias
        probs = jax.nn.sigmoid(logits)
        signed = logits
        if s == 0:
            row = lax.broadcasted_iota(jnp.int32, logits.shape, 0)
            col = lax.broadcasted_iota(jnp.int32, logits.shape, 1)
            match = ((row == col) & (row < n)).astype(jnp.float32)
            probs = probs - match
            signed = logits - 2.0 * match * logits
        loss = loss + jnp.sum(jax.nn.softplus(signed))
        w = probs.astype(jnp.bfloat16)
        weights.append(w)
        sums.append(
            lax.dot_general(w, images, contract_first, preferred_element_type=jnp.float32)
        )
    loss_total = total_over_devices(jnp.broadcast_to(loss, (8, 128)))

    def narrow(value):
        return (value * SEND_SCALE).astype(jnp.float16)

    def wide(value):
        return value.astype(jnp.float32) * (1.0 / SEND_SCALE)

    sum_0, sum_1, sum_2 = sums
    swapped = send(sum_1, OTHER_CORE)
    sum_0 = sum_0 + jnp.where(core == 0, swapped, 0.0)
    sum_2 = sum_2 + jnp.where(core == 1, swapped, 0.0)
    back_z = send(narrow(sum_0[n:]), along_z(2))
    back_a = send(narrow(sum_2[:n]), next_column(-1, 0, 0))
    back_b = send(narrow(sum_2[n:]), next_column(-1, 1, 0))
    text_sum = sum_0[:n] + wide(back_z) + wide(back_a) + wide(back_b)

    image_sum = jnp.dot(
        jnp.concatenate(weights, axis=1),
        jnp.concatenate([text_0, text_1, text_2]),
        preferred_element_type=jnp.float32,
    )
    home_l = send(narrow(image_sum[n : 2 * n]), along_x(-1))
    home_r = send(narrow(image_sum[2 * n : 3 * n]), along_x(1))
    home_f = send(narrow(image_sum[3 * n :]), along_x(2))
    image_own = image_sum[:n] + wide(home_l) + wide(home_r) + wide(home_f)

    pair_count = 128 * n * 3 * 8 * n
    mean_loss = (loss_total[0, 0] / pair_count).reshape(1)
    return scale * image_own, scale * text_sum, mean_loss


def solution(mesh):
    placed = (P(("blk", "grp"), None), P(("blk", "grp"), None), P(), P())
    return jax.shard_map(
        local,
        mesh=mesh,
        in_specs=placed,
        out_specs=(P(("blk", "grp"), None), P(("blk", "grp"), None), P()),
        check_vma=False,
    )
```

time: 532 us -> 115 us (0.22)
  waiting for transfers between devices: 401 us -> 36 us
  blocking collectives: 71.4 us -> 0 us
  starting transfers between devices: 3.48 us -> 42.2 us
  between operations: 19.2 us -> 5.7 us
    ppermute x5 -> x25, waiting for transfers between devices: 237 us -> 36 us  [send(): return lax.ppermute(value, AXES, pairs)]
    reduce_scatter x1 -> x0, waiting for transfers between devices: 94.6 us -> none  [local(): lax.psum_scatter(loop_state, 'grp', scatter_dimension=0, tiled=True)]
    psum x1 -> x0, blocking collectives: 71.4 us -> none  [local(): loss_total = lax.psum(loss_local, ('blk', 'grp'))]
    all_gather x1 -> x0, waiting for transfers between devices: 69.1 us -> none  [local(): moving = lax.all_gather(text_b, 'grp', axis=0, tiled=True)]
    ppermute x5 -> x25, starting transfers between devices: 3.4 us -> 42.2 us  [send(): return lax.ppermute(value, AXES, pairs)]
    add x2 -> x4, other arithmetic: 6.64 us -> 0.02 us  [the longest x3 0.02 us: total_over_devices(): value + send(value, axis(1)) + send(value, axis(2)) + send(value, axis(3))]
    dot_general x9 -> x7, matrix products: 26 us -> 25.2 us  [the longest x3 12.8 us: local(): lax.dot_general(images, text, contract_last, preferred_element_type=jnp.f...]
  transfers between devices with their start and end apart: 7 -> 25, of which waited for: 4 -> 11; matrix products, arithmetic and copies ran while one was open for 4% -> 20% of each run, Pallas kernels for 0% -> 0%
where the time goes in v1:
time: 115 us; the launch traced here: 114 us
  starting transfers between devices  42.2 us (37%)
  waiting for transfers between devices  36 us (31%)
  matrix products  25.2 us (22%)
  between operations  5.7 us (5%)
  other arithmetic  4.45 us (4%)
    ppermute x25, starting transfers between devices, send(): return lax.ppermute(value, AXES, pairs)  42.2 us
    ppermute x25, waiting for transfers between devices, send(): return lax.ppermute(value, AXES, pairs)  36 us
    dot_general x3, matrix products, local(): lax.dot_general(images, text, contract_last, preferred_element_type=jnp.f...  12.8 us
    dot_general x3, matrix products, local(): lax.dot_general(w, images, contract_first, preferred_element_type=jnp.flo...  7.99 us
    dot_general x1, matrix products, local(): jnp.dot(jnp.concatenate(weights, axis=1), jnp.concatenate([text_0, text_1...  4.4 us
    mul x2, other arithmetic, local(): return (scale * image_own, scale * text_sum, mean_loss)  2.43 us
  transfers between devices with their start and end apart: 25, of which 11 were waited for; matrix products, arithmetic and copies ran while one was open for 20% of the time, Pallas kernels for 0%

profile of v1, /device:TPU:0, one launch (start us, length us, event | category | flops | bytes accessed | tf_op | source)
XLA Modules:
  0.0 114.2 jit_solution(2836084218885693404)
XLA Ops:
  1.9 4.0 %collective-permute-start.3 = (bf16[192,1152]{1,0:T(8,128)(2,1)S(1)}, bf16[192,1152]{1,0:T(8,128)(2,1)S(1)}, u32[]{:S(2)}, u32[]{:S(2)}) collective-permute-start(bf16[192,1152]{1,0:T(8,128)(2,1)S(1)} %convert_element_type.55), channel_id=1, source_target_pairs={{0,1},{2,3},{4,5},{6,7},{8,9},{10,11},{12,13},{14,15},{16,17},{18,... | collective-permute-start | bytes 1327112 | tf_op jit(solution)/shard_map/ppermute | solution.py:51
  7.4 3.1 %collective-permute-start.2 = (bf16[192,1152]{1,0:T(8,128)(2,1)S(1)}, bf16[192,1152]{1,0:T(8,128)(2,1)S(1)}, u32[]{:S(2)}, u32[]{:S(2)}) collective-permute-start(bf16[192,1152]{1,0:T(8,128)(2,1)S(1)} %convert_element_type.54), channel_id=1, source_target_pairs={{0,4},{2,6},{4,0},{6,2},{8,12},{10,14},{12,8},{14,10},{16,20},{18,... | collective-permute-start | bytes 1327112 | tf_op jit(solution)/shard_map/ppermute | solution.py:51
  13.0 4.0 %collective-permute-done.3 = bf16[192,1152]{1,0:T(8,128)(2,1)S(1)} collective-permute-done((bf16[192,1152]{1,0:T(8,128)(2,1)S(1)}, bf16[192,1152]{1,0:T(8,128)(2,1)S(1)}, u32[]{:S(2)}, u32[]{:S(2)}) %collective-permute-start.3) | collective-permute-done | bytes 442400 | tf_op jit(solution)/shard_map/ppermute | solution.py:51
  18.5 6.3 %collective-permute-done.4 = bf16[192,1152]{1,0:T(8,128)(2,1)S(1)} collective-permute-done((bf16[192,1152]{1,0:T(8,128)(2,1)S(1)}, bf16[192,1152]{1,0:T(8,128)(2,1)S(1)}, u32[]{:S(2)}, u32[]{:S(2)}) %collective-permute-start.4) | collective-permute-done | bytes 442400 | tf_op jit(solution)/shard_map/ppermute | solution.py:51
  24.9 2.8 %collective-permute-done.5 = bf16[192,1152]{1,0:T(8,128)(2,1)S(1)} collective-permute-done((bf16[192,1152]{1,0:T(8,128)(2,1)S(1)}, bf16[192,1152]{1,0:T(8,128)(2,1)S(1)}, u32[]{:S(2)}, u32[]{:S(2)}) %collective-permute-start.5) | collective-permute-done | bytes 442400 | tf_op jit(solution)/shard_map/ppermute | solution.py:51
  28.7 2.0 %collective-permute-done.1 = bf16[192,1152]{1,0:T(8,128)(2,1)} collective-permute-done((bf16[192,1152]{1,0:T(8,128)(2,1)S(1)}, bf16[192,1152]{1,0:T(8,128)(2,1)}, u32[]{:S(2)}, u32[]{:S(2)}) %collective-permute-start.1) | collective-permute-done | bytes 442400 | tf_op jit(solution)/shard_map/ppermute | solution.py:51
  30.6 4.3 %fusion.16 = (f32[]{:T(128)}, bf16[768,384]{0,1:T(8,128)(2,1)}) fusion(pred[768]{0:T(1024)(128)(4,1)S(1)} %iota_compare_fusion.1, f32[]{:T(128)} %bitcast.13, bf16[192,1152]{1,0:T(8,128)(2,1)S(1)} %collective-permute-done.3, bf16[192,1152]{1,0:T(8,128)(2,1)S(1)} %convert_element_type.55, bf16[192,1152]{1,0:T(8,128)(2,1)S(1)} %collective-permute-done.2, ...), kind=kOutput, calls=%fused_computation.26 | convolution fusion | flops 694222848 | bytes 3244812 | tf_op jit(solution)/shard_map/dot_general | solution.py:87
  35.1 4.0 %fusion.17 = (f32[]{:T(128)}, bf16[768,384]{0,1:T(8,128)(2,1)}) fusion(f32[]{:T(128)} %bitcast.15, bf16[384,1152]{1,0:T(8,128)(2,1)S(1)} %broadcast_select_fusion, bf16[192,1152]{1,0:T(8,128)(2,1)S(1)} %collective-permute-done.2, bf16[192,1152]{1,0:T(8,128)(2,1)} %collective-permute-done.1, bf16[192,1152]{1,0:T(8,128)(2,1)S(1)} %collective-permute-done, ...), kind=kOutput, calls=%fused_computation.27 | convolution fusion | flops 690388992 | bytes 3244044 | tf_op jit(solution)/shard_map/dot_general | solution.py:87
  40.3 4.5 %fusion.18 = (f32[]{:T(128)}, bf16[768,384]{0,1:T(8,128)(2,1)}) fusion(f32[]{:T(128)} %bitcast.14, bf16[384,1152]{1,0:T(8,128)(2,1)} %collective-permute-done.7, bf16[192,1152]{1,0:T(8,128)(2,1)S(1)} %collective-permute-done.2, bf16[192,1152]{1,0:T(8,128)(2,1)} %collective-permute-done.1, bf16[192,1152]{1,0:T(8,128)(2,1)} %copy-done.1, ...), kind=kOutput, calls=%fused_computation.28 | convolution fusion | flops 690388992 | bytes 3244044 | tf_op jit(solution)/shard_map/dot_general | solution.py:87
  45.5 3.3 %fusion.33 = f32[384,1152]{1,0:T(8,128)} fusion(bf16[768,384]{0,1:T(8,128)(2,1)} %get-tuple-element.13, bf16[192,1152]{1,0:T(8,128)(2,1)S(1)} %collective-permute-done.2, bf16[192,1152]{1,0:T(8,128)(2,1)} %collective-permute-done.1, bf16[192,1152]{1,0:T(8,128)(2,1)S(1)} %copy-done.2, bf16[192,1152]{1,0:T(8,128)(2,1)S(1)} %convert_element_type.54), kind=kOutput, calls=%fused_computation.64 | convolution fusion | flops 686555136 | bytes 4128768 | tf_op jit(solution)/shard_map/dot_general | solution.py:102
  49.3 2.6 %collective-permute-start.18 = (f32[8,128]{1,0:T(8,128)S(1)}, f32[8,128]{1,0:T(8,128)S(1)}, u32[]{:S(2)}, u32[]{:S(2)}) collective-permute-start(f32[8,128]{1,0:T(8,128)S(1)} %broadcast_add_fusion), channel_id=1, source_target_pairs={{0,6},{2,0},{4,2},{6,4},{8,14},{10,8},{12,10},{14,12},{16,22},{18,... | collective-permute-start | bytes 12296 | tf_op jit(solution)/shard_map/ppermute | solution.py:51
  53.6 3.5 %collective-permute-done.17 = f32[8,128]{1,0:T(8,128)S(1)} collective-permute-done((f32[8,128]{1,0:T(8,128)S(1)}, f32[8,128]{1,0:T(8,128)S(1)}, u32[]{:S(2)}, u32[]{:S(2)}) %collective-permute-start.17) | collective-permute-done | bytes 4128 | tf_op jit(solution)/shard_map/ppermute | solution.py:51
  57.6 9.6 %collective-permute-start.21 = (f32[8,128]{1,0:T(8,128)S(1)}, f32[8,128]{1,0:T(8,128)S(1)}, u32[]{:S(2)}, u32[]{:S(2)}) collective-permute-start(f32[8,128]{1,0:T(8,128)S(1)} %add_add_fusion.2), channel_id=1, source_target_pairs={{0,17},{2,19},{4,21},{6,23},{8,25},{10,27},{12,29},{14,31},{16,0},... | collective-permute-start | bytes 12296 | tf_op jit(solution)/shard_map/ppermute | solution.py:51
  68.2 4.4 %fusion = f32[768,1152]{1,0:T(8,128)S(1)} fusion(bf16[384,1152]{1,0:T(8,128)(2,1)} %collective-permute-done.7, bf16[384,1152]{1,0:T(8,128)(2,1)S(1)} %broadcast_select_fusion, bf16[192,1152]{1,0:T(8,128)(2,1)S(1)} %collective-permute-done.3, bf16[192,1152]{1,0:T(8,128)(2,1)S(1)} %convert_element_type.55, bf16[768,384]{0,1:T(8,128)(2,1)} %get-tuple-element.11, ...), kind=kOutput, calls=%fused_computation.5 | convolution fusion | flops 2054356992 | bytes 7962624 | tf_op jit(solution)/shard_map/dot_general | solution.py:121
  72.6 3.0 %collective-permute-start.24 = (f32[8,128]{1,0:T(8,128)S(1)}, f32[8,128]{1,0:T(8,128)S(1)}, u32[]{:S(2)}, u32[]{:S(2)}) collective-permute-start(f32[8,128]{1,0:T(8,128)S(1)} %add_add_fusion.1), channel_id=1, source_target_pairs={{0,96},{2,98},{4,100},{6,102},{8,104},{10,106},{12,108},{14,110},{... | collective-permute-start | bytes 12296 | tf_op jit(solution)/shard_map/ppermute | solution.py:51
  77.5 1.6 %collective-permute-start.10 = (f16[192,1152]{1,0:T(8,128)(2,1)S(1)}, f16[192,1152]{1,0:T(8,128)(2,1)S(1)}, u32[]{:S(2)}, u32[]{:S(2)}) collective-permute-start(f16[192,1152]{1,0:T(8,128)(2,1)S(1)} %get-tuple-element.4), channel_id=1, source_target_pairs={{0,4},{2,6},{4,0},{6,2},{8,12},{10,14},{12,8},{14,10},{16,20},{18,... | collective-permute-start | bytes 1327112 | tf_op jit(solution)/shard_map/ppermute | solution.py:51
  83.5 2.0 %convolution_add_fusion = f32[384,1152]{1,0:T(8,128)S(1)} fusion(bf16[768,384]{0,1:T(8,128)(2,1)S(1)} %copy-done.4, f32[384,1152]{1,0:T(8,128)} %collective-permute-done.11, pred[]{:T(512)S(6)} %eq.16, bf16[192,1152]{1,0:T(8,128)(2,1)S(1)} %collective-permute-done.2, bf16[192,1152]{1,0:T(8,128)(2,1)} %collective-permute-done.1, ...), kind=kOutput, calls=%fused_computation.3 | convolution fusion | flops 687439872 | bytes 5898241 | tf_op jit(solution)/shard_map/dot_general | solution.py:102
  85.7 4.1 %collective-permute-start.14 = (f16[192,1152]{1,0:T(8,128)(2,1)S(1)}, f16[192,1152]{1,0:T(8,128)(2,1)S(1)}, u32[]{:S(2)}, u32[]{:S(2)}) collective-permute-start(f16[192,1152]{1,0:T(8,128)(2,1)S(1)} %get-tuple-element.7), channel_id=1, source_target_pairs={{0,113},{2,115},{4,117},{6,119},{8,121},{10,123},{12,125},{14,127}... | collective-permute-start | bytes 1327112 | tf_op jit(solution)/shard_map/ppermute | solution.py:51
  90.2 2.6 %convolution_add_fusion.1 = f32[384,1152]{1,0:T(8,128)S(1)} fusion(bf16[768,384]{0,1:T(8,128)(2,1)S(1)} %copy-done.3, f32[384,1152]{1,0:T(8,128)} %collective-permute-done.11, pred[]{:T(512)S(6)} %eq.15, bf16[192,1152]{1,0:T(8,128)(2,1)S(1)} %collective-permute-done.2, bf16[192,1152]{1,0:T(8,128)(2,1)} %collective-permute-done.1, ...), kind=kOutput, calls=%fused_computation.4 | convolution fusion | flops 687439872 | bytes 5898241 | tf_op jit(solution)/shard_map/dot_general | solution.py:102
  92.9 2.1 %collective-permute-start.12 = (f16[192,1152]{1,0:T(8,128)(2,1)S(1)}, f16[192,1152]{1,0:T(8,128)(2,1)S(1)}, u32[]{:S(2)}, u32[]{:S(2)}) collective-permute-start(f16[192,1152]{1,0:T(8,128)(2,1)S(1)} %fusion.22), channel_id=1, source_target_pairs={{0,1},{2,3},{4,5},{6,7},{8,9},{10,11},{12,13},{14,15},{16,17},{18,... | collective-permute-start | bytes 1327112 | tf_op jit(solution)/shard_map/ppermute | solution.py:51
  95.0 2.6 %collective-permute-done.9 = f16[192,1152]{1,0:T(8,128)(2,1)S(1)} collective-permute-done((f16[192,1152]{1,0:T(8,128)(2,1)S(1)}, f16[192,1152]{1,0:T(8,128)(2,1)S(1)}, u32[]{:S(2)}, u32[]{:S(2)}) %collective-permute-start.9) | collective-permute-done | bytes 442400 | tf_op jit(solution)/shard_map/ppermute | solution.py:51
  98.8 1.7 %collective-permute-done.14 = f16[192,1152]{1,0:T(8,128)(2,1)S(1)} collective-permute-done((f16[192,1152]{1,0:T(8,128)(2,1)S(1)}, f16[192,1152]{1,0:T(8,128)(2,1)S(1)}, u32[]{:S(2)}, u32[]{:S(2)}) %collective-permute-start.14) | collective-permute-done | bytes 442400 | tf_op jit(solution)/shard_map/ppermute | solution.py:51
  100.5 5.5 %collective-permute-done.13 = f16[192,1152]{1,0:T(8,128)(2,1)S(1)} collective-permute-done((f16[192,1152]{1,0:T(8,128)(2,1)S(1)}, f16[192,1152]{1,0:T(8,128)(2,1)S(1)}, u32[]{:S(2)}, u32[]{:S(2)}) %collective-permute-start.13) | collective-permute-done | bytes 442400 | tf_op jit(solution)/shard_map/ppermute | solution.py:51
  106.0 5.9 %collective-permute-done.12 = f16[192,1152]{1,0:T(8,128)(2,1)S(1)} collective-permute-done((f16[192,1152]{1,0:T(8,128)(2,1)S(1)}, f16[192,1152]{1,0:T(8,128)(2,1)S(1)}, u32[]{:S(2)}, u32[]{:S(2)}) %collective-permute-start.12) | collective-permute-done | bytes 442400 | tf_op jit(solution)/shard_map/ppermute | solution.py:51
  (61 shorter events, 18.7 us)
Async XLA Ops:
  1.9 15.0 %collective-permute-start.3 = (bf16[192,1152]{1,0:T(8,128)(2,1)S(1)}, bf16[192,1152]{1,0:T(8,128)(2,1)S(1)}, u32[]{:S(2)}, u32[]{:S(2)}) collective-permute-start(bf16[192,1152]{1,0:T(8,128)(2,1)S(1)} %convert_element_type.55), channel_id=1, source_target_pairs={{0,1},{2,3},{4,5},{6,7},{8,9},{10,11},{12,13},{14,15},{16,17},{18,... | collective-permute-start | bytes 1327112 | tf_op jit(solution)/shard_map/ppermute | solution.py:51
  6.0 18.9 %collective-permute-start.4 = (bf16[192,1152]{1,0:T(8,128)(2,1)S(1)}, bf16[192,1152]{1,0:T(8,128)(2,1)S(1)}, u32[]{:S(2)}, u32[]{:S(2)}) collective-permute-start(bf16[192,1152]{1,0:T(8,128)(2,1)S(1)} %convert_element_type.55), channel_id=1, source_target_pairs={{0,24},{2,26},{4,28},{6,30},{8,16},{10,18},{12,20},{14,22},{16,40}... | collective-permute-start | bytes 1327112 | tf_op jit(solution)/shard_map/ppermute | solution.py:51
  6.2 21.6 %collective-permute-start.5 = (bf16[192,1152]{1,0:T(8,128)(2,1)S(1)}, bf16[192,1152]{1,0:T(8,128)(2,1)S(1)}, u32[]{:S(2)}, u32[]{:S(2)}) collective-permute-start(bf16[192,1152]{1,0:T(8,128)(2,1)S(1)} %convert_element_type.55), channel_id=1, source_target_pairs={{0,25},{2,27},{4,29},{6,31},{8,17},{10,19},{12,21},{14,23},{16,41}... | collective-permute-start | bytes 1327112 | tf_op jit(solution)/shard_map/ppermute | solution.py:51
  7.4 21.2 %collective-permute-start.2 = (bf16[192,1152]{1,0:T(8,128)(2,1)S(1)}, bf16[192,1152]{1,0:T(8,128)(2,1)S(1)}, u32[]{:S(2)}, u32[]{:S(2)}) collective-permute-start(bf16[192,1152]{1,0:T(8,128)(2,1)S(1)} %convert_element_type.54), channel_id=1, source_target_pairs={{0,4},{2,6},{4,0},{6,2},{8,12},{10,14},{12,8},{14,10},{16,20},{18,... | collective-permute-start | bytes 1327112 | tf_op jit(solution)/shard_map/ppermute | solution.py:51
  10.5 20.1 %collective-permute-start.1 = (bf16[192,1152]{1,0:T(8,128)(2,1)S(1)}, bf16[192,1152]{1,0:T(8,128)(2,1)}, u32[]{:S(2)}, u32[]{:S(2)}) collective-permute-start(bf16[192,1152]{1,0:T(8,128)(2,1)S(1)} %convert_element_type.54), channel_id=1, source_target_pairs={{0,6},{2,0},{4,2},{6,4},{8,14},{10,8},{12,10},{14,12},{16,22},{18,... | collective-permute-start | bytes 1327112 | tf_op jit(solution)/shard_map/ppermute | solution.py:51
  17.0 13.6 %collective-permute-start = (bf16[192,1152]{1,0:T(8,128)(2,1)S(1)}, bf16[192,1152]{1,0:T(8,128)(2,1)S(1)}, u32[]{:S(2)}, u32[]{:S(2)}) collective-permute-start(bf16[192,1152]{1,0:T(8,128)(2,1)S(1)} %convert_element_type.54), channel_id=1, source_target_pairs={{0,2},{2,4},{4,6},{6,0},{8,10},{10,12},{12,14},{14,8},{16,18},{18,... | collective-permute-start | bytes 1327112 | tf_op jit(solution)/shard_map/ppermute | solution.py:51
  24.9 10.1 %collective-permute-start.6 = (bf16[384,1152]{1,0:T(8,128)(2,1)S(1)}, bf16[384,1152]{1,0:T(8,128)(2,1)S(1)}, u32[]{:S(2)}, u32[]{:S(2)}) collective-permute-start(bf16[384,1152]{1,0:T(8,128)(2,1)S(1)} %pad_maximum_fusion.1), channel_id=1, source_target_pairs={{0,8},{2,10},{4,12},{6,14},{8,0},{10,2},{12,4},{14,6},{16,24},{18,... | collective-permute-start | bytes 2654216 | tf_op jit(solution)/shard_map/ppermute | solution.py:51
  27.8 12.6 %collective-permute-start.7 = (bf16[384,1152]{1,0:T(8,128)(2,1)S(1)}, bf16[384,1152]{1,0:T(8,128)(2,1)}, u32[]{:S(2)}, u32[]{:S(2)}) collective-permute-start(bf16[384,1152]{1,0:T(8,128)(2,1)S(1)} %constant_dynamic-update-slice_fusion), channel_id=1, source_target_pairs={{0,8},{2,10},{4,12},{6,14},{8,0},{10,2},{12,4},{14,6},{16,24},{18,... | collective-permute-start | bytes 2654216 | tf_op jit(solution)/shard_map/ppermute | solution.py:51
  48.8 34.7 %collective-permute-start.11 = (f32[384,1152]{1,0:T(8,128)}, f32[384,1152]{1,0:T(8,128)}, u32[]{:S(2)}, u32[]{:S(2)}) collective-permute-start(f32[384,1152]{1,0:T(8,128)} %fusion.33), channel_id=1, source_target_pairs={{0,8},{2,10},{4,12},{6,14},{8,0},{10,2},{12,4},{14,6},{16,24},{18,... | collective-permute-start | bytes 5308424 | tf_op jit(solution)/shard_map/ppermute | solution.py:51
  49.3 4.2 %collective-permute-start.18 = (f32[8,128]{1,0:T(8,128)S(1)}, f32[8,128]{1,0:T(8,128)S(1)}, u32[]{:S(2)}, u32[]{:S(2)}) collective-permute-start(f32[8,128]{1,0:T(8,128)S(1)} %broadcast_add_fusion), channel_id=1, source_target_pairs={{0,6},{2,0},{4,2},{6,4},{8,14},{10,8},{12,10},{14,12},{16,22},{18,... | collective-permute-start | bytes 12296 | tf_op jit(solution)/shard_map/ppermute | solution.py:51
  52.0 5.1 %collective-permute-start.17 = (f32[8,128]{1,0:T(8,128)S(1)}, f32[8,128]{1,0:T(8,128)S(1)}, u32[]{:S(2)}, u32[]{:S(2)}) collective-permute-start(f32[8,128]{1,0:T(8,128)S(1)} %broadcast_add_fusion), channel_id=1, source_target_pairs={{0,4},{2,6},{4,0},{6,2},{8,12},{10,14},{12,8},{14,10},{16,20},{18,... | collective-permute-start | bytes 12296 | tf_op jit(solution)/shard_map/ppermute | solution.py:51
  52.8 4.8 %collective-permute-start.16 = (f32[8,128]{1,0:T(8,128)S(1)}, f32[8,128]{1,0:T(8,128)S(1)}, u32[]{:S(2)}, u32[]{:S(2)}) collective-permute-start(f32[8,128]{1,0:T(8,128)S(1)} %broadcast_add_fusion), channel_id=1, source_target_pairs={{0,2},{2,4},{4,6},{6,0},{8,10},{10,12},{12,14},{14,8},{16,18},{18,... | collective-permute-start | bytes 12296 | tf_op jit(solution)/shard_map/ppermute | solution.py:51
  57.6 15.0 %collective-permute-start.21 = (f32[8,128]{1,0:T(8,128)S(1)}, f32[8,128]{1,0:T(8,128)S(1)}, u32[]{:S(2)}, u32[]{:S(2)}) collective-permute-start(f32[8,128]{1,0:T(8,128)S(1)} %add_add_fusion.2), channel_id=1, source_target_pairs={{0,17},{2,19},{4,21},{6,23},{8,25},{10,27},{12,29},{14,31},{16,0},... | collective-permute-start | bytes 12296 | tf_op jit(solution)/shard_map/ppermute | solution.py:51
  67.2 5.4 %collective-permute-start.20 = (f32[8,128]{1,0:T(8,128)S(1)}, f32[8,128]{1,0:T(8,128)S(1)}, u32[]{:S(2)}, u32[]{:S(2)}) collective-permute-start(f32[8,128]{1,0:T(8,128)S(1)} %add_add_fusion.2), channel_id=1, source_target_pairs={{0,1},{2,3},{4,5},{6,7},{8,9},{10,11},{12,13},{14,15},{16,17},{18,... | collective-permute-start | bytes 12296 | tf_op jit(solution)/shard_map/ppermute | solution.py:51
  67.2 5.4 %collective-permute-start.19 = (f32[8,128]{1,0:T(8,128)S(1)}, f32[8,128]{1,0:T(8,128)S(1)}, u32[]{:S(2)}, u32[]{:S(2)}) collective-permute-start(f32[8,128]{1,0:T(8,128)S(1)} %add_add_fusion.2), channel_id=1, source_target_pairs={{0,16},{2,18},{4,20},{6,22},{8,24},{10,26},{12,28},{14,30},{16,1},... | collective-permute-start | bytes 12296 | tf_op jit(solution)/shard_map/ppermute | solution.py:51
  72.6 6.5 %collective-permute-start.24 = (f32[8,128]{1,0:T(8,128)S(1)}, f32[8,128]{1,0:T(8,128)S(1)}, u32[]{:S(2)}, u32[]{:S(2)}) collective-permute-start(f32[8,128]{1,0:T(8,128)S(1)} %add_add_fusion.1), channel_id=1, source_target_pairs={{0,96},{2,98},{4,100},{6,102},{8,104},{10,106},{12,108},{14,110},{... | collective-permute-start | bytes 12296 | tf_op jit(solution)/shard_map/ppermute | solution.py:51
  75.7 5.1 %collective-permute-start.23 = (f32[8,128]{1,0:T(8,128)S(1)}, f32[8,128]{1,0:T(8,128)S(1)}, u32[]{:S(2)}, u32[]{:S(2)}) collective-permute-start(f32[8,128]{1,0:T(8,128)S(1)} %add_add_fusion.1), channel_id=1, source_target_pairs={{0,64},{2,66},{4,68},{6,70},{8,72},{10,74},{12,76},{14,78},{16,80}... | collective-permute-start | bytes 12296 | tf_op jit(solution)/shard_map/ppermute | solution.py:51
  76.3 6.1 %collective-permute-start.22 = (f32[8,128]{1,0:T(8,128)S(1)}, f32[8,128]{1,0:T(8,128)S(1)}, u32[]{:S(2)}, u32[]{:S(2)}) collective-permute-start(f32[8,128]{1,0:T(8,128)S(1)} %add_add_fusion.1), channel_id=1, source_target_pairs={{0,32},{2,34},{4,36},{6,38},{8,40},{10,42},{12,44},{14,46},{16,48}... | collective-permute-start | bytes 12296 | tf_op jit(solution)/shard_map/ppermute | solution.py:51
  77.5 15.4 %collective-permute-start.10 = (f16[192,1152]{1,0:T(8,128)(2,1)S(1)}, f16[192,1152]{1,0:T(8,128)(2,1)S(1)}, u32[]{:S(2)}, u32[]{:S(2)}) collective-permute-start(f16[192,1152]{1,0:T(8,128)(2,1)S(1)} %get-tuple-element.4), channel_id=1, source_target_pairs={{0,4},{2,6},{4,0},{6,2},{8,12},{10,14},{12,8},{14,10},{16,20},{18,... | collective-permute-start | bytes 1327112 | tf_op jit(solution)/shard_map/ppermute | solution.py:51
  79.1 18.5 %collective-permute-start.9 = (f16[192,1152]{1,0:T(8,128)(2,1)S(1)}, f16[192,1152]{1,0:T(8,128)(2,1)S(1)}, u32[]{:S(2)}, u32[]{:S(2)}) collective-permute-start(f16[192,1152]{1,0:T(8,128)(2,1)S(1)} %get-tuple-element.5), channel_id=1, source_target_pairs={{0,2},{2,4},{4,6},{6,0},{8,10},{10,12},{12,14},{14,8},{16,18},{18,... | collective-permute-start | bytes 1327112 | tf_op jit(solution)/shard_map/ppermute | solution.py:51
  80.8 16.8 %collective-permute-start.8 = (f16[192,1152]{1,0:T(8,128)(2,1)S(1)}, f16[192,1152]{1,0:T(8,128)(2,1)S(1)}, u32[]{:S(2)}, u32[]{:S(2)}) collective-permute-start(f16[192,1152]{1,0:T(8,128)(2,1)S(1)} %get-tuple-element.3), channel_id=1, source_target_pairs={{0,6},{2,0},{4,2},{6,4},{8,14},{10,8},{12,10},{14,12},{16,22},{18,... | collective-permute-start | bytes 1327112 | tf_op jit(solution)/shard_map/ppermute | solution.py:51
  85.7 14.8 %collective-permute-start.14 = (f16[192,1152]{1,0:T(8,128)(2,1)S(1)}, f16[192,1152]{1,0:T(8,128)(2,1)S(1)}, u32[]{:S(2)}, u32[]{:S(2)}) collective-permute-start(f16[192,1152]{1,0:T(8,128)(2,1)S(1)} %get-tuple-element.7), channel_id=1, source_target_pairs={{0,113},{2,115},{4,117},{6,119},{8,121},{10,123},{12,125},{14,127}... | collective-permute-start | bytes 1327112 | tf_op jit(solution)/shard_map/ppermute | solution.py:51
  89.9 16.1 %collective-permute-start.13 = (f16[192,1152]{1,0:T(8,128)(2,1)S(1)}, f16[192,1152]{1,0:T(8,128)(2,1)S(1)}, u32[]{:S(2)}, u32[]{:S(2)}) collective-permute-start(f16[192,1152]{1,0:T(8,128)(2,1)S(1)} %get-tuple-element.6), channel_id=1, source_target_pairs={{0,112},{2,114},{4,116},{6,118},{8,120},{10,122},{12,124},{14,126}... | collective-permute-start | bytes 1327112 | tf_op jit(solution)/shard_map/ppermute | solution.py:51
  92.9 19.0 %collective-permute-start.12 = (f16[192,1152]{1,0:T(8,128)(2,1)S(1)}, f16[192,1152]{1,0:T(8,128)(2,1)S(1)}, u32[]{:S(2)}, u32[]{:S(2)}) collective-permute-start(f16[192,1152]{1,0:T(8,128)(2,1)S(1)} %fusion.22), channel_id=1, source_target_pairs={{0,1},{2,3},{4,5},{6,7},{8,9},{10,11},{12,13},{14,15},{16,17},{18,... | collective-permute-start | bytes 1327112 | tf_op jit(solution)/shard_map/ppermute | solution.py:51
  (6 other events, 35.8 us)

commit v2 on v1

v2 whole, which is shorter than its diff:
```python
import functools

import jax
import jax.numpy as jnp
from jax import lax
from jax.experimental import pallas as pl
from jax.experimental.pallas import tpu as pltpu
from jax.sharding import Mesh
from jax.sharding import PartitionSpec as P

AXES = ("y", "z_lo", "core", "x", "z_hi")
CHIPS = ("y", "z_lo", "x", "z_hi")
NY, NX = 4, 4
DEVICES = 128
CHIP_COUNT = 64
SEND_SCALE = 64.0
LAST = (((1,), (1,)), ((), ()))
FIRST = (((0,), (0,)), ((), ()))
PLAIN = (((1,), (0,)), ((), ()))
VMEM_BYTES = 16 * 1024 * 1024


def place(y, z, core, x):
    z = z % 4
    return (((y % NY) * 2 + z % 2) * 2 + core % 2) * 8 + (x % NX) * 2 + z // 2


def route(move):
    pairs = []
    for y in range(NY):
        for z in range(4):
            for core in range(2):
                for x in range(NX):
                    pairs.append((place(y, z, core, x), place(*move(y, z, core, x))))
    return pairs


def along_x(k):
    return route(lambda y, z, core, x: (y, z, core, x + k))


def along_z(k):
    return route(lambda y, z, core, x: (y, z + k, core, x))


def next_column(k, flip_zh):
    def move(y, z, core, x):
        zh, zl = z // 2, z % 2
        column = (y * 2 + zl + k) % 8
        return column // 2, (zh ^ flip_zh(core)) * 2 + column % 2, core, x

    return route(move)


ACROSS = route(lambda y, z, core, x: (y, z, core, x + 1 - 2 * core))
OTHER_CORE = route(lambda y, z, core, x: (y, z, core + 1, x))


def send(value, pairs):
    return lax.ppermute(value, AXES, pairs)


def dot(a, b, dims):
    return lax.dot_general(a, b, dims, preferred_element_type=jnp.float32)


WHOLE = pl.BlockSpec(memory_space=pltpu.VMEM)
SCALAR = pl.BlockSpec(memory_space=pltpu.SMEM)


def call(body, outs, ins, flops, transcendentals=0, scalars=1):
    return pl.pallas_call(
        body,
        out_shape=tuple(jax.ShapeDtypeStruct(s, t) for s, t in outs),
        in_specs=[SCALAR] * scalars + [WHOLE] * (len(ins) - scalars),
        out_specs=(WHOLE,) * len(outs),
        compiler_params=pltpu.CompilerParams(vmem_limit_bytes=VMEM_BYTES),
        cost_estimate=pl.CostEstimate(
            flops=flops, bytes_accessed=1 << 20, transcendentals=transcendentals
        ),
    )(*ins)


def pair_weights(scalars, images, text, weights, part, total, labelled):
    z = scalars[0] * dot(text, images[...], LAST) + scalars[1]
    e = jnp.exp(-jnp.abs(z))
    r = 1.0 / (1.0 + e)
    p = jnp.where(z >= 0.0, r, e * r)
    top = jnp.maximum(z, 0.0)
    if labelled:
        row = lax.broadcasted_iota(jnp.int32, z.shape, 0)
        col = lax.broadcasted_iota(jnp.int32, z.shape, 1)
        match = (row == col).astype(jnp.float32)
        p = p - match
        top = top - match * z
    rows, cols = z.shape
    total = total + jnp.sum(top.reshape(rows // 8, 8, cols), axis=0)
    e = e.reshape(rows // 8, 8, cols)
    for first in range(0, rows // 8, 8):
        q = e[first]
        for k in range(first + 1, min(first + 8, rows // 8)):
            q = q + (e[k] + q * e[k])
        total = total + jnp.log1p(q)
    weights[part, :] = p.astype(jnp.bfloat16)
    return total


def fold(total):
    out = total[:, :128]
    for k in range(128, total.shape[1], 128):
        out = out + total[:, k : k + 128]
    return out


def near_body(scalars, i0, i1, i2, i3, ta, tb, images, weights, loss):
    n = ta.shape[0]
    for k, ref in enumerate((i0, i1, i2, i3)):
        images[pl.ds(k * n, n), :] = ref[...]
    total = jnp.zeros((8, 4 * n), jnp.float32)
    total = pair_weights(scalars, images, ta[...], weights, pl.ds(0, n), total, True)
    total = pair_weights(scalars, images, tb[...], weights, pl.ds(n, n), total, False)
    loss[...] = fold(total)


def far_body(scalars, core, images, ta, tb, w0, own_o, z_o, far, far_o, loss_0, t1, t2, w1, w2, across, sum_1, loss):
    n = own_o.shape[0]
    low, high, last = pl.ds(0, n), pl.ds(n, n), pl.ds(3 * n, n)
    first = core[0] == 0
    total = jnp.zeros((8, 4 * n), jnp.float32)
    t1[low, :] = jnp.where(first, far[high, :], own_o[...])
    total = pair_weights(scalars, images, t1[low, :], w1, low, total, False)
    t1[high, :] = jnp.where(first, far_o[high, :], z_o[...])
    total = pair_weights(scalars, images, t1[high, :], w1, high, total, False)
    sum_1[low, :] = dot(w1[low, :], images[...], PLAIN)
    t2[low, :] = jnp.where(first, far[low, :], far_o[high, :])
    total = pair_weights(scalars, images, t2[low, :], w2, low, total, False)
    sum_1[high, :] = dot(w1[high, :], images[...], PLAIN)
    t2[high, :] = jnp.where(first, far_o[low, :], far[high, :])
    total = pair_weights(scalars, images, t2[high, :], w2, high, total, False)
    across[...] = image_sum(last, w0, w1, w2, ta, tb, t1, t2)
    loss[...] = loss_0[...] + fold(total)


def image_sum(cut, w0, w1, w2, ta, tb, t1, t2):
    n = ta.shape[0]
    total = dot(w0[pl.ds(0, n), cut], ta[...], FIRST)
    total = total + dot(w0[pl.ds(n, n), cut], tb[...], FIRST)
    total = total + dot(w1[:, cut], t1[...], FIRST)
    return total + dot(w2[:, cut], t2[...], FIRST)


def rest_body(images, w0, w1, w2, ta, tb, t1, t2, sum_a, sum_b, sum_2, own, left, right):
    n = ta.shape[0]
    sum_a[...] = dot(w0[pl.ds(0, n), :], images[...], PLAIN)
    sum_b[...] = dot(w0[pl.ds(n, n), :], images[...], PLAIN)
    for k in range(2):
        part = pl.ds(k * n, n)
        sum_2[part, :] = dot(w2[part, :], images[...], PLAIN)
    for k, out in enumerate((own, left, right)):
        out[...] = image_sum(pl.ds(k * n, n), w0, w1, w2, ta, tb, t1, t2)


def narrow(value):
    return (value * SEND_SCALE).astype(jnp.float16)


def wide(value):
    return value.astype(jnp.float32) * (1.0 / SEND_SCALE)


def local(image_embed, text_embed, scale_parameter, logit_bias):
    n, width = image_embed.shape
    scale = scale_parameter[0]
    scalars = jnp.concatenate([scale_parameter, logit_bias])
    core = lax.axis_index("core").astype(jnp.int32).reshape(1)
    first_core = core[0] == 0
    bf16, f32 = jnp.bfloat16, jnp.float32
    unit = 2 * n * 4 * n * width

    text_b = text_embed.astype(bf16)
    image_b = image_embed.astype(bf16)
    text_o = send(text_b, OTHER_CORE)
    both = jnp.where(
        first_core,
        jnp.concatenate([text_b, text_o]),
        jnp.concatenate([text_o, text_b]),
    )
    far = send(both, next_column(1, lambda core: core))
    text_z = send(text_b, along_z(2))
    image_l = send(image_b, along_x(1))
    image_r = send(image_b, along_x(-1))
    image_f = send(image_b, along_x(2))
    far, text_z, image_l, image_r, image_f, scalars, core = lax.optimization_barrier(
        (far, text_z, image_l, image_r, image_f, scalars, core)
    )
    z_o = send(text_z, OTHER_CORE)
    far_o = send(far, OTHER_CORE)

    images, w0, loss_0 = call(
        near_body,
        [((4 * n, width), bf16), ((2 * n, 4 * n), bf16), ((8, 128), f32)],
        (scalars, image_b, image_l, image_r, image_f, text_b, text_z),
        4 * unit,
    )
    t1, t2, w1, w2, across, sum_1, loss = call(
        far_body,
        [((2 * n, width), bf16)] * 2
        + [((2 * n, 4 * n), bf16)] * 2
        + [((n, width), f32), ((2 * n, width), f32), ((8, 128), f32)],
        (scalars, core, images, text_b, text_z, w0, text_o, z_o, far, far_o, loss_0),
        8 * unit,
        scalars=2,
    )
    passed = send(narrow(across), ACROSS)
    swapped = send(narrow(sum_1), OTHER_CORE)
    sum_a, sum_b, sum_2, own, left, right = call(
        rest_body,
        [((n, width), f32)] * 2 + [((2 * n, width), f32)] + [((n, width), f32)] * 3,
        (images, w0, w1, w2, text_b, text_z, t1, t2),
        7 * unit,
        scalars=0,
    )
    passed = wide(passed)
    swapped = wide(swapped)
    to_first = jnp.where(first_core, swapped, 0.0)
    sum_a = sum_a + to_first[:n]
    sum_b = sum_b + to_first[n:]
    sum_2 = sum_2 + jnp.where(first_core, 0.0, swapped)
    left = left + jnp.where(first_core, 0.0, passed)
    right = right + jnp.where(first_core, passed, 0.0)
    loss = loss + send(loss, OTHER_CORE)
    out = lax.optimization_barrier(
        tuple(narrow(v) for v in (sum_b, sum_2[:n], sum_2[n:]))
    )
    out = out + lax.optimization_barrier((narrow(left), narrow(right), loss))
    back_z = send(out[0], along_z(2))
    back_a = send(out[1], next_column(-1, lambda core: 0))
    back_b = send(out[2], next_column(-1, lambda core: 1))
    home_l = send(out[3], along_x(-1))
    home_r = send(out[4], along_x(1))

    loss = jnp.broadcast_to(jnp.sum(out[5]), (CHIP_COUNT, 1, 128))
    losses = lax.all_to_all(loss, CHIPS, 0, 0, tiled=True)
    pair_count = DEVICES * n * 3 * 8 * n
    mean_loss = (jnp.sum(losses[:, 0, 0]) / pair_count).reshape(1)
    text_out = scale * (sum_a + wide(back_z) + wide(back_a) + wide(back_b))
    own, text_out = lax.optimization_barrier((own, text_out))
    image_out = scale * (own + wide(home_l) + wide(home_r))
    return image_out, text_out, mean_loss


def solution(mesh):
    fine = Mesh(mesh.devices.reshape(NY, 2, 2, NX, 2), AXES)
    placed = (P(AXES, None), P(AXES, None), P(), P())
    return jax.shard_map(
        local,
        mesh=fine,
        in_specs=placed,
        out_specs=(P(AXES, None), P(AXES, None), P()),
        check_vma=False,
    )
```

time: 115 us -> 85.3 us (0.74)
  matrix products: 25.2 us -> 0 us
  starting transfers between devices: 42.2 us -> 28.5 us
  Pallas kernels: 0 us -> 11.4 us
  waiting for transfers between devices: 36 us -> 27.5 us
  other arithmetic: 4.45 us -> 11.5 us
  between operations: 5.7 us -> 3.86 us
    dot_general x7 -> x0, matrix products: 25.2 us -> none  [the longest x3 12.8 us: local(): lax.dot_general(images, text, contract_last, preferred_element_type=jnp.f...]
    ppermute x25 -> x16, starting transfers between devices: 42.2 us -> 21.3 us  [send(): return lax.ppermute(value, AXES, pairs)]
    ppermute x25 -> x16, waiting for transfers between devices: 36 us -> 18.6 us  [send(): return lax.ppermute(value, AXES, pairs)]
    pallas_call x0 -> x3, Pallas kernels: none -> 11.4 us  [call(): pl.pallas_call(body, out_shape=tuple((jax.ShapeDtypeStruct(s, t) for s, t...]
    all_to_all x0 -> x1, waiting for transfers between devices: none -> 8.88 us  [local(): losses = lax.all_to_all(loss, CHIPS, 0, 0, tiled=True)]
    all_to_all x0 -> x1, starting transfers between devices: none -> 7.17 us  [local(): losses = lax.all_to_all(loss, CHIPS, 0, 0, tiled=True)]
    mul x2, other arithmetic: 2.43 us -> 4.78 us  [the longest x1 2.51 us: local(): text_out = scale * (sum_a + wide(back_z) + wide(back_a) + wide(back_b))]
    convert_element_type x3 -> x4, other arithmetic: 0.46 us -> 2.73 us  [narrow(): return (value * SEND_SCALE).astype(jnp.float16)]
  transfers between devices with their start and end apart: 25 -> 17, of which waited for: 11 -> 7; matrix products, arithmetic and copies ran while one was open for 20% -> 10% of each run, Pallas kernels for 0% -> 7%
where the time goes in v2:
time: 85.3 us; the launch traced here: 84.2 us
  starting transfers between devices  28.5 us (33%)
  waiting for transfers between devices  27.5 us (32%)
  other arithmetic  11.5 us (13%)
  Pallas kernels  11.4 us (13%)
  between operations  3.86 us (5%)
  local copies, waits for them, and re-layouts  1.39 us (2%)
    ppermute x16, starting transfers between devices, send(): return lax.ppermute(value, AXES, pairs)  21.3 us
    ppermute x16, waiting for transfers between devices, send(): return lax.ppermute(value, AXES, pairs)  18.6 us
    pallas_call x3, Pallas kernels, call(): pl.pallas_call(body, out_shape=tuple((jax.ShapeDtypeStruct(s, t) for s, t...  11.4 us
    all_to_all x1, waiting for transfers between devices, local(): losses = lax.all_to_all(loss, CHIPS, 0, 0, tiled=True)  8.88 us
    all_to_all x1, starting transfers between devices, local(): losses = lax.all_to_all(loss, CHIPS, 0, 0, tiled=True)  7.17 us
    convert_element_type x4, other arithmetic, narrow(): return (value * SEND_SCALE).astype(jnp.float16)  2.73 us
    mul x1, other arithmetic, local(): text_out = scale * (sum_a + wide(back_z) + wide(back_a) + wide(back_b))  2.51 us
    mul x1, other arithmetic, local(): image_out = scale * (own + wide(home_l) + wide(home_r))  2.26 us
  transfers between devices with their start and end apart: 17, of which 7 were waited for; matrix products, arithmetic and copies ran while one was open for 10% of the time, Pallas kernels for 7%

profile of v2, /device:TPU:0, one launch (start us, length us, event | category | flops | bytes accessed | tf_op | source)
XLA Modules:
  0.0 84.2 jit_solution(128129898853247235)
XLA Ops:
  0.6 1.3 %convert_element_type.48.ta = bf16[192,1152]{1,0:T(8,128)(2,1)S(1)} convert(f32[192,1152]{1,0:T(8,128)} %param.5) | non-fusion elementwise | flops 221184 | bytes 1327104 | tf_op jit(solution)/shard_map/convert_element_type | solution.py:180
  2.0 1.8 %collective-permute-done.own_o = bf16[192,1152]{1,0:T(8,128)(2,1)S(1)} collective-permute-done((bf16[192,1152]{1,0:T(8,128)(2,1)S(1)}, bf16[192,1152]{1,0:T(8,128)(2,1)S(1)}, u32[]{:S(2)}, u32[]{:S(2)}) %collective-permute-start) | collective-permute-done | bytes 442400 | tf_op jit(solution)/shard_map/ppermute | solution.py:60
  4.1 2.1 %collective-permute-start.1 = (bf16[384,1152]{1,0:T(8,128)(2,1)S(1)}, bf16[384,1152]{1,0:T(8,128)(2,1)S(1)}, u32[]{:S(2)}, u32[]{:S(2)}) collective-permute-start(bf16[384,1152]{1,0:T(8,128)(2,1)S(1)} %maximum_select_fusion), channel_id=1, source_target_pairs={{0,16},{2,18},{4,20},{6,22},{8,25},{10,27},{12,29},{14,31},{16,32}... | collective-permute-start | bytes 2654216 | tf_op jit(solution)/shard_map/ppermute | solution.py:60
  6.2 3.1 %collective-permute-start.5 = (bf16[192,1152]{1,0:T(8,128)(2,1)S(1)}, bf16[192,1152]{1,0:T(8,128)(2,1)S(1)}, u32[]{:S(2)}, u32[]{:S(2)}) collective-permute-start(bf16[192,1152]{1,0:T(8,128)(2,1)S(1)} %convert_element_type.49.i0), channel_id=1, source_target_pairs={{0,4},{2,6},{4,0},{6,2},{8,12},{10,14},{12,8},{14,10},{16,20},{18,... | collective-permute-start | bytes 1327112 | tf_op jit(solution)/shard_map/ppermute | solution.py:60
  9.3 1.1 %collective-permute-start.4 = (bf16[192,1152]{1,0:T(8,128)(2,1)S(1)}, bf16[192,1152]{1,0:T(8,128)(2,1)S(1)}, u32[]{:S(2)}, u32[]{:S(2)}) collective-permute-start(bf16[192,1152]{1,0:T(8,128)(2,1)S(1)} %convert_element_type.49.i0), channel_id=1, source_target_pairs={{0,6},{2,0},{4,2},{6,4},{8,14},{10,8},{12,10},{14,12},{16,22},{18,... | collective-permute-start | bytes 1327112 | tf_op jit(solution)/shard_map/ppermute | solution.py:60
  11.3 3.6 %collective-permute-start.2 = (bf16[192,1152]{1,0:T(8,128)(2,1)S(1)}, bf16[192,1152]{1,0:T(8,128)(2,1)S(1)}, u32[]{:S(2)}, u32[]{:S(2)}) collective-permute-start(bf16[192,1152]{1,0:T(8,128)(2,1)S(1)} %convert_element_type.48.ta), channel_id=1, source_target_pairs={{0,1},{2,3},{4,5},{6,7},{8,9},{10,11},{12,13},{14,15},{16,17},{18,... | collective-permute-start | bytes 1327112 | tf_op jit(solution)/shard_map/ppermute | solution.py:60
  16.3 3.6 %collective-permute-done.5.i3 = bf16[192,1152]{1,0:T(8,128)(2,1)S(1)} collective-permute-done((bf16[192,1152]{1,0:T(8,128)(2,1)S(1)}, bf16[192,1152]{1,0:T(8,128)(2,1)S(1)}, u32[]{:S(2)}, u32[]{:S(2)}) %collective-permute-start.5) | collective-permute-done | bytes 442400 | tf_op jit(solution)/shard_map/ppermute | solution.py:60
  19.9 9.5 %collective-permute-done.4.i2 = bf16[192,1152]{1,0:T(8,128)(2,1)S(1)} collective-permute-done((bf16[192,1152]{1,0:T(8,128)(2,1)S(1)}, bf16[192,1152]{1,0:T(8,128)(2,1)S(1)}, u32[]{:S(2)}, u32[]{:S(2)}) %collective-permute-start.4) | collective-permute-done | bytes 442400 | tf_op jit(solution)/shard_map/ppermute | solution.py:60
  30.3 2.6 %collective-permute-done.2.tb = bf16[192,1152]{1,0:T(8,128)(2,1)S(1)} collective-permute-done((bf16[192,1152]{1,0:T(8,128)(2,1)S(1)}, bf16[192,1152]{1,0:T(8,128)(2,1)S(1)}, u32[]{:S(2)}, u32[]{:S(2)}) %collective-permute-start.2) | collective-permute-done | bytes 442400 | tf_op jit(solution)/shard_map/ppermute | solution.py:60
  33.4 2.3 %shard_map.67 = (bf16[768,1152]{1,0:T(8,128)(2,1)S(1)}, bf16[384,768]{1,0:T(8,128)(2,1)S(1)}, f32[8,128]{1,0:T(8,128)S(1)}) custom-call(f32[2]{0:T(128)S(1)} %pad_maximum_fusion.scalars, bf16[192,1152]{1,0:T(8,128)(2,1)S(1)} %convert_element_type.49.i0, bf16[192,1152]{1,0:T(8,128)(2,1)S(1)} %collective-permute-done.3.i1, ...), custom_call_target="tpu_custom_call" | custom-call | flops 1358954496 | bytes 1048576 | tf_op jit(solution)/shard_map/pallas_call | solution.py:72
  35.9 5.2 %shard_map.68 = (bf16[384,1152]{1,0:T(8,128)(2,1)S(1)}, bf16[384,1152]{1,0:T(8,128)(2,1)S(1)}, bf16[384,768]{1,0:T(8,128)(2,1)S(1)}, bf16[384,768]{1,0:T(8,128)(...) custom-call(f32[2]{0:T(128)S(1)} %pad_maximum_fusion.scalars, s32[1]{0:T(128)} %bitcast.1.core, ...), custom_call_target="tpu_custom_call" | custom-call | flops 2717908992 | bytes 1048576 | tf_op jit(solution)/shard_map/pallas_call | solution.py:72
  41.9 1.4 %collective-permute-start.12 = (f16[192,1152]{1,0:T(8,128)(2,1)S(1)}, f16[192,1152]{1,0:T(8,128)(2,1)S(1)}, u32[]{:S(2)}, u32[]{:S(2)}) collective-permute-start(f16[192,1152]{1,0:T(8,128)(2,1)S(1)} %multiply_convert_fusion.3), channel_id=1, source_target_pairs={{0,2},{2,4},{4,6},{6,0},{8,14},{10,8},{12,10},{14,12},{16,18},{18,... | collective-permute-start | bytes 1327112 | tf_op jit(solution)/shard_map/ppermute | solution.py:60
  43.3 4.0 %shard_map.69 = (f32[192,1152]{1,0:T(8,128)S(1)}, f32[192,1152]{1,0:T(8,128)S(1)}, f32[384,1152]{1,0:T(8,128)S(1)}, f32[192,1152]{1,0:T(8,128)S(1)}, f32[192,1152]{1,0:T(8,128)S(1)}, /*index=5*/f32[192,1152]{1,0:T(8,128)S(1)}) custom-call(bf16[768,1152]{1,0:T(8,128)(2,1)S(1)} %get-tuple-element.39.images, bf16[384,768]{1,0:T(8,128)(2,1)S(1)} %get-tuple-element.40.w0, ...), custom_call_target="tpu_custom_call" | custom-call | flops 2378170368 | bytes 1048576 | tf_op jit(solution)/shard_map/pallas_call | solution.py:72
  47.7 1.3 %fusion.1 = (f16[192,1152]{1,0:T(8,128)(2,1)S(1)}, f16[192,1152]{1,0:T(8,128)(2,1)S(1)}, f16[192,1152]{1,0:T(8,128)(2,1)}) fusion(f32[384,1152]{1,0:T(8,128)S(1)} %get-tuple-element.67, f32[192,1152]{1,0:T(8,128)S(1)} %get-tuple-element.51, f32[384,1152]{1,0:T(8,128)S(1)} %get-tuple-element.68), kind=kLoop, calls=%fused_computation.5 | loop fusion | flops 1548288 | bytes 4866048 | tf_op jit(solution)/shard_map/convert_element_type | solution.py:164
  50.0 2.0 %collective-permute-start.10 = (f16[192,1152]{1,0:T(8,128)(2,1)S(1)}, f16[192,1152]{1,0:T(8,128)(2,1)S(1)}, u32[]{:S(2)}, u32[]{:S(2)}) collective-permute-start(f16[192,1152]{1,0:T(8,128)(2,1)S(1)} %get-tuple-element.54), channel_id=1, source_target_pairs={{0,112},{2,114},{4,116},{6,118},{8,120},{10,122},{12,124},{14,126}... | collective-permute-start | bytes 1327112 | tf_op jit(solution)/shard_map/ppermute | solution.py:60
  52.0 2.2 %collective-permute-start.11 = (f16[192,1152]{1,0:T(8,128)(2,1)S(1)}, f16[192,1152]{1,0:T(8,128)(2,1)}, u32[]{:S(2)}, u32[]{:S(2)}) collective-permute-start(f16[192,1152]{1,0:T(8,128)(2,1)S(1)} %get-tuple-element.55), channel_id=1, source_target_pairs={{0,113},{2,115},{4,117},{6,119},{8,121},{10,123},{12,125},{14,127}... | collective-permute-start | bytes 1327112 | tf_op jit(solution)/shard_map/ppermute | solution.py:60
  54.2 1.2 %multiply_convert_fusion.1 = (f16[192,1152]{1,0:T(8,128)(2,1)}, f16[192,1152]{1,0:T(8,128)(2,1)}) fusion(f32[192,1152]{1,0:T(8,128)S(1)} %get-tuple-element.59, f16[192,1152]{1,0:T(8,128)(2,1)S(1)} %collective-permute-done.12, pred[]{:T(512)S(6)} %eq.3, f32[192,1152]{1,0:T(8,128)S(1)} %get-tuple-element.57), kind=kLoop, calls=%fused_computation.18 | loop fusion | flops 2211840 | bytes 3096577 | tf_op jit(solution)/shard_map/convert_element_type | solution.py:164
  56.1 1.3 %broadcast_in_dim.17 = f32[64,1,128]{2,1,0:T(1,128)} broadcast(f32[]{:T(128)} %reduce_sum.18), dimensions={} | broadcast | bytes 32772 | tf_op jit(solution)/shard_map/broadcast_in_dim | solution.py:242
  57.3 7.2 %all-to-all-start = ((f32[64,1,128]{2,1,0:T(1,128)}), f32[64,1,128]{2,1,0:T(1,128)}, u32[]{:S(2)}, u32[]{:S(2)}) async-start(f32[64,1,128]{2,1,0:T(1,128)} %broadcast_in_dim.17), calls=%async_computation | async-start | bytes 65536 | tf_op jit(solution)/shard_map/all_to_all | solution.py:243
  64.5 2.8 %collective-permute-start.14 = (f16[192,1152]{1,0:T(8,128)(2,1)}, f16[192,1152]{1,0:T(8,128)(2,1)}, u32[]{:S(2)}, u32[]{:S(2)}) collective-permute-start(f16[192,1152]{1,0:T(8,128)(2,1)} %get-tuple-element.61), channel_id=1, source_target_pairs={{0,6},{2,0},{4,2},{6,4},{8,14},{10,8},{12,10},{14,12},{16,22},{18,... | collective-permute-start | bytes 1327112 | tf_op jit(solution)/shard_map/ppermute | solution.py:60
  67.3 8.9 %all-to-all-done = f32[64,1,128]{2,1,0:T(1,128)} async-done(((f32[64,1,128]{2,1,0:T(1,128)}), f32[64,1,128]{2,1,0:T(1,128)}, u32[]{:S(2)}, u32[]{:S(2)}) %all-to-all-start) | async-done | bytes 32800 | tf_op jit(solution)/shard_map/all_to_all | solution.py:243
  76.2 1.4 %slice_reduce_fusion = f32[]{:T(128)} fusion(f32[64,1,128]{2,1,0:T(1,128)} %all-to-all-done), kind=kLoop, calls=%fused_computation.22 | loop fusion | flops 63 | bytes 260 | tf_op jit(solution)/shard_map/reduce_sum | solution.py:245
  78.3 2.5 %fusion.8 = f32[192,1152]{1,0:T(8,128)} fusion(f32[192,1152]{1,0:T(8,128)S(1)} %get-tuple-element.49, f32[384,1152]{1,0:T(8,128)} %copy-done, f16[192,1152]{1,0:T(8,128)(2,1)} %collective-permute-done.11, f16[192,1152]{1,0:T(8,128)(2,1)S(1)} %collective-permute-done.10, f16[192,1152]{1,0:T(8,128)(2,1)S(1)} %collective-permute-done.9, f32[]{:T(128)} %bitcast.3), kind=kLoop, calls=%fused_computation.15 | loop fusion | flops 2433024 | bytes 3981316 | tf_op jit(solution)/shard_map/mul | solution.py:246
  80.8 2.3 %add_multiply_fusion = f32[192,1152]{1,0:T(8,128)} fusion(f16[192,1152]{1,0:T(8,128)(2,1)} %collective-permute-done.15, f32[192,1152]{1,0:T(8,128)S(1)} %get-tuple-element.56, f16[192,1152]{1,0:T(8,128)(2,1)} %collective-permute-done.14, f32[]{:T(128)} %bitcast.4), kind=kLoop, calls=%fused_computation.17 | loop fusion | flops 1548288 | bytes 2654212 | tf_op jit(solution)/shard_map/mul | solution.py:248
  (32 shorter events, 5.7 us)
Async XLA Ops:
  0.6 5.5 %copy-start.1 = (f32[192,1152]{1,0:T(8,128)S(1)}, f32[192,1152]{1,0:T(8,128)}, u32[]{:S(2)}) copy-start(f32[192,1152]{1,0:T(8,128)} %param.4) | copy-start | bytes 2654212
  1.9 1.9 %collective-permute-start = (bf16[192,1152]{1,0:T(8,128)(2,1)S(1)}, bf16[192,1152]{1,0:T(8,128)(2,1)S(1)}, u32[]{:S(2)}, u32[]{:S(2)}) collective-permute-start(bf16[192,1152]{1,0:T(8,128)(2,1)S(1)} %convert_element_type.48.ta), channel_id=1, source_target_pairs={{0,8},{2,10},{4,12},{6,14},{8,0},{10,2},{12,4},{14,6},{16,24},{18,... | collective-permute-start | bytes 1327112 | tf_op jit(solution)/shard_map/ppermute | solution.py:60
  4.1 28.8 %collective-permute-start.1 = (bf16[384,1152]{1,0:T(8,128)(2,1)S(1)}, bf16[384,1152]{1,0:T(8,128)(2,1)S(1)}, u32[]{:S(2)}, u32[]{:S(2)}) collective-permute-start(bf16[384,1152]{1,0:T(8,128)(2,1)S(1)} %maximum_select_fusion), channel_id=1, source_target_pairs={{0,16},{2,18},{4,20},{6,22},{8,25},{10,27},{12,29},{14,31},{16,32}... | collective-permute-start | bytes 2654216 | tf_op jit(solution)/shard_map/ppermute | solution.py:60
  6.2 13.7 %collective-permute-start.5 = (bf16[192,1152]{1,0:T(8,128)(2,1)S(1)}, bf16[192,1152]{1,0:T(8,128)(2,1)S(1)}, u32[]{:S(2)}, u32[]{:S(2)}) collective-permute-start(bf16[192,1152]{1,0:T(8,128)(2,1)S(1)} %convert_element_type.49.i0), channel_id=1, source_target_pairs={{0,4},{2,6},{4,0},{6,2},{8,12},{10,14},{12,8},{14,10},{16,20},{18,... | collective-permute-start | bytes 1327112 | tf_op jit(solution)/shard_map/ppermute | solution.py:60
  9.3 20.1 %collective-permute-start.4 = (bf16[192,1152]{1,0:T(8,128)(2,1)S(1)}, bf16[192,1152]{1,0:T(8,128)(2,1)S(1)}, u32[]{:S(2)}, u32[]{:S(2)}) collective-permute-start(bf16[192,1152]{1,0:T(8,128)(2,1)S(1)} %convert_element_type.49.i0), channel_id=1, source_target_pairs={{0,6},{2,0},{4,2},{6,4},{8,14},{10,8},{12,10},{14,12},{16,22},{18,... | collective-permute-start | bytes 1327112 | tf_op jit(solution)/shard_map/ppermute | solution.py:60
  10.4 19.8 %collective-permute-start.3 = (bf16[192,1152]{1,0:T(8,128)(2,1)S(1)}, bf16[192,1152]{1,0:T(8,128)(2,1)S(1)}, u32[]{:S(2)}, u32[]{:S(2)}) collective-permute-start(bf16[192,1152]{1,0:T(8,128)(2,1)S(1)} %convert_element_type.49.i0), channel_id=1, source_target_pairs={{0,2},{2,4},{4,6},{6,0},{8,10},{10,12},{12,14},{14,8},{16,18},{18,... | collective-permute-start | bytes 1327112 | tf_op jit(solution)/shard_map/ppermute | solution.py:60
  11.3 21.5 %collective-permute-start.2 = (bf16[192,1152]{1,0:T(8,128)(2,1)S(1)}, bf16[192,1152]{1,0:T(8,128)(2,1)S(1)}, u32[]{:S(2)}, u32[]{:S(2)}) collective-permute-start(bf16[192,1152]{1,0:T(8,128)(2,1)S(1)} %convert_element_type.48.ta), channel_id=1, source_target_pairs={{0,1},{2,3},{4,5},{6,7},{8,9},{10,11},{12,13},{14,15},{16,17},{18,... | collective-permute-start | bytes 1327112 | tf_op jit(solution)/shard_map/ppermute | solution.py:60
  32.9 3.1 %collective-permute-start.7 = (bf16[384,1152]{1,0:T(8,128)(2,1)S(1)}, bf16[384,1152]{1,0:T(8,128)(2,1)S(1)}, u32[]{:S(2)}, u32[]{:S(2)}) collective-permute-start(bf16[384,1152]{1,0:T(8,128)(2,1)S(1)} %collective-permute-done.1.far), channel_id=1, source_target_pairs={{0,8},{2,10},{4,12},{6,14},{8,0},{10,2},{12,4},{14,6},{16,24},{18,... | collective-permute-start | bytes 2654216 | tf_op jit(solution)/shard_map/ppermute | solution.py:60
  32.9 3.1 %collective-permute-start.6 = (bf16[192,1152]{1,0:T(8,128)(2,1)S(1)}, bf16[192,1152]{1,0:T(8,128)(2,1)S(1)}, u32[]{:S(2)}, u32[]{:S(2)}) collective-permute-start(bf16[192,1152]{1,0:T(8,128)(2,1)S(1)} %collective-permute-done.2.tb), channel_id=1, source_target_pairs={{0,8},{2,10},{4,12},{6,14},{8,0},{10,2},{12,4},{14,6},{16,24},{18,... | collective-permute-start | bytes 1327112 | tf_op jit(solution)/shard_map/ppermute | solution.py:60
  41.3 6.1 %collective-permute-start.8 = (f16[384,1152]{1,0:T(8,128)(2,1)S(1)}, f16[384,1152]{1,0:T(8,128)(2,1)S(1)}, u32[]{:S(2)}, u32[]{:S(2)}) collective-permute-start(f16[384,1152]{1,0:T(8,128)(2,1)S(1)} %multiply_convert_fusion), channel_id=1, source_target_pairs={{0,8},{2,10},{4,12},{6,14},{8,0},{10,2},{12,4},{14,6},{16,24},{18,... | collective-permute-start | bytes 2654216 | tf_op jit(solution)/shard_map/ppermute | solution.py:60
  41.5 5.9 %collective-permute-start.13 = (f32[8,128]{1,0:T(8,128)S(1)}, f32[8,128]{1,0:T(8,128)S(1)}, u32[]{:S(2)}, u32[]{:S(2)}) collective-permute-start(f32[8,128]{1,0:T(8,128)S(1)} %get-tuple-element.60), channel_id=1, source_target_pairs={{0,8},{2,10},{4,12},{6,14},{8,0},{10,2},{12,4},{14,6},{16,24},{18,... | collective-permute-start | bytes 12296 | tf_op jit(solution)/shard_map/ppermute | solution.py:60
  41.9 12.3 %collective-permute-start.12 = (f16[192,1152]{1,0:T(8,128)(2,1)S(1)}, f16[192,1152]{1,0:T(8,128)(2,1)S(1)}, u32[]{:S(2)}, u32[]{:S(2)}) collective-permute-start(f16[192,1152]{1,0:T(8,128)(2,1)S(1)} %multiply_convert_fusion.3), channel_id=1, source_target_pairs={{0,2},{2,4},{4,6},{6,0},{8,14},{10,8},{12,10},{14,12},{16,18},{18,... | collective-permute-start | bytes 1327112 | tf_op jit(solution)/shard_map/ppermute | solution.py:60
  47.7 1.4 %copy-start = (f32[384,1152]{1,0:T(8,128)}, f32[384,1152]{1,0:T(8,128)S(1)}, u32[]{:S(2)}) copy-start(f32[384,1152]{1,0:T(8,128)S(1)} %get-tuple-element.68) | copy-start | bytes 5308420
  49.1 29.2 %collective-permute-start.9 = (f16[192,1152]{1,0:T(8,128)(2,1)}, f16[192,1152]{1,0:T(8,128)(2,1)S(1)}, u32[]{:S(2)}, u32[]{:S(2)}) collective-permute-start(f16[192,1152]{1,0:T(8,128)(2,1)} %get-tuple-element.53), channel_id=1, source_target_pairs={{0,1},{2,3},{4,5},{6,7},{8,9},{10,11},{12,13},{14,15},{16,17},{18,... | collective-permute-start | bytes 1327112 | tf_op jit(solution)/shard_map/ppermute | solution.py:60
  50.0 28.3 %collective-permute-start.10 = (f16[192,1152]{1,0:T(8,128)(2,1)S(1)}, f16[192,1152]{1,0:T(8,128)(2,1)S(1)}, u32[]{:S(2)}, u32[]{:S(2)}) collective-permute-start(f16[192,1152]{1,0:T(8,128)(2,1)S(1)} %get-tuple-element.54), channel_id=1, source_target_pairs={{0,112},{2,114},{4,116},{6,118},{8,120},{10,122},{12,124},{14,126}... | collective-permute-start | bytes 1327112 | tf_op jit(solution)/shard_map/ppermute | solution.py:60
  52.0 26.2 %collective-permute-start.11 = (f16[192,1152]{1,0:T(8,128)(2,1)S(1)}, f16[192,1152]{1,0:T(8,128)(2,1)}, u32[]{:S(2)}, u32[]{:S(2)}) collective-permute-start(f16[192,1152]{1,0:T(8,128)(2,1)S(1)} %get-tuple-element.55), channel_id=1, source_target_pairs={{0,113},{2,115},{4,117},{6,119},{8,121},{10,123},{12,125},{14,127}... | collective-permute-start | bytes 1327112 | tf_op jit(solution)/shard_map/ppermute | solution.py:60
  57.3 18.8 %all-to-all-start = ((f32[64,1,128]{2,1,0:T(1,128)}), f32[64,1,128]{2,1,0:T(1,128)}, u32[]{:S(2)}, u32[]{:S(2)}) async-start(f32[64,1,128]{2,1,0:T(1,128)} %broadcast_in_dim.17), calls=%async_computation | async-start | bytes 65536 | tf_op jit(solution)/shard_map/all_to_all | solution.py:243
  64.5 16.3 %collective-permute-start.14 = (f16[192,1152]{1,0:T(8,128)(2,1)}, f16[192,1152]{1,0:T(8,128)(2,1)}, u32[]{:S(2)}, u32[]{:S(2)}) collective-permute-start(f16[192,1152]{1,0:T(8,128)(2,1)} %get-tuple-element.61), channel_id=1, source_target_pairs={{0,6},{2,0},{4,2},{6,4},{8,14},{10,8},{12,10},{14,12},{16,22},{18,... | collective-permute-start | bytes 1327112 | tf_op jit(solution)/shard_map/ppermute | solution.py:60
  67.3 13.5 %collective-permute-start.15 = (f16[192,1152]{1,0:T(8,128)(2,1)}, f16[192,1152]{1,0:T(8,128)(2,1)}, u32[]{:S(2)}, u32[]{:S(2)}) collective-permute-start(f16[192,1152]{1,0:T(8,128)(2,1)} %get-tuple-element.62), channel_id=1, source_target_pairs={{0,2},{2,4},{4,6},{6,0},{8,10},{10,12},{12,14},{14,8},{16,18},{18,... | collective-permute-start | bytes 1327112 | tf_op jit(solution)/shard_map/ppermute | solution.py:60

commit v3 on v2

v3 whole, which is shorter than its diff:
```python
import functools

import jax
import jax.numpy as jnp
from jax import lax
from jax.experimental import pallas as pl
from jax.experimental.pallas import tpu as pltpu
from jax.sharding import Mesh
from jax.sharding import PartitionSpec as P

AXES = ("y", "z_lo", "core", "x", "z_hi")
CHIPS = ("y", "z_lo", "x", "z_hi")
NY, NX = 4, 4
DEVICES = 128
CHIP_COUNT = 64
SEND_SCALE = 64.0
TILE = 64
LAST = (((1,), (1,)), ((), ()))
FIRST = (((0,), (0,)), ((), ()))
PLAIN = (((1,), (0,)), ((), ()))
VMEM_BYTES = 16 * 1024 * 1024


def place(y, z, core, x):
    z = z % 4
    return (((y % NY) * 2 + z % 2) * 2 + core % 2) * 8 + (x % NX) * 2 + z // 2


def route(move):
    pairs = []
    for y in range(NY):
        for z in range(4):
            for core in range(2):
                for x in range(NX):
                    pairs.append((place(y, z, core, x), place(*move(y, z, core, x))))
    return pairs


def along_x(k):
    return route(lambda y, z, core, x: (y, z, core, x + k))


def along_z(k):
    return route(lambda y, z, core, x: (y, z + k, core, x))


def next_column(k, flip_zh):
    def move(y, z, core, x):
        zh, zl = z // 2, z % 2
        column = (y * 2 + zl + k) % 8
        return column // 2, (zh ^ flip_zh(core)) * 2 + column % 2, core, x

    return route(move)


ACROSS = route(lambda y, z, core, x: (y, z, core, x + 1 - 2 * core))
OTHER_CORE = route(lambda y, z, core, x: (y, z, core + 1, x))


def send(value, pairs):
    return lax.ppermute(value, AXES, pairs)


def dot(a, b, dims):
    return lax.dot_general(a, b, dims, preferred_element_type=jnp.float32)


WHOLE = pl.BlockSpec(memory_space=pltpu.VMEM)
SCALAR = pl.BlockSpec(memory_space=pltpu.SMEM)


def call(body, outs, ins, flops, scalars=1, scratch=()):
    return pl.pallas_call(
        body,
        out_shape=tuple(jax.ShapeDtypeStruct(s, t) for s, t in outs),
        in_specs=[SCALAR] * scalars + [WHOLE] * (len(ins) - scalars),
        out_specs=(WHOLE,) * len(outs),
        scratch_shapes=scratch,
        compiler_params=pltpu.CompilerParams(vmem_limit_bytes=VMEM_BYTES),
        cost_estimate=pl.CostEstimate(
            flops=flops, bytes_accessed=1 << 20, transcendentals=0
        ),
    )(*ins)


def tile_terms(scalars, z, match):
    z = scalars[0] * z + scalars[1]
    e = jnp.exp(-jnp.abs(z))
    d = 1.0 + e
    r = pltpu.reciprocal(d, approx=True)
    r = r * (2.0 - d * r)
    p = r * jnp.where(z >= 0.0, 1.0, e)
    top = jnp.maximum(z, 0.0)
    if match is not None:
        p = p - match
        top = top - match * z
    rows, cols = z.shape
    total = jnp.sum(top.reshape(rows // 8, 8, cols), axis=0)
    e = e.reshape(rows // 8, 8, cols)
    d = d.reshape(rows // 8, 8, cols)
    q = e[0]
    for k in range(1, rows // 8):
        q = q * d[k] + e[k]
    return p.astype(jnp.bfloat16), total + jnp.log1p(q)


def pair_weights(scalars, images, text, weights, products, loss, labelled):
    step = products.shape[2]
    rows, cols = weights.shape
    own = rows // 2

    def multiply(k):
        products[k % 2, :, :] = dot(text, images[pl.ds(k * step, step), :], LAST)

    multiply(0)
    for k in range(cols // step):
        if (k + 1) * step < cols:
            multiply(k + 1)
        for r in range(0, rows, TILE):
            for c in range(0, step, 128):
                match = None
                at = k * step + c
                if labelled and r < own and at < own and at < r + TILE and r < at + 128:
                    row = lax.broadcasted_iota(jnp.int32, (TILE, 128), 0) + r
                    col = lax.broadcasted_iota(jnp.int32, (TILE, 128), 1) + at
                    match = ((row == col) & (row < own)).astype(jnp.float32)
                part, terms = tile_terms(
                    scalars, products[k % 2, pl.ds(r, TILE), pl.ds(c, 128)], match
                )
                weights[pl.ds(r, TILE), pl.ds(at, 128)] = part
                loss = loss + terms
    return loss


def near_body(scalars, i0, i1, i2, i3, ta, tb, images, text, weights, loss, products):
    n = ta.shape[0]
    for k, ref in enumerate((i0, i1, i2, i3)):
        images[pl.ds(k * n, n), :] = ref[...]
    text[pl.ds(0, n), :] = ta[...]
    text[pl.ds(n, n), :] = tb[...]
    none = jnp.zeros((8, 128), jnp.float32)
    loss[...] = pair_weights(scalars, images, text[...], weights, products, none, True)


def far_body(scalars, core, images, t0, w0, own_o, z_o, far, far_o, loss_0, text, weights, across, sum_1, loss, products):
    n = own_o.shape[0]
    low, high, last = pl.ds(0, n), pl.ds(n, n), pl.ds(3 * n, n)
    first = core[0] == 0
    text[pl.ds(0, n), :] = jnp.where(first, far[high, :], own_o[...])
    text[pl.ds(n, n), :] = jnp.where(first, far_o[high, :], z_o[...])
    text[pl.ds(2 * n, n), :] = jnp.where(first, far[low, :], far_o[high, :])
    text[pl.ds(3 * n, n), :] = jnp.where(first, far_o[low, :], far[high, :])
    loss[...] = pair_weights(scalars, images, text[...], weights, products, loss_0[...], False)
    sum_1[...] = dot(weights[pl.ds(0, 2 * n), :], images[...], PLAIN)
    across[...] = dot(w0[:, last], t0[...], FIRST) + dot(weights[:, last], text[...], FIRST)


def text_body(images, w0, weights, sum_a, sum_b, sum_2):
    n = sum_a.shape[0]
    out = dot(w0[...], images[...], PLAIN)
    sum_a[...] = out[:n]
    sum_b[...] = out[n:]
    sum_2[...] = dot(weights[pl.ds(2 * n, 2 * n), :], images[...], PLAIN)


def image_body(w0, weights, t0, text, *outs):
    n = outs[0].shape[0]
    cut = pl.ds(0, len(outs) * n)
    out = dot(w0[:, cut], t0[...], FIRST) + dot(weights[:, cut], text[...], FIRST)
    for k, ref in enumerate(outs):
        ref[...] = out[k * n : (k + 1) * n]


def spread_body(mine, other, out):
    total = jnp.sum(mine[...] + other[...])
    out[...] = jnp.full(out.shape, total, jnp.float32)


def total_body(parts, out):
    out[...] = jnp.broadcast_to(jnp.sum(parts[...], axis=0), out.shape)


def narrow(value):
    return (value * SEND_SCALE).astype(jnp.float16)


def wide(value):
    return value.astype(jnp.float32) * (1.0 / SEND_SCALE)


def local(image_embed, text_embed, scale_parameter, logit_bias):
    n, width = image_embed.shape
    scale = scale_parameter[0]
    scalars = jnp.concatenate([scale_parameter, logit_bias])
    core = lax.axis_index("core").astype(jnp.int32).reshape(1)
    first_core = core[0] == 0
    bf16, f32 = jnp.bfloat16, jnp.float32
    unit = 2 * n * 4 * n * width

    text_b = text_embed.astype(bf16)
    image_b = image_embed.astype(bf16)
    text_o = send(text_b, OTHER_CORE)
    both = jnp.where(
        first_core,
        jnp.concatenate([text_b, text_o]),
        jnp.concatenate([text_o, text_b]),
    )
    far = send(both, next_column(1, lambda core: core))
    text_z = send(text_b, along_z(2))
    image_l = send(image_b, along_x(1))
    image_r = send(image_b, along_x(-1))
    image_f = send(image_b, along_x(2))
    far, text_z, image_l, image_r, image_f, scalars, core = lax.optimization_barrier(
        (far, text_z, image_l, image_r, image_f, scalars, core)
    )
    z_o = send(text_z, OTHER_CORE)
    far_o = send(far, OTHER_CORE)

    images, t0, w0, loss_0 = call(
        near_body,
        [((4 * n, width), bf16), ((2 * n, width), bf16), ((2 * n, 4 * n), bf16), ((8, 128), f32)],
        (scalars, image_b, image_l, image_r, image_f, text_b, text_z),
        2 * unit,
        scratch=[pltpu.VMEM((2, 2 * n, 2 * n), f32)],
    )
    text, weights, across, sum_1, loss = call(
        far_body,
        [
            ((4 * n, width), bf16),
            ((4 * n, 4 * n), bf16),
            ((n, width), f32),
            ((2 * n, width), f32),
            ((8, 128), f32),
        ],
        (scalars, core, images, t0, w0, text_o, z_o, far, far_o, loss_0),
        8 * unit,
        scalars=2,
        scratch=[pltpu.VMEM((2, 4 * n, 2 * n), f32)],
    )
    passed = send(narrow(across), ACROSS)
    swapped = send(narrow(sum_1), OTHER_CORE)
    sum_a, sum_b, sum_2 = call(
        text_body,
        [((n, width), f32)] * 2 + [((2 * n, width), f32)],
        (images, w0, weights),
        4 * unit,
        scalars=0,
    )
    passed = wide(passed)
    swapped = wide(swapped)
    to_first = jnp.where(first_core, swapped, 0.0)
    sum_b = sum_b + to_first[n:]
    sum_2 = sum_2 + jnp.where(first_core, 0.0, swapped)
    (loss,) = call(spread_body, [((CHIP_COUNT, 1, 128), f32)], (loss, send(loss, OTHER_CORE)), 4, scalars=0)
    out = lax.optimization_barrier(
        tuple(narrow(v) for v in (sum_b, sum_2[:n], sum_2[n:])) + (sum_a + to_first[:n], w0)
    )
    sum_a, w0 = out[3:]
    out = out[:3]
    own, left, right = call(
        image_body, [((n, width), f32)] * 3, (w0, weights, t0, text), 9 * unit // 2, scalars=0
    )
    left = left + jnp.where(first_core, 0.0, passed)
    right = right + jnp.where(first_core, passed, 0.0)
    out = out + lax.optimization_barrier((narrow(left), narrow(right), loss))
    back_z = send(out[0], along_z(2))
    back_a = send(out[1], next_column(-1, lambda core: 0))
    back_b = send(out[2], next_column(-1, lambda core: 1))
    home_l = send(out[3], along_x(-1))
    home_r = send(out[4], along_x(1))

    losses = lax.all_to_all(out[5], CHIPS, 0, 0, tiled=True)
    text_out = scale * (sum_a + wide(back_z) + wide(back_a) + wide(back_b))
    own, text_out = lax.optimization_barrier((own, text_out))
    image_out = scale * (own + wide(home_l) + wide(home_r))
    losses, image_out = lax.optimization_barrier((losses, image_out))
    pair_count = DEVICES * n * 3 * 8 * n
    mean_loss = call(total_body, [((8, 128), f32)], (losses,), 4, scalars=0)[0][0, :1] / pair_count
    return image_out, text_out, mean_loss


def solution(mesh):
    fine = Mesh(mesh.devices.reshape(NY, 2, 2, NX, 2), AXES)
    placed = (P(AXES, None), P(AXES, None), P(), P())
    return jax.shard_map(
        local,
        mesh=fine,
        in_specs=placed,
        out_specs=(P(AXES, None), P(AXES, None), P()),
        check_vma=False,
    )
```

time: 85.3 us -> 80.8 us (0.947); the launches traced: 84.2 us -> 80.6 us
  other arithmetic: 11.5 us -> 7.01 us
  local copies, waits for them, and re-layouts: 1.39 us -> 0.52 us
    ppermute x16, waiting for transfers between devices: 18.6 us -> 28.2 us  [send(): return lax.ppermute(value, AXES, pairs)]
    all_to_all x1, waiting for transfers between devices: 8.88 us -> 0.01 us  [local(): losses = lax.all_to_all(out[5], CHIPS, 0, 0, tiled=True)]
    reduce_sum x2 -> x0, other arithmetic: 2.03 us -> none  [the longest x1 1.43 us: local(): mean_loss = (jnp.sum(losses[:, 0, 0]) / pair_count).reshape(1)]
    mul x1, other arithmetic: 2.51 us -> 1.2 us  [local(): text_out = scale * (sum_a + wide(back_z) + wide(back_a) + wide(back_b))]
    broadcast_in_dim x1 -> x0, local copies, waits for them, and re-layouts: 1.27 us -> none  [local(): loss = jnp.broadcast_to(jnp.sum(out[5]), (CHIP_COUNT, 1, 128))]
    convert_element_type x4 -> x3, other arithmetic: 2.73 us -> 1.48 us  [narrow(): return (value * SEND_SCALE).astype(jnp.float16)]
    add x1, other arithmetic: 0.01 us -> 1.21 us  [local(): sum_a + to_first[:n]]
    mul x1, other arithmetic: 2.26 us -> 1.12 us  [local(): image_out = scale * (own + wide(home_l) + wide(home_r))]
  transfers between devices with their start and end apart: 17 -> 17, of which waited for: 7 -> 6; matrix products, arithmetic and copies ran while one was open for 10% -> 7% of each run, Pallas kernels for 7% -> 9%
where the time goes in v3:
time: 80.8 us; the launch traced here: 80.6 us
  starting transfers between devices  29 us (36%)
  waiting for transfers between devices  28.2 us (35%)
  Pallas kernels  12.1 us (15%)
  other arithmetic  7.01 us (9%)
  between operations  3.84 us (5%)
    ppermute x16, waiting for transfers between devices, send(): return lax.ppermute(value, AXES, pairs)  28.2 us
    ppermute x16, starting transfers between devices, send(): return lax.ppermute(value, AXES, pairs)  21.8 us
    pallas_call x6, Pallas kernels, call(): pl.pallas_call(body, out_shape=tuple((jax.ShapeDtypeStruct(s, t) for s, t...  12.1 us
    all_to_all x1, starting transfers between devices, local(): losses = lax.all_to_all(out[5], CHIPS, 0, 0, tiled=True)  7.23 us
  transfers between devices with their start and end apart: 17, of which 6 were waited for; matrix products, arithmetic and copies ran while one was open for 7% of the time, Pallas kernels for 9%

profile of v3, /device:TPU:0, one launch (start us, length us, event | category | flops | bytes accessed | tf_op | source)
XLA Modules:
  0.0 80.6 jit_solution(4346746146023372271)
XLA Ops:
  0.6 1.3 %convert_element_type.48.ta = bf16[192,1152]{1,0:T(8,128)(2,1)S(1)} convert(f32[192,1152]{1,0:T(8,128)} %param.5) | non-fusion elementwise | flops 221184 | bytes 1327104 | tf_op jit(solution)/shard_map/convert_element_type | solution.py:200
  2.0 1.8 %collective-permute-done.own_o = bf16[192,1152]{1,0:T(8,128)(2,1)S(1)} collective-permute-done((bf16[192,1152]{1,0:T(8,128)(2,1)S(1)}, bf16[192,1152]{1,0:T(8,128)(2,1)S(1)}, u32[]{:S(2)}, u32[]{:S(2)}) %collective-permute-start) | collective-permute-done | bytes 442400 | tf_op jit(solution)/shard_map/ppermute | solution.py:61
  4.1 2.1 %collective-permute-start.1 = (bf16[384,1152]{1,0:T(8,128)(2,1)S(1)}, bf16[384,1152]{1,0:T(8,128)(2,1)S(1)}, u32[]{:S(2)}, u32[]{:S(2)}) collective-permute-start(bf16[384,1152]{1,0:T(8,128)(2,1)S(1)} %maximum_select_fusion), channel_id=1, source_target_pairs={{0,16},{2,18},{4,20},{6,22},{8,25},{10,27},{12,29},{14,31},{16,32}... | collective-permute-start | bytes 2654216 | tf_op jit(solution)/shard_map/ppermute | solution.py:61
  6.1 3.6 %collective-permute-start.2 = (bf16[192,1152]{1,0:T(8,128)(2,1)S(1)}, bf16[192,1152]{1,0:T(8,128)(2,1)S(1)}, u32[]{:S(2)}, u32[]{:S(2)}) collective-permute-start(bf16[192,1152]{1,0:T(8,128)(2,1)S(1)} %convert_element_type.48.ta), channel_id=1, source_target_pairs={{0,1},{2,3},{4,5},{6,7},{8,9},{10,11},{12,13},{14,15},{16,17},{18,... | collective-permute-start | bytes 1327112 | tf_op jit(solution)/shard_map/ppermute | solution.py:61
  9.8 3.1 %collective-permute-start.5 = (bf16[192,1152]{1,0:T(8,128)(2,1)S(1)}, bf16[192,1152]{1,0:T(8,128)(2,1)S(1)}, u32[]{:S(2)}, u32[]{:S(2)}) collective-permute-start(bf16[192,1152]{1,0:T(8,128)(2,1)S(1)} %convert_element_type.49.i0), channel_id=1, source_target_pairs={{0,4},{2,6},{4,0},{6,2},{8,12},{10,14},{12,8},{14,10},{16,20},{18,... | collective-permute-start | bytes 1327112 | tf_op jit(solution)/shard_map/ppermute | solution.py:61
  12.9 1.1 %collective-permute-start.4 = (bf16[192,1152]{1,0:T(8,128)(2,1)S(1)}, bf16[192,1152]{1,0:T(8,128)(2,1)S(1)}, u32[]{:S(2)}, u32[]{:S(2)}) collective-permute-start(bf16[192,1152]{1,0:T(8,128)(2,1)S(1)} %convert_element_type.49.i0), channel_id=1, source_target_pairs={{0,6},{2,0},{4,2},{6,4},{8,14},{10,8},{12,10},{14,12},{16,22},{18,... | collective-permute-start | bytes 1327112 | tf_op jit(solution)/shard_map/ppermute | solution.py:61
  16.3 16.2 %collective-permute-done.2.tb = bf16[192,1152]{1,0:T(8,128)(2,1)S(1)} collective-permute-done((bf16[192,1152]{1,0:T(8,128)(2,1)S(1)}, bf16[192,1152]{1,0:T(8,128)(2,1)S(1)}, u32[]{:S(2)}, u32[]{:S(2)}) %collective-permute-start.2) | collective-permute-done | bytes 442400 | tf_op jit(solution)/shard_map/ppermute | solution.py:61
  33.1 2.3 %shard_map.67 = (bf16[768,1152]{1,0:T(8,128)(2,1)S(1)}, bf16[384,1152]{1,0:T(8,128)(2,1)S(1)}, bf16[384,768]{1,0:T(8,128)(2,1)S(1)}, f32[8,128]{1,0:T(8,128)S(1)}) custom-call(f32[2]{0:T(128)S(1)} %pad_maximum_fusion.scalars, bf16[192,1152]{1,0:T(8,128)(2,1)S(1)} %convert_element_type.49.i0, bf16[192,1152]{1,0:T(8,128)(2,1)S(1)} %collective-permute-done.3.i1, ...), custom_call_target="tpu_custom_call" | custom-call | flops 679477248 | bytes 1048576 | tf_op jit(solution)/shard_map/pallas_call | solution.py:73
  35.7 5.1 %shard_map.68 = (bf16[768,1152]{1,0:T(8,128)(2,1)S(1)}, bf16[768,768]{1,0:T(8,128)(2,1)S(1)}, f32[192,1152]{1,0:T(8,128)S(1)}, f32[384,1152]{1,0:T(8,128)S(1)}, f32[8,128]{1,0:T(8,128)S(1)}) custom-call(f32[2]{0:T(128)S(1)} %pad_maximum_fusion.scalars, s32[1]{0:T(128)} %bitcast.core, bf16[768,1152]{1,0:T(8,128)(2,1)S(1)} %get-tuple-element.42.images, ...), custom_call_target="tpu_custom_call" | custom-call | flops 2717908992 | bytes 1048576 | tf_op jit(solution)/shard_map/pallas_call | solution.py:73
  41.7 1.6 %collective-permute-start.9 = (f16[192,1152]{1,0:T(8,128)(2,1)S(1)}, f16[192,1152]{1,0:T(8,128)(2,1)S(1)}, u32[]{:S(2)}, u32[]{:S(2)}) collective-permute-start(f16[192,1152]{1,0:T(8,128)(2,1)S(1)} %multiply_convert_fusion.3), channel_id=1, source_target_pairs={{0,2},{2,4},{4,6},{6,0},{8,14},{10,8},{12,10},{14,12},{16,18},{18,... | collective-permute-start | bytes 1327112 | tf_op jit(solution)/shard_map/ppermute | solution.py:61
  43.2 1.7 %shard_map.69 = (f32[192,1152]{1,0:T(8,128)S(1)}, f32[192,1152]{1,0:T(8,128)S(1)}, f32[384,1152]{1,0:T(8,128)S(1)}) custom-call(bf16[768,1152]{1,0:T(8,128)(2,1)S(1)} %get-tuple-element.42.images, bf16[384,768]{1,0:T(8,128)(2,1)S(1)} %get-tuple-element.53.w0, bf16[768,768]{1,0:T(8,128)(2,1)S(1)} %get-tuple-element.48.weights), custom_call_target="tpu_custom_call" | custom-call | flops 1358954496 | bytes 1048576 | tf_op jit(solution)/shard_map/pallas_call | solution.py:73
  46.0 1.2 %slice_add_fusion = (f32[192,1152]{1,0:T(8,128)S(1)}, f16[192,1152]{1,0:T(8,128)(2,1)}, f16[192,1152]{1,0:T(8,128)(2,1)}, f16[192,1152]{1,0:T(8,128)(2,1)}) fusion(f32[192,1152]{1,0:T(8,128)S(1)} %get-tuple-element.52, f32[384,1152]{1,0:T(8,128)S(1)} %get-tuple-element.76, f32[192,1152]{1,0:T(8,128)S(1)} %get-tuple-element.49, ...), kind=kLoop, calls=%fused_computation.4 | loop fusion | flops 1769472 | bytes 7520256 | tf_op jit(solution)/shard_map/add | solution.py:256
  47.3 1.2 %collective-permute-start.11 = (f16[192,1152]{1,0:T(8,128)(2,1)}, f16[192,1152]{1,0:T(8,128)(2,1)S(1)}, u32[]{:S(2)}, u32[]{:S(2)}) collective-permute-start(f16[192,1152]{1,0:T(8,128)(2,1)} %get-tuple-element.62), channel_id=1, source_target_pairs={{0,1},{2,3},{4,5},{6,7},{8,9},{10,11},{12,13},{14,15},{16,17},{18,... | collective-permute-start | bytes 1327112 | tf_op jit(solution)/shard_map/ppermute | solution.py:61
  48.5 2.5 %collective-permute-start.12 = (f16[192,1152]{1,0:T(8,128)(2,1)}, f16[192,1152]{1,0:T(8,128)(2,1)S(1)}, u32[]{:S(2)}, u32[]{:S(2)}) collective-permute-start(f16[192,1152]{1,0:T(8,128)(2,1)} %get-tuple-element.63), channel_id=1, source_target_pairs={{0,112},{2,114},{4,116},{6,118},{8,120},{10,122},{12,124},{14,126}... | collective-permute-start | bytes 1327112 | tf_op jit(solution)/shard_map/ppermute | solution.py:61
  51.0 1.5 %collective-permute-start.13 = (f16[192,1152]{1,0:T(8,128)(2,1)}, f16[192,1152]{1,0:T(8,128)(2,1)S(1)}, u32[]{:S(2)}, u32[]{:S(2)}) collective-permute-start(f16[192,1152]{1,0:T(8,128)(2,1)} %get-tuple-element.64), channel_id=1, source_target_pairs={{0,113},{2,115},{4,117},{6,119},{8,121},{10,123},{12,125},{14,127}... | collective-permute-start | bytes 1327112 | tf_op jit(solution)/shard_map/ppermute | solution.py:61
  52.6 2.1 %shard_map.70 = (f32[192,1152]{1,0:T(8,128)S(1)}, f32[192,1152]{1,0:T(8,128)S(1)}, f32[192,1152]{1,0:T(8,128)S(1)}) custom-call(bf16[384,768]{1,0:T(8,128)(2,1)S(1)} %get-tuple-element.53.w0, bf16[768,768]{1,0:T(8,128)(2,1)S(1)} %get-tuple-element.48.weights, bf16[384,1152]{1,0:T(8,128)(2,1)S(1)} %get-tuple-element.45.t0, ...), custom_call_target="tpu_custom_call" | custom-call | flops 1528823808 | bytes 1048576 | tf_op jit(solution)/shard_map/pallas_call | solution.py:73
  54.7 1.3 %multiply_convert_fusion.1 = (f16[192,1152]{1,0:T(8,128)(2,1)}, f16[192,1152]{1,0:T(8,128)(2,1)}) fusion(f32[192,1152]{1,0:T(8,128)S(1)} %get-tuple-element.57, f16[192,1152]{1,0:T(8,128)(2,1)S(1)} %collective-permute-done.9, pred[]{:T(512)S(6)} %eq.3, f32[192,1152]{1,0:T(8,128)S(1)} %get-tuple-element.55), kind=kLoop, calls=%fused_computation.15 | loop fusion | flops 2211840 | bytes 3096577 | tf_op jit(solution)/shard_map/convert_element_type | solution.py:184
  55.9 7.2 %all-to-all-start = ((f32[64,1,128]{2,1,0:T(1,128)}), f32[64,1,128]{2,1,0:T(1,128)S(1)}, u32[]{:S(2)}, u32[]{:S(2)}) async-start(f32[64,1,128]{2,1,0:T(1,128)} %shard_map.71), calls=%async_computation | async-start | bytes 65536 | tf_op jit(solution)/shard_map/all_to_all | solution.py:272
  63.1 2.9 %collective-permute-start.14 = (f16[192,1152]{1,0:T(8,128)(2,1)}, f16[192,1152]{1,0:T(8,128)(2,1)S(1)}, u32[]{:S(2)}, u32[]{:S(2)}) collective-permute-start(f16[192,1152]{1,0:T(8,128)(2,1)} %get-tuple-element.66), channel_id=1, source_target_pairs={{0,6},{2,0},{4,2},{6,4},{8,14},{10,8},{12,10},{14,12},{16,22},{18,... | collective-permute-start | bytes 1327112 | tf_op jit(solution)/shard_map/ppermute | solution.py:61
  66.0 5.7 %collective-permute-done.11 = f16[192,1152]{1,0:T(8,128)(2,1)S(1)} collective-permute-done((f16[192,1152]{1,0:T(8,128)(2,1)}, f16[192,1152]{1,0:T(8,128)(2,1)S(1)}, u32[]{:S(2)}, u32[]{:S(2)}) %collective-permute-start.11) | collective-permute-done | bytes 442400 | tf_op jit(solution)/shard_map/ppermute | solution.py:61
  71.7 2.1 %collective-permute-done.13 = f16[192,1152]{1,0:T(8,128)(2,1)S(1)} collective-permute-done((f16[192,1152]{1,0:T(8,128)(2,1)}, f16[192,1152]{1,0:T(8,128)(2,1)S(1)}, u32[]{:S(2)}, u32[]{:S(2)}) %collective-permute-start.13) | collective-permute-done | bytes 442400 | tf_op jit(solution)/shard_map/ppermute | solution.py:61
  73.8 1.2 %add_multiply_fusion.1 = f32[192,1152]{1,0:T(8,128)} fusion(f16[192,1152]{1,0:T(8,128)(2,1)S(1)} %collective-permute-done.13, f16[192,1152]{1,0:T(8,128)(2,1)S(1)} %collective-permute-done.12, f32[192,1152]{1,0:T(8,128)S(1)} %get-tuple-element.61, f16[192,1152]{1,0:T(8,128)(2,1)S(1)} %collective-permute-done.11, f32[]{:T(128)} %bitcast.3), kind=kLoop, calls=%fused_computation.14 | loop fusion | flops 2211840 | bytes 3096580 | tf_op jit(solution)/shard_map/mul | solution.py:273
  75.0 2.2 %collective-permute-done.15 = f16[192,1152]{1,0:T(8,128)(2,1)S(1)} collective-permute-done((f16[192,1152]{1,0:T(8,128)(2,1)}, f16[192,1152]{1,0:T(8,128)(2,1)S(1)}, u32[]{:S(2)}, u32[]{:S(2)}) %collective-permute-start.15) | collective-permute-done | bytes 442400 | tf_op jit(solution)/shard_map/ppermute | solution.py:61
  77.1 1.1 %add_multiply_fusion = f32[192,1152]{1,0:T(8,128)} fusion(f16[192,1152]{1,0:T(8,128)(2,1)S(1)} %collective-permute-done.15, f32[192,1152]{1,0:T(8,128)S(1)} %get-tuple-element.65, f16[192,1152]{1,0:T(8,128)(2,1)S(1)} %collective-permute-done.14, f32[]{:T(128)} %bitcast.4), kind=kLoop, calls=%fused_computation.13 | loop fusion | flops 1548288 | bytes 2654212 | tf_op jit(solution)/shard_map/mul | solution.py:275
  (30 shorter events, 4.7 us)
Async XLA Ops:
  0.6 9.1 %copy-start = (f32[192,1152]{1,0:T(8,128)S(1)}, f32[192,1152]{1,0:T(8,128)}, u32[]{:S(2)}) copy-start(f32[192,1152]{1,0:T(8,128)} %param.4) | copy-start | bytes 2654212
  1.9 1.9 %collective-permute-start = (bf16[192,1152]{1,0:T(8,128)(2,1)S(1)}, bf16[192,1152]{1,0:T(8,128)(2,1)S(1)}, u32[]{:S(2)}, u32[]{:S(2)}) collective-permute-start(bf16[192,1152]{1,0:T(8,128)(2,1)S(1)} %convert_element_type.48.ta), channel_id=1, source_target_pairs={{0,8},{2,10},{4,12},{6,14},{8,0},{10,2},{12,4},{14,6},{16,24},{18,... | collective-permute-start | bytes 1327112 | tf_op jit(solution)/shard_map/ppermute | solution.py:61
  4.1 28.5 %collective-permute-start.1 = (bf16[384,1152]{1,0:T(8,128)(2,1)S(1)}, bf16[384,1152]{1,0:T(8,128)(2,1)S(1)}, u32[]{:S(2)}, u32[]{:S(2)}) collective-permute-start(bf16[384,1152]{1,0:T(8,128)(2,1)S(1)} %maximum_select_fusion), channel_id=1, source_target_pairs={{0,16},{2,18},{4,20},{6,22},{8,25},{10,27},{12,29},{14,31},{16,32}... | collective-permute-start | bytes 2654216 | tf_op jit(solution)/shard_map/ppermute | solution.py:61
  6.1 26.4 %collective-permute-start.2 = (bf16[192,1152]{1,0:T(8,128)(2,1)S(1)}, bf16[192,1152]{1,0:T(8,128)(2,1)S(1)}, u32[]{:S(2)}, u32[]{:S(2)}) collective-permute-start(bf16[192,1152]{1,0:T(8,128)(2,1)S(1)} %convert_element_type.48.ta), channel_id=1, source_target_pairs={{0,1},{2,3},{4,5},{6,7},{8,9},{10,11},{12,13},{14,15},{16,17},{18,... | collective-permute-start | bytes 1327112 | tf_op jit(solution)/shard_map/ppermute | solution.py:61
  9.8 22.8 %collective-permute-start.5 = (bf16[192,1152]{1,0:T(8,128)(2,1)S(1)}, bf16[192,1152]{1,0:T(8,128)(2,1)S(1)}, u32[]{:S(2)}, u32[]{:S(2)}) collective-permute-start(bf16[192,1152]{1,0:T(8,128)(2,1)S(1)} %convert_element_type.49.i0), channel_id=1, source_target_pairs={{0,4},{2,6},{4,0},{6,2},{8,12},{10,14},{12,8},{14,10},{16,20},{18,... | collective-permute-start | bytes 1327112 | tf_op jit(solution)/shard_map/ppermute | solution.py:61
  12.9 19.7 %collective-permute-start.4 = (bf16[192,1152]{1,0:T(8,128)(2,1)S(1)}, bf16[192,1152]{1,0:T(8,128)(2,1)S(1)}, u32[]{:S(2)}, u32[]{:S(2)}) collective-permute-start(bf16[192,1152]{1,0:T(8,128)(2,1)S(1)} %convert_element_type.49.i0), channel_id=1, source_target_pairs={{0,6},{2,0},{4,2},{6,4},{8,14},{10,8},{12,10},{14,12},{16,22},{18,... | collective-permute-start | bytes 1327112 | tf_op jit(solution)/shard_map/ppermute | solution.py:61
  14.0 18.5 %collective-permute-start.3 = (bf16[192,1152]{1,0:T(8,128)(2,1)S(1)}, bf16[192,1152]{1,0:T(8,128)(2,1)S(1)}, u32[]{:S(2)}, u32[]{:S(2)}) collective-permute-start(bf16[192,1152]{1,0:T(8,128)(2,1)S(1)} %convert_element_type.49.i0), channel_id=1, source_target_pairs={{0,2},{2,4},{4,6},{6,0},{8,10},{10,12},{12,14},{14,8},{16,18},{18,... | collective-permute-start | bytes 1327112 | tf_op jit(solution)/shard_map/ppermute | solution.py:61
  32.6 3.1 %collective-permute-start.7 = (bf16[384,1152]{1,0:T(8,128)(2,1)S(1)}, bf16[384,1152]{1,0:T(8,128)(2,1)S(1)}, u32[]{:S(2)}, u32[]{:S(2)}) collective-permute-start(bf16[384,1152]{1,0:T(8,128)(2,1)S(1)} %collective-permute-done.1.far), channel_id=1, source_target_pairs={{0,8},{2,10},{4,12},{6,14},{8,0},{10,2},{12,4},{14,6},{16,24},{18,... | collective-permute-start | bytes 2654216 | tf_op jit(solution)/shard_map/ppermute | solution.py:61
  32.7 3.0 %collective-permute-start.6 = (bf16[192,1152]{1,0:T(8,128)(2,1)S(1)}, bf16[192,1152]{1,0:T(8,128)(2,1)S(1)}, u32[]{:S(2)}, u32[]{:S(2)}) collective-permute-start(bf16[192,1152]{1,0:T(8,128)(2,1)S(1)} %collective-permute-done.2.tb), channel_id=1, source_target_pairs={{0,8},{2,10},{4,12},{6,14},{8,0},{10,2},{12,4},{14,6},{16,24},{18,... | collective-permute-start | bytes 1327112 | tf_op jit(solution)/shard_map/ppermute | solution.py:61
  41.0 4.7 %collective-permute-start.8 = (f16[384,1152]{1,0:T(8,128)(2,1)S(1)}, f16[384,1152]{1,0:T(8,128)(2,1)S(1)}, u32[]{:S(2)}, u32[]{:S(2)}) collective-permute-start(f16[384,1152]{1,0:T(8,128)(2,1)S(1)} %multiply_convert_fusion), channel_id=1, source_target_pairs={{0,8},{2,10},{4,12},{6,14},{8,0},{10,2},{12,4},{14,6},{16,24},{18,... | collective-permute-start | bytes 2654216 | tf_op jit(solution)/shard_map/ppermute | solution.py:61
  41.2 3.7 %collective-permute-start.10 = (f32[8,128]{1,0:T(8,128)S(1)}, f32[8,128]{1,0:T(8,128)S(1)}, u32[]{:S(2)}, u32[]{:S(2)}) collective-permute-start(f32[8,128]{1,0:T(8,128)S(1)} %get-tuple-element.58.mine), channel_id=1, source_target_pairs={{0,8},{2,10},{4,12},{6,14},{8,0},{10,2},{12,4},{14,6},{16,24},{18,... | collective-permute-start | bytes 12296 | tf_op jit(solution)/shard_map/ppermute | solution.py:61
  41.7 13.0 %collective-permute-start.9 = (f16[192,1152]{1,0:T(8,128)(2,1)S(1)}, f16[192,1152]{1,0:T(8,128)(2,1)S(1)}, u32[]{:S(2)}, u32[]{:S(2)}) collective-permute-start(f16[192,1152]{1,0:T(8,128)(2,1)S(1)} %multiply_convert_fusion.3), channel_id=1, source_target_pairs={{0,2},{2,4},{4,6},{6,0},{8,14},{10,8},{12,10},{14,12},{16,18},{18,... | collective-permute-start | bytes 1327112 | tf_op jit(solution)/shard_map/ppermute | solution.py:61
  47.3 24.5 %collective-permute-start.11 = (f16[192,1152]{1,0:T(8,128)(2,1)}, f16[192,1152]{1,0:T(8,128)(2,1)S(1)}, u32[]{:S(2)}, u32[]{:S(2)}) collective-permute-start(f16[192,1152]{1,0:T(8,128)(2,1)} %get-tuple-element.62), channel_id=1, source_target_pairs={{0,1},{2,3},{4,5},{6,7},{8,9},{10,11},{12,13},{14,15},{16,17},{18,... | collective-permute-start | bytes 1327112 | tf_op jit(solution)/shard_map/ppermute | solution.py:61
  48.5 23.2 %collective-permute-start.12 = (f16[192,1152]{1,0:T(8,128)(2,1)}, f16[192,1152]{1,0:T(8,128)(2,1)S(1)}, u32[]{:S(2)}, u32[]{:S(2)}) collective-permute-start(f16[192,1152]{1,0:T(8,128)(2,1)} %get-tuple-element.63), channel_id=1, source_target_pairs={{0,112},{2,114},{4,116},{6,118},{8,120},{10,122},{12,124},{14,126}... | collective-permute-start | bytes 1327112 | tf_op jit(solution)/shard_map/ppermute | solution.py:61
  51.0 22.8 %collective-permute-start.13 = (f16[192,1152]{1,0:T(8,128)(2,1)}, f16[192,1152]{1,0:T(8,128)(2,1)S(1)}, u32[]{:S(2)}, u32[]{:S(2)}) collective-permute-start(f16[192,1152]{1,0:T(8,128)(2,1)} %get-tuple-element.64), channel_id=1, source_target_pairs={{0,113},{2,115},{4,117},{6,119},{8,121},{10,123},{12,125},{14,127}... | collective-permute-start | bytes 1327112 | tf_op jit(solution)/shard_map/ppermute | solution.py:61
  55.9 22.4 %all-to-all-start = ((f32[64,1,128]{2,1,0:T(1,128)}), f32[64,1,128]{2,1,0:T(1,128)S(1)}, u32[]{:S(2)}, u32[]{:S(2)}) async-start(f32[64,1,128]{2,1,0:T(1,128)} %shard_map.71), calls=%async_computation | async-start | bytes 65536 | tf_op jit(solution)/shard_map/all_to_all | solution.py:272
  63.1 11.8 %collective-permute-start.14 = (f16[192,1152]{1,0:T(8,128)(2,1)}, f16[192,1152]{1,0:T(8,128)(2,1)S(1)}, u32[]{:S(2)}, u32[]{:S(2)}) collective-permute-start(f16[192,1152]{1,0:T(8,128)(2,1)} %get-tuple-element.66), channel_id=1, source_target_pairs={{0,6},{2,0},{4,2},{6,4},{8,14},{10,8},{12,10},{14,12},{16,22},{18,... | collective-permute-start | bytes 1327112 | tf_op jit(solution)/shard_map/ppermute | solution.py:61
  66.0 11.1 %collective-permute-start.15 = (f16[192,1152]{1,0:T(8,128)(2,1)}, f16[192,1152]{1,0:T(8,128)(2,1)S(1)}, u32[]{:S(2)}, u32[]{:S(2)}) collective-permute-start(f16[192,1152]{1,0:T(8,128)(2,1)} %get-tuple-element.67), channel_id=1, source_target_pairs={{0,2},{2,4},{4,6},{6,0},{8,10},{10,12},{12,14},{14,8},{16,18},{18,... | collective-permute-start | bytes 1327112 | tf_op jit(solution)/shard_map/ppermute | solution.py:61

commit v4 on v3

--- a/solution.py
+++ b/solution.py
@@ -176,8 +176,8 @@
     out[...] = jnp.full(out.shape, total, jnp.float32)
 
 
-def total_body(parts, out):
-    out[...] = jnp.broadcast_to(jnp.sum(parts[...], axis=0), out.shape)
+def mean_body(pairs, parts, out):
+    out[0] = jnp.sum(parts[...][:, 0, :1]) / pairs
 
 
 def narrow(value):
@@ -251,7 +251,7 @@
     to_first = jnp.where(first_core, swapped, 0.0)
     sum_b = sum_b + to_first[n:]
     sum_2 = sum_2 + jnp.where(first_core, 0.0, swapped)
-    (loss,) = call(spread_body, [((CHIP_COUNT, 1, 128), f32)], (loss, send(loss, OTHER_CORE)), 4, scalars=0)
+    loss_o = send(loss, OTHER_CORE)
     out = lax.optimization_barrier(
         tuple(narrow(v) for v in (sum_b, sum_2[:n], sum_2[n:])) + (sum_a + to_first[:n], w0)
     )
@@ -262,7 +262,9 @@
     )
     left = left + jnp.where(first_core, 0.0, passed)
     right = right + jnp.where(first_core, passed, 0.0)
-    out = out + lax.optimization_barrier((narrow(left), narrow(right), loss))
+    out = out + lax.optimization_barrier((narrow(left), narrow(right), loss, loss_o))
+    (loss,) = call(spread_body, [((CHIP_COUNT, 1, 128), f32)], out[5:], 4, scalars=0)
+    out = out[:5] + (loss,)
     back_z = send(out[0], along_z(2))
     back_a = send(out[1], next_column(-1, lambda core: 0))
     back_b = send(out[2], next_column(-1, lambda core: 1))
@@ -275,7 +277,12 @@
     image_out = scale * (own + wide(home_l) + wide(home_r))
     losses, image_out = lax.optimization_barrier((losses, image_out))
     pair_count = DEVICES * n * 3 * 8 * n
-    mean_loss = call(total_body, [((8, 128), f32)], (losses,), 4, scalars=0)[0][0, :1] / pair_count
+    mean_loss = pl.pallas_call(
+        functools.partial(mean_body, pair_count),
+        out_shape=jax.ShapeDtypeStruct((1,), f32),
+        in_specs=[WHOLE],
+        out_specs=SCALAR,
+    )(losses)
     return image_out, text_out, mean_loss
 
 

time: 80.8 us -> 79.9 us (0.989)
  between operations: 3.84 us -> 2.22 us
  Pallas kernels: 12.1 us -> 13.4 us
    pallas_call x0 -> x1, Pallas kernels: none -> 1.41 us  [local(): pl.pallas_call(functools.partial(mean_body, pair_count), out_shape=jax.Sh...]
    pallas_call x6 -> x5, Pallas kernels: 12.1 us -> 12 us  [call(): pl.pallas_call(body, out_shape=tuple((jax.ShapeDtypeStruct(s, t) for s, t...]
  transfers between devices with their start and end apart: 17 -> 17, of which waited for: 6 -> 6; matrix products, arithmetic and copies ran while one was open for 7% -> 6% of each run, Pallas kernels for 9% -> 9%
where the time goes in v4:
time: 79.9 us; the launch traced here: 79.7 us
  starting transfers between devices  29.2 us (37%)
  waiting for transfers between devices  28 us (35%)
  Pallas kernels  13.4 us (17%)
  other arithmetic  6.84 us (9%)
  between operations  2.22 us (3%)
    ppermute x16, waiting for transfers between devices, send(): return lax.ppermute(value, AXES, pairs)  28 us
    ppermute x16, starting transfers between devices, send(): return lax.ppermute(value, AXES, pairs)  21.7 us
    pallas_call x5, Pallas kernels, call(): pl.pallas_call(body, out_shape=tuple((jax.ShapeDtypeStruct(s, t) for s, t...  12 us
    all_to_all x1, starting transfers between devices, local(): losses = lax.all_to_all(out[5], CHIPS, 0, 0, tiled=True)  7.49 us
  transfers between devices with their start and end apart: 17, of which 6 were waited for; matrix products, arithmetic and copies ran while one was open for 6% of the time, Pallas kernels for 9%

profile of v4, /device:TPU:0, one launch (start us, length us, event | category | flops | bytes accessed | tf_op | source)
XLA Modules:
  0.0 79.7 jit_solution(11532779163021557006)
XLA Ops:
  0.6 1.3 %convert_element_type.48.ta = bf16[192,1152]{1,0:T(8,128)(2,1)S(1)} convert(f32[192,1152]{1,0:T(8,128)} %param.5) | non-fusion elementwise | flops 221184 | bytes 1327104 | tf_op jit(solution)/shard_map/convert_element_type | solution.py:200
  2.0 1.8 %collective-permute-done.own_o = bf16[192,1152]{1,0:T(8,128)(2,1)S(1)} collective-permute-done((bf16[192,1152]{1,0:T(8,128)(2,1)S(1)}, bf16[192,1152]{1,0:T(8,128)(2,1)S(1)}, u32[]{:S(2)}, u32[]{:S(2)}) %collective-permute-start) | collective-permute-done | bytes 442400 | tf_op jit(solution)/shard_map/ppermute | solution.py:61
  4.1 2.1 %collective-permute-start.1 = (bf16[384,1152]{1,0:T(8,128)(2,1)S(1)}, bf16[384,1152]{1,0:T(8,128)(2,1)S(1)}, u32[]{:S(2)}, u32[]{:S(2)}) collective-permute-start(bf16[384,1152]{1,0:T(8,128)(2,1)S(1)} %maximum_select_fusion), channel_id=1, source_target_pairs={{0,16},{2,18},{4,20},{6,22},{8,25},{10,27},{12,29},{14,31},{16,32}... | collective-permute-start | bytes 2654216 | tf_op jit(solution)/shard_map/ppermute | solution.py:61
  6.1 3.6 %collective-permute-start.2 = (bf16[192,1152]{1,0:T(8,128)(2,1)S(1)}, bf16[192,1152]{1,0:T(8,128)(2,1)S(1)}, u32[]{:S(2)}, u32[]{:S(2)}) collective-permute-start(bf16[192,1152]{1,0:T(8,128)(2,1)S(1)} %convert_element_type.48.ta), channel_id=1, source_target_pairs={{0,1},{2,3},{4,5},{6,7},{8,9},{10,11},{12,13},{14,15},{16,17},{18,... | collective-permute-start | bytes 1327112 | tf_op jit(solution)/shard_map/ppermute | solution.py:61
  9.8 3.1 %collective-permute-start.5 = (bf16[192,1152]{1,0:T(8,128)(2,1)S(1)}, bf16[192,1152]{1,0:T(8,128)(2,1)S(1)}, u32[]{:S(2)}, u32[]{:S(2)}) collective-permute-start(bf16[192,1152]{1,0:T(8,128)(2,1)S(1)} %convert_element_type.49.i0), channel_id=1, source_target_pairs={{0,4},{2,6},{4,0},{6,2},{8,12},{10,14},{12,8},{14,10},{16,20},{18,... | collective-permute-start | bytes 1327112 | tf_op jit(solution)/shard_map/ppermute | solution.py:61
  12.9 1.1 %collective-permute-start.4 = (bf16[192,1152]{1,0:T(8,128)(2,1)S(1)}, bf16[192,1152]{1,0:T(8,128)(2,1)S(1)}, u32[]{:S(2)}, u32[]{:S(2)}) collective-permute-start(bf16[192,1152]{1,0:T(8,128)(2,1)S(1)} %convert_element_type.49.i0), channel_id=1, source_target_pairs={{0,6},{2,0},{4,2},{6,4},{8,14},{10,8},{12,10},{14,12},{16,22},{18,... | collective-permute-start | bytes 1327112 | tf_op jit(solution)/shard_map/ppermute | solution.py:61
  16.3 16.2 %collective-permute-done.2.tb = bf16[192,1152]{1,0:T(8,128)(2,1)S(1)} collective-permute-done((bf16[192,1152]{1,0:T(8,128)(2,1)S(1)}, bf16[192,1152]{1,0:T(8,128)(2,1)S(1)}, u32[]{:S(2)}, u32[]{:S(2)}) %collective-permute-start.2) | collective-permute-done | bytes 442400 | tf_op jit(solution)/shard_map/ppermute | solution.py:61
  33.1 2.3 %shard_map.67 = (bf16[768,1152]{1,0:T(8,128)(2,1)S(1)}, bf16[384,1152]{1,0:T(8,128)(2,1)S(1)}, bf16[384,768]{1,0:T(8,128)(2,1)S(1)}, f32[8,128]{1,0:T(8,128)S(1)}) custom-call(f32[2]{0:T(128)S(1)} %pad_maximum_fusion.scalars, bf16[192,1152]{1,0:T(8,128)(2,1)S(1)} %convert_element_type.49.i0, bf16[192,1152]{1,0:T(8,128)(2,1)S(1)} %collective-permute-done.3.i1, ...), custom_call_target="tpu_custom_call" | custom-call | flops 679477248 | bytes 1048576 | tf_op jit(solution)/shard_map/pallas_call | solution.py:73
  35.7 5.1 %shard_map.68 = (bf16[768,1152]{1,0:T(8,128)(2,1)S(1)}, bf16[768,768]{1,0:T(8,128)(2,1)S(1)}, f32[192,1152]{1,0:T(8,128)S(1)}, f32[384,1152]{1,0:T(8,128)S(1)}, f32[8,128]{1,0:T(8,128)S(1)}) custom-call(f32[2]{0:T(128)S(1)} %pad_maximum_fusion.scalars, s32[1]{0:T(128)} %bitcast.core, bf16[768,1152]{1,0:T(8,128)(2,1)S(1)} %get-tuple-element.43.images, ...), custom_call_target="tpu_custom_call" | custom-call | flops 2717908992 | bytes 1048576 | tf_op jit(solution)/shard_map/pallas_call | solution.py:73
  41.7 1.6 %collective-permute-start.9 = (f16[192,1152]{1,0:T(8,128)(2,1)S(1)}, f16[192,1152]{1,0:T(8,128)(2,1)S(1)}, u32[]{:S(2)}, u32[]{:S(2)}) collective-permute-start(f16[192,1152]{1,0:T(8,128)(2,1)S(1)} %multiply_convert_fusion.3), channel_id=1, source_target_pairs={{0,2},{2,4},{4,6},{6,0},{8,14},{10,8},{12,10},{14,12},{16,18},{18,... | collective-permute-start | bytes 1327112 | tf_op jit(solution)/shard_map/ppermute | solution.py:61
  43.2 1.7 %shard_map.69 = (f32[192,1152]{1,0:T(8,128)S(1)}, f32[192,1152]{1,0:T(8,128)S(1)}, f32[384,1152]{1,0:T(8,128)S(1)}) custom-call(bf16[768,1152]{1,0:T(8,128)(2,1)S(1)} %get-tuple-element.43.images, bf16[384,768]{1,0:T(8,128)(2,1)S(1)} %get-tuple-element.54.w0, bf16[768,768]{1,0:T(8,128)(2,1)S(1)} %get-tuple-element.49.weights), custom_call_target="tpu_custom_call" | custom-call | flops 1358954496 | bytes 1048576 | tf_op jit(solution)/shard_map/pallas_call | solution.py:73
  45.3 1.2 %slice_add_fusion = (f32[192,1152]{1,0:T(8,128)S(1)}, f16[192,1152]{1,0:T(8,128)(2,1)}, f16[192,1152]{1,0:T(8,128)(2,1)}, f16[192,1152]{1,0:T(8,128)(2,1)}) fusion(f32[192,1152]{1,0:T(8,128)S(1)} %get-tuple-element.53, f32[384,1152]{1,0:T(8,128)S(1)} %get-tuple-element.78, f32[192,1152]{1,0:T(8,128)S(1)} %get-tuple-element.50, ...), kind=kLoop, calls=%fused_computation.4 | loop fusion | flops 1769472 | bytes 7520256 | tf_op jit(solution)/shard_map/add | solution.py:256
  46.5 1.2 %collective-permute-start.11 = (f16[192,1152]{1,0:T(8,128)(2,1)}, f16[192,1152]{1,0:T(8,128)(2,1)S(1)}, u32[]{:S(2)}, u32[]{:S(2)}) collective-permute-start(f16[192,1152]{1,0:T(8,128)(2,1)} %get-tuple-element.64), channel_id=1, source_target_pairs={{0,1},{2,3},{4,5},{6,7},{8,9},{10,11},{12,13},{14,15},{16,17},{18,... | collective-permute-start | bytes 1327112 | tf_op jit(solution)/shard_map/ppermute | solution.py:61
  47.7 2.5 %collective-permute-start.12 = (f16[192,1152]{1,0:T(8,128)(2,1)}, f16[192,1152]{1,0:T(8,128)(2,1)S(1)}, u32[]{:S(2)}, u32[]{:S(2)}) collective-permute-start(f16[192,1152]{1,0:T(8,128)(2,1)} %get-tuple-element.65), channel_id=1, source_target_pairs={{0,112},{2,114},{4,116},{6,118},{8,120},{10,122},{12,124},{14,126}... | collective-permute-start | bytes 1327112 | tf_op jit(solution)/shard_map/ppermute | solution.py:61
  50.3 1.6 %collective-permute-start.13 = (f16[192,1152]{1,0:T(8,128)(2,1)}, f16[192,1152]{1,0:T(8,128)(2,1)S(1)}, u32[]{:S(2)}, u32[]{:S(2)}) collective-permute-start(f16[192,1152]{1,0:T(8,128)(2,1)} %get-tuple-element.66), channel_id=1, source_target_pairs={{0,113},{2,115},{4,117},{6,119},{8,121},{10,123},{12,125},{14,127}... | collective-permute-start | bytes 1327112 | tf_op jit(solution)/shard_map/ppermute | solution.py:61
  51.8 2.1 %shard_map.70 = (f32[192,1152]{1,0:T(8,128)S(1)}, f32[192,1152]{1,0:T(8,128)S(1)}, f32[192,1152]{1,0:T(8,128)S(1)}) custom-call(bf16[384,768]{1,0:T(8,128)(2,1)S(1)} %get-tuple-element.54.w0, bf16[768,768]{1,0:T(8,128)(2,1)S(1)} %get-tuple-element.49.weights, bf16[384,1152]{1,0:T(8,128)(2,1)S(1)} %get-tuple-element.46.t0, ...), custom_call_target="tpu_custom_call" | custom-call | flops 1528823808 | bytes 1048576 | tf_op jit(solution)/shard_map/pallas_call | solution.py:73
  55.7 7.5 %all-to-all-start = ((f32[64,1,128]{2,1,0:T(1,128)}), f32[64,1,128]{2,1,0:T(1,128)}, u32[]{:S(2)}, u32[]{:S(2)}) async-start(f32[64,1,128]{2,1,0:T(1,128)} %shard_map.71), calls=%async_computation | async-start | bytes 65536 | tf_op jit(solution)/shard_map/all_to_all | solution.py:274
  63.2 2.8 %collective-permute-start.14 = (f16[192,1152]{1,0:T(8,128)(2,1)}, f16[192,1152]{1,0:T(8,128)(2,1)S(1)}, u32[]{:S(2)}, u32[]{:S(2)}) collective-permute-start(f16[192,1152]{1,0:T(8,128)(2,1)} %get-tuple-element.68), channel_id=1, source_target_pairs={{0,6},{2,0},{4,2},{6,4},{8,14},{10,8},{12,10},{14,12},{16,22},{18,... | collective-permute-start | bytes 1327112 | tf_op jit(solution)/shard_map/ppermute | solution.py:61
  66.0 4.9 %collective-permute-done.11 = f16[192,1152]{1,0:T(8,128)(2,1)S(1)} collective-permute-done((f16[192,1152]{1,0:T(8,128)(2,1)}, f16[192,1152]{1,0:T(8,128)(2,1)S(1)}, u32[]{:S(2)}, u32[]{:S(2)}) %collective-permute-start.11) | collective-permute-done | bytes 442400 | tf_op jit(solution)/shard_map/ppermute | solution.py:61
  70.9 2.1 %collective-permute-done.13 = f16[192,1152]{1,0:T(8,128)(2,1)S(1)} collective-permute-done((f16[192,1152]{1,0:T(8,128)(2,1)}, f16[192,1152]{1,0:T(8,128)(2,1)S(1)}, u32[]{:S(2)}, u32[]{:S(2)}) %collective-permute-start.13) | collective-permute-done | bytes 442400 | tf_op jit(solution)/shard_map/ppermute | solution.py:61
  73.0 1.2 %add_multiply_fusion.1 = f32[192,1152]{1,0:T(8,128)} fusion(f16[192,1152]{1,0:T(8,128)(2,1)S(1)} %collective-permute-done.13, f16[192,1152]{1,0:T(8,128)(2,1)S(1)} %collective-permute-done.12, f32[192,1152]{1,0:T(8,128)S(1)} %get-tuple-element.63, f16[192,1152]{1,0:T(8,128)(2,1)S(1)} %collective-permute-done.11, f32[]{:T(128)} %bitcast.2), kind=kLoop, calls=%fused_computation.14 | loop fusion | flops 2211840 | bytes 3096580 | tf_op jit(solution)/shard_map/mul | solution.py:275
  74.2 2.7 %collective-permute-done.15 = f16[192,1152]{1,0:T(8,128)(2,1)S(1)} collective-permute-done((f16[192,1152]{1,0:T(8,128)(2,1)S(1)}, f16[192,1152]{1,0:T(8,128)(2,1)S(1)}, u32[]{:S(2)}, u32[]{:S(2)}) %collective-permute-start.15) | collective-permute-done | bytes 442400 | tf_op jit(solution)/shard_map/ppermute | solution.py:61
  77.0 1.1 %add_multiply_fusion = f32[192,1152]{1,0:T(8,128)} fusion(f16[192,1152]{1,0:T(8,128)(2,1)S(1)} %collective-permute-done.15, f32[192,1152]{1,0:T(8,128)S(1)} %get-tuple-element.67, f16[192,1152]{1,0:T(8,128)(2,1)S(1)} %collective-permute-done.14, f32[]{:T(128)} %bitcast.3), kind=kLoop, calls=%fused_computation.13 | loop fusion | flops 1548288 | bytes 2654212 | tf_op jit(solution)/shard_map/mul | solution.py:277
  78.1 1.4 %shard_map.72 = f32[1]{0:T(128)} custom-call(f32[64,1,128]{2,1,0:T(1,128)} %all-to-all-done.parts), custom_call_target="tpu_custom_call" | custom-call | tf_op jit(solution)/shard_map/pallas_call | solution.py:280
  (29 shorter events, 5.2 us)
Async XLA Ops:
  0.6 9.1 %copy-start = (f32[192,1152]{1,0:T(8,128)S(1)}, f32[192,1152]{1,0:T(8,128)}, u32[]{:S(2)}) copy-start(f32[192,1152]{1,0:T(8,128)} %param.4) | copy-start | bytes 2654212
  1.9 1.9 %collective-permute-start = (bf16[192,1152]{1,0:T(8,128)(2,1)S(1)}, bf16[192,1152]{1,0:T(8,128)(2,1)S(1)}, u32[]{:S(2)}, u32[]{:S(2)}) collective-permute-start(bf16[192,1152]{1,0:T(8,128)(2,1)S(1)} %convert_element_type.48.ta), channel_id=1, source_target_pairs={{0,8},{2,10},{4,12},{6,14},{8,0},{10,2},{12,4},{14,6},{16,24},{18,... | collective-permute-start | bytes 1327112 | tf_op jit(solution)/shard_map/ppermute | solution.py:61
  4.1 28.5 %collective-permute-start.1 = (bf16[384,1152]{1,0:T(8,128)(2,1)S(1)}, bf16[384,1152]{1,0:T(8,128)(2,1)S(1)}, u32[]{:S(2)}, u32[]{:S(2)}) collective-permute-start(bf16[384,1152]{1,0:T(8,128)(2,1)S(1)} %maximum_select_fusion), channel_id=1, source_target_pairs={{0,16},{2,18},{4,20},{6,22},{8,25},{10,27},{12,29},{14,31},{16,32}... | collective-permute-start | bytes 2654216 | tf_op jit(solution)/shard_map/ppermute | solution.py:61
  6.1 26.4 %collective-permute-start.2 = (bf16[192,1152]{1,0:T(8,128)(2,1)S(1)}, bf16[192,1152]{1,0:T(8,128)(2,1)S(1)}, u32[]{:S(2)}, u32[]{:S(2)}) collective-permute-start(bf16[192,1152]{1,0:T(8,128)(2,1)S(1)} %convert_element_type.48.ta), channel_id=1, source_target_pairs={{0,1},{2,3},{4,5},{6,7},{8,9},{10,11},{12,13},{14,15},{16,17},{18,... | collective-permute-start | bytes 1327112 | tf_op jit(solution)/shard_map/ppermute | solution.py:61
  9.8 22.8 %collective-permute-start.5 = (bf16[192,1152]{1,0:T(8,128)(2,1)S(1)}, bf16[192,1152]{1,0:T(8,128)(2,1)S(1)}, u32[]{:S(2)}, u32[]{:S(2)}) collective-permute-start(bf16[192,1152]{1,0:T(8,128)(2,1)S(1)} %convert_element_type.49.i0), channel_id=1, source_target_pairs={{0,4},{2,6},{4,0},{6,2},{8,12},{10,14},{12,8},{14,10},{16,20},{18,... | collective-permute-start | bytes 1327112 | tf_op jit(solution)/shard_map/ppermute | solution.py:61
  12.9 19.7 %collective-permute-start.4 = (bf16[192,1152]{1,0:T(8,128)(2,1)S(1)}, bf16[192,1152]{1,0:T(8,128)(2,1)S(1)}, u32[]{:S(2)}, u32[]{:S(2)}) collective-permute-start(bf16[192,1152]{1,0:T(8,128)(2,1)S(1)} %convert_element_type.49.i0), channel_id=1, source_target_pairs={{0,6},{2,0},{4,2},{6,4},{8,14},{10,8},{12,10},{14,12},{16,22},{18,... | collective-permute-start | bytes 1327112 | tf_op jit(solution)/shard_map/ppermute | solution.py:61
  14.0 18.5 %collective-permute-start.3 = (bf16[192,1152]{1,0:T(8,128)(2,1)S(1)}, bf16[192,1152]{1,0:T(8,128)(2,1)S(1)}, u32[]{:S(2)}, u32[]{:S(2)}) collective-permute-start(bf16[192,1152]{1,0:T(8,128)(2,1)S(1)} %convert_element_type.49.i0), channel_id=1, source_target_pairs={{0,2},{2,4},{4,6},{6,0},{8,10},{10,12},{12,14},{14,8},{16,18},{18,... | collective-permute-start | bytes 1327112 | tf_op jit(solution)/shard_map/ppermute | solution.py:61
  32.6 3.1 %collective-permute-start.7 = (bf16[384,1152]{1,0:T(8,128)(2,1)S(1)}, bf16[384,1152]{1,0:T(8,128)(2,1)S(1)}, u32[]{:S(2)}, u32[]{:S(2)}) collective-permute-start(bf16[384,1152]{1,0:T(8,128)(2,1)S(1)} %collective-permute-done.1.far), channel_id=1, source_target_pairs={{0,8},{2,10},{4,12},{6,14},{8,0},{10,2},{12,4},{14,6},{16,24},{18,... | collective-permute-start | bytes 2654216 | tf_op jit(solution)/shard_map/ppermute | solution.py:61
  32.7 3.0 %collective-permute-start.6 = (bf16[192,1152]{1,0:T(8,128)(2,1)S(1)}, bf16[192,1152]{1,0:T(8,128)(2,1)S(1)}, u32[]{:S(2)}, u32[]{:S(2)}) collective-permute-start(bf16[192,1152]{1,0:T(8,128)(2,1)S(1)} %collective-permute-done.2.tb), channel_id=1, source_target_pairs={{0,8},{2,10},{4,12},{6,14},{8,0},{10,2},{12,4},{14,6},{16,24},{18,... | collective-permute-start | bytes 1327112 | tf_op jit(solution)/shard_map/ppermute | solution.py:61
  41.0 3.9 %collective-permute-start.8 = (f16[384,1152]{1,0:T(8,128)(2,1)S(1)}, f16[384,1152]{1,0:T(8,128)(2,1)S(1)}, u32[]{:S(2)}, u32[]{:S(2)}) collective-permute-start(f16[384,1152]{1,0:T(8,128)(2,1)S(1)} %multiply_convert_fusion), channel_id=1, source_target_pairs={{0,8},{2,10},{4,12},{6,14},{8,0},{10,2},{12,4},{14,6},{16,24},{18,... | collective-permute-start | bytes 2654216 | tf_op jit(solution)/shard_map/ppermute | solution.py:61
  41.2 13.8 %collective-permute-start.10 = (f32[8,128]{1,0:T(8,128)S(1)}, f32[8,128]{1,0:T(8,128)S(1)}, u32[]{:S(2)}, u32[]{:S(2)}) collective-permute-start(f32[8,128]{1,0:T(8,128)S(1)} %get-tuple-element.60.mine), channel_id=1, source_target_pairs={{0,8},{2,10},{4,12},{6,14},{8,0},{10,2},{12,4},{14,6},{16,24},{18,... | collective-permute-start | bytes 12296 | tf_op jit(solution)/shard_map/ppermute | solution.py:61
  41.7 12.2 %collective-permute-start.9 = (f16[192,1152]{1,0:T(8,128)(2,1)S(1)}, f16[192,1152]{1,0:T(8,128)(2,1)S(1)}, u32[]{:S(2)}, u32[]{:S(2)}) collective-permute-start(f16[192,1152]{1,0:T(8,128)(2,1)S(1)} %multiply_convert_fusion.3), channel_id=1, source_target_pairs={{0,2},{2,4},{4,6},{6,0},{8,14},{10,8},{12,10},{14,12},{16,18},{18,... | collective-permute-start | bytes 1327112 | tf_op jit(solution)/shard_map/ppermute | solution.py:61
  46.5 24.4 %collective-permute-start.11 = (f16[192,1152]{1,0:T(8,128)(2,1)}, f16[192,1152]{1,0:T(8,128)(2,1)S(1)}, u32[]{:S(2)}, u32[]{:S(2)}) collective-permute-start(f16[192,1152]{1,0:T(8,128)(2,1)} %get-tuple-element.64), channel_id=1, source_target_pairs={{0,1},{2,3},{4,5},{6,7},{8,9},{10,11},{12,13},{14,15},{16,17},{18,... | collective-permute-start | bytes 1327112 | tf_op jit(solution)/shard_map/ppermute | solution.py:61
  47.7 23.2 %collective-permute-start.12 = (f16[192,1152]{1,0:T(8,128)(2,1)}, f16[192,1152]{1,0:T(8,128)(2,1)S(1)}, u32[]{:S(2)}, u32[]{:S(2)}) collective-permute-start(f16[192,1152]{1,0:T(8,128)(2,1)} %get-tuple-element.65), channel_id=1, source_target_pairs={{0,112},{2,114},{4,116},{6,118},{8,120},{10,122},{12,124},{14,126}... | collective-permute-start | bytes 1327112 | tf_op jit(solution)/shard_map/ppermute | solution.py:61
  50.3 22.8 %collective-permute-start.13 = (f16[192,1152]{1,0:T(8,128)(2,1)}, f16[192,1152]{1,0:T(8,128)(2,1)S(1)}, u32[]{:S(2)}, u32[]{:S(2)}) collective-permute-start(f16[192,1152]{1,0:T(8,128)(2,1)} %get-tuple-element.66), channel_id=1, source_target_pairs={{0,113},{2,115},{4,117},{6,119},{8,121},{10,123},{12,125},{14,127}... | collective-permute-start | bytes 1327112 | tf_op jit(solution)/shard_map/ppermute | solution.py:61
  55.7 22.3 %all-to-all-start = ((f32[64,1,128]{2,1,0:T(1,128)}), f32[64,1,128]{2,1,0:T(1,128)}, u32[]{:S(2)}, u32[]{:S(2)}) async-start(f32[64,1,128]{2,1,0:T(1,128)} %shard_map.71), calls=%async_computation | async-start | bytes 65536 | tf_op jit(solution)/shard_map/all_to_all | solution.py:274
  63.2 11.0 %collective-permute-start.14 = (f16[192,1152]{1,0:T(8,128)(2,1)}, f16[192,1152]{1,0:T(8,128)(2,1)S(1)}, u32[]{:S(2)}, u32[]{:S(2)}) collective-permute-start(f16[192,1152]{1,0:T(8,128)(2,1)} %get-tuple-element.68), channel_id=1, source_target_pairs={{0,6},{2,0},{4,2},{6,4},{8,14},{10,8},{12,10},{14,12},{16,22},{18,... | collective-permute-start | bytes 1327112 | tf_op jit(solution)/shard_map/ppermute | solution.py:61
  66.0 11.0 %collective-permute-start.15 = (f16[192,1152]{1,0:T(8,128)(2,1)S(1)}, f16[192,1152]{1,0:T(8,128)(2,1)S(1)}, u32[]{:S(2)}, u32[]{:S(2)}) collective-permute-start(f16[192,1152]{1,0:T(8,128)(2,1)S(1)} %get-tuple-element.69), channel_id=1, source_target_pairs={{0,2},{2,4},{4,6},{6,0},{8,10},{10,12},{12,14},{14,8},{16,18},{18,... | collective-permute-start | bytes 1327112 | tf_op jit(solution)/shard_map/ppermute | solution.py:61

commit v5 on v4

--- a/solution.py
+++ b/solution.py
@@ -53,7 +53,8 @@
     return route(move)
 
 
-ACROSS = route(lambda y, z, core, x: (y, z, core, x + 1 - 2 * core))
+AHEAD = route(lambda y, z, core, x: (y, z, core, x + 1 - 2 * core))
+BEHIND = route(lambda y, z, core, x: (y, z, core, x - 1 + 2 * core))
 OTHER_CORE = route(lambda y, z, core, x: (y, z, core + 1, x))
 
 
@@ -207,8 +208,8 @@
     )
     far = send(both, next_column(1, lambda core: core))
     text_z = send(text_b, along_z(2))
-    image_l = send(image_b, along_x(1))
-    image_r = send(image_b, along_x(-1))
+    image_l = send(image_b, AHEAD)
+    image_r = send(image_b, BEHIND)
     image_f = send(image_b, along_x(2))
     far, text_z, image_l, image_r, image_f, scalars, core = lax.optimization_barrier(
         (far, text_z, image_l, image_r, image_f, scalars, core)
@@ -237,7 +238,7 @@
         scalars=2,
         scratch=[pltpu.VMEM((2, 4 * n, 2 * n), f32)],
     )
-    passed = send(narrow(across), ACROSS)
+    passed = send(narrow(across), AHEAD)
     swapped = send(narrow(sum_1), OTHER_CORE)
     sum_a, sum_b, sum_2 = call(
         text_body,
@@ -260,16 +261,15 @@
     own, left, right = call(
         image_body, [((n, width), f32)] * 3, (w0, weights, t0, text), 9 * unit // 2, scalars=0
     )
-    left = left + jnp.where(first_core, 0.0, passed)
-    right = right + jnp.where(first_core, passed, 0.0)
+    right = right + passed
     out = out + lax.optimization_barrier((narrow(left), narrow(right), loss, loss_o))
     (loss,) = call(spread_body, [((CHIP_COUNT, 1, 128), f32)], out[5:], 4, scalars=0)
     out = out[:5] + (loss,)
     back_z = send(out[0], along_z(2))
     back_a = send(out[1], next_column(-1, lambda core: 0))
     back_b = send(out[2], next_column(-1, lambda core: 1))
-    home_l = send(out[3], along_x(-1))
-    home_r = send(out[4], along_x(1))
+    home_l = send(out[3], BEHIND)
+    home_r = send(out[4], AHEAD)
 
     losses = lax.all_to_all(out[5], CHIPS, 0, 0, tiled=True)
     text_out = scale * (sum_a + wide(back_z) + wide(back_a) + wide(back_b))

time: 79.9 us -> 78.3 us (0.980)
  waiting for transfers between devices: 28 us -> 26.6 us
    ppermute x16, waiting for transfers between devices: 28 us -> 26.6 us  [send(): return lax.ppermute(value, AXES, pairs)]
  transfers between devices with their start and end apart: 17 -> 17, of which waited for: 6 -> 7; matrix products, arithmetic and copies ran while one was open for 6% -> 7% of each run, Pallas kernels for 9% -> 9%
where the time goes in v5:
time: 78.3 us; the launch traced here: 78.1 us
  starting transfers between devices  29.1 us (37%)
  waiting for transfers between devices  26.6 us (34%)
  Pallas kernels  13.4 us (17%)
  other arithmetic  6.79 us (9%)
  between operations  2.22 us (3%)
    ppermute x16, waiting for transfers between devices, send(): return lax.ppermute(value, AXES, pairs)  26.6 us
    ppermute x16, starting transfers between devices, send(): return lax.ppermute(value, AXES, pairs)  21.7 us
    pallas_call x5, Pallas kernels, call(): pl.pallas_call(body, out_shape=tuple((jax.ShapeDtypeStruct(s, t) for s, t...  12 us
    all_to_all x1, starting transfers between devices, local(): losses = lax.all_to_all(out[5], CHIPS, 0, 0, tiled=True)  7.4 us
  transfers between devices with their start and end apart: 17, of which 7 were waited for; matrix products, arithmetic and copies ran while one was open for 7% of the time, Pallas kernels for 9%

profile of v5, /device:TPU:0, one launch (start us, length us, event | category | flops | bytes accessed | tf_op | source)
XLA Modules:
  0.0 78.1 jit_solution(8860163669510613614)
XLA Ops:
  0.6 1.3 %convert_element_type.48.ta = bf16[192,1152]{1,0:T(8,128)(2,1)S(1)} convert(f32[192,1152]{1,0:T(8,128)} %param.5) | non-fusion elementwise | flops 221184 | bytes 1327104 | tf_op jit(solution)/shard_map/convert_element_type | solution.py:201
  2.0 1.8 %collective-permute-done.own_o = bf16[192,1152]{1,0:T(8,128)(2,1)S(1)} collective-permute-done((bf16[192,1152]{1,0:T(8,128)(2,1)S(1)}, bf16[192,1152]{1,0:T(8,128)(2,1)S(1)}, u32[]{:S(2)}, u32[]{:S(2)}) %collective-permute-start) | collective-permute-done | bytes 442400 | tf_op jit(solution)/shard_map/ppermute | solution.py:62
  4.1 2.1 %collective-permute-start.1 = (bf16[384,1152]{1,0:T(8,128)(2,1)S(1)}, bf16[384,1152]{1,0:T(8,128)(2,1)S(1)}, u32[]{:S(2)}, u32[]{:S(2)}) collective-permute-start(bf16[384,1152]{1,0:T(8,128)(2,1)S(1)} %maximum_select_fusion), channel_id=1, source_target_pairs={{0,16},{2,18},{4,20},{6,22},{8,25},{10,27},{12,29},{14,31},{16,32}... | collective-permute-start | bytes 2654216 | tf_op jit(solution)/shard_map/ppermute | solution.py:62
  6.1 3.6 %collective-permute-start.2 = (bf16[192,1152]{1,0:T(8,128)(2,1)S(1)}, bf16[192,1152]{1,0:T(8,128)(2,1)S(1)}, u32[]{:S(2)}, u32[]{:S(2)}) collective-permute-start(bf16[192,1152]{1,0:T(8,128)(2,1)S(1)} %convert_element_type.48.ta), channel_id=1, source_target_pairs={{0,1},{2,3},{4,5},{6,7},{8,9},{10,11},{12,13},{14,15},{16,17},{18,... | collective-permute-start | bytes 1327112 | tf_op jit(solution)/shard_map/ppermute | solution.py:62
  9.8 3.1 %collective-permute-start.5 = (bf16[192,1152]{1,0:T(8,128)(2,1)S(1)}, bf16[192,1152]{1,0:T(8,128)(2,1)S(1)}, u32[]{:S(2)}, u32[]{:S(2)}) collective-permute-start(bf16[192,1152]{1,0:T(8,128)(2,1)S(1)} %convert_element_type.49.i0), channel_id=1, source_target_pairs={{0,4},{2,6},{4,0},{6,2},{8,12},{10,14},{12,8},{14,10},{16,20},{18,... | collective-permute-start | bytes 1327112 | tf_op jit(solution)/shard_map/ppermute | solution.py:62
  12.9 1.1 %collective-permute-start.4 = (bf16[192,1152]{1,0:T(8,128)(2,1)S(1)}, bf16[192,1152]{1,0:T(8,128)(2,1)S(1)}, u32[]{:S(2)}, u32[]{:S(2)}) collective-permute-start(bf16[192,1152]{1,0:T(8,128)(2,1)S(1)} %convert_element_type.49.i0), channel_id=1, source_target_pairs={{0,6},{2,0},{4,2},{6,4},{8,10},{10,12},{12,14},{14,8},{16,22},{18,... | collective-permute-start | bytes 1327112 | tf_op jit(solution)/shard_map/ppermute | solution.py:62
  14.0 0.9 %collective-permute-start.3 = (bf16[192,1152]{1,0:T(8,128)(2,1)S(1)}, bf16[192,1152]{1,0:T(8,128)(2,1)S(1)}, u32[]{:S(2)}, u32[]{:S(2)}) collective-permute-start(bf16[192,1152]{1,0:T(8,128)(2,1)S(1)} %convert_element_type.49.i0), channel_id=1, source_target_pairs={{0,2},{2,4},{4,6},{6,0},{8,14},{10,8},{12,10},{14,12},{16,18},{18,... | collective-permute-start | bytes 1327112 | tf_op jit(solution)/shard_map/ppermute | solution.py:62
  16.3 16.2 %collective-permute-done.2.tb = bf16[192,1152]{1,0:T(8,128)(2,1)S(1)} collective-permute-done((bf16[192,1152]{1,0:T(8,128)(2,1)S(1)}, bf16[192,1152]{1,0:T(8,128)(2,1)S(1)}, u32[]{:S(2)}, u32[]{:S(2)}) %collective-permute-start.2) | collective-permute-done | bytes 442400 | tf_op jit(solution)/shard_map/ppermute | solution.py:62
  33.1 2.3 %shard_map.67 = (bf16[768,1152]{1,0:T(8,128)(2,1)S(1)}, bf16[384,1152]{1,0:T(8,128)(2,1)S(1)}, bf16[384,768]{1,0:T(8,128)(2,1)S(1)}, f32[8,128]{1,0:T(8,128)S(1)}) custom-call(f32[2]{0:T(128)S(1)} %pad_maximum_fusion.scalars, bf16[192,1152]{1,0:T(8,128)(2,1)S(1)} %convert_element_type.49.i0, bf16[192,1152]{1,0:T(8,128)(2,1)S(1)} %collective-permute-done.3.i1, ...), custom_call_target="tpu_custom_call" | custom-call | flops 679477248 | bytes 1048576 | tf_op jit(solution)/shard_map/pallas_call | solution.py:74
  35.7 5.2 %shard_map.68 = (bf16[768,1152]{1,0:T(8,128)(2,1)S(1)}, bf16[768,768]{1,0:T(8,128)(2,1)S(1)}, f32[192,1152]{1,0:T(8,128)S(1)}, f32[384,1152]{1,0:T(8,128)S(1)}, f32[8,128]{1,0:T(8,128)S(1)}) custom-call(f32[2]{0:T(128)S(1)} %pad_maximum_fusion.scalars, s32[1]{0:T(128)} %bitcast.core, bf16[768,1152]{1,0:T(8,128)(2,1)S(1)} %get-tuple-element.43.images, ...), custom_call_target="tpu_custom_call" | custom-call | flops 2717908992 | bytes 1048576 | tf_op jit(solution)/shard_map/pallas_call | solution.py:74
  41.7 1.6 %collective-permute-start.9 = (f16[192,1152]{1,0:T(8,128)(2,1)S(1)}, f16[192,1152]{1,0:T(8,128)(2,1)S(1)}, u32[]{:S(2)}, u32[]{:S(2)}) collective-permute-start(f16[192,1152]{1,0:T(8,128)(2,1)S(1)} %multiply_convert_fusion.2), channel_id=1, source_target_pairs={{0,2},{2,4},{4,6},{6,0},{8,14},{10,8},{12,10},{14,12},{16,18},{18,... | collective-permute-start | bytes 1327112 | tf_op jit(solution)/shard_map/ppermute | solution.py:62
  43.2 1.7 %shard_map.69 = (f32[192,1152]{1,0:T(8,128)S(1)}, f32[192,1152]{1,0:T(8,128)S(1)}, f32[384,1152]{1,0:T(8,128)S(1)}) custom-call(bf16[768,1152]{1,0:T(8,128)(2,1)S(1)} %get-tuple-element.43.images, bf16[384,768]{1,0:T(8,128)(2,1)S(1)} %get-tuple-element.54.w0, bf16[768,768]{1,0:T(8,128)(2,1)S(1)} %get-tuple-element.49.weights), custom_call_target="tpu_custom_call" | custom-call | flops 1358954496 | bytes 1048576 | tf_op jit(solution)/shard_map/pallas_call | solution.py:74
  45.3 1.2 %slice_add_fusion = (f32[192,1152]{1,0:T(8,128)S(1)}, f16[192,1152]{1,0:T(8,128)(2,1)}, f16[192,1152]{1,0:T(8,128)(2,1)}, f16[192,1152]{1,0:T(8,128)(2,1)}) fusion(f32[192,1152]{1,0:T(8,128)S(1)} %get-tuple-element.53, f32[384,1152]{1,0:T(8,128)S(1)} %get-tuple-element.78, f32[192,1152]{1,0:T(8,128)S(1)} %get-tuple-element.50, ...), kind=kLoop, calls=%fused_computation.4 | loop fusion | flops 1769472 | bytes 7520256 | tf_op jit(solution)/shard_map/add | solution.py:257
  46.5 1.2 %collective-permute-start.11 = (f16[192,1152]{1,0:T(8,128)(2,1)}, f16[192,1152]{1,0:T(8,128)(2,1)S(1)}, u32[]{:S(2)}, u32[]{:S(2)}) collective-permute-start(f16[192,1152]{1,0:T(8,128)(2,1)} %get-tuple-element.64), channel_id=1, source_target_pairs={{0,1},{2,3},{4,5},{6,7},{8,9},{10,11},{12,13},{14,15},{16,17},{18,... | collective-permute-start | bytes 1327112 | tf_op jit(solution)/shard_map/ppermute | solution.py:62
  47.7 2.5 %collective-permute-start.12 = (f16[192,1152]{1,0:T(8,128)(2,1)}, f16[192,1152]{1,0:T(8,128)(2,1)S(1)}, u32[]{:S(2)}, u32[]{:S(2)}) collective-permute-start(f16[192,1152]{1,0:T(8,128)(2,1)} %get-tuple-element.65), channel_id=1, source_target_pairs={{0,112},{2,114},{4,116},{6,118},{8,120},{10,122},{12,124},{14,126}... | collective-permute-start | bytes 1327112 | tf_op jit(solution)/shard_map/ppermute | solution.py:62
  50.2 1.6 %collective-permute-start.13 = (f16[192,1152]{1,0:T(8,128)(2,1)}, f16[192,1152]{1,0:T(8,128)(2,1)S(1)}, u32[]{:S(2)}, u32[]{:S(2)}) collective-permute-start(f16[192,1152]{1,0:T(8,128)(2,1)} %get-tuple-element.66), channel_id=1, source_target_pairs={{0,113},{2,115},{4,117},{6,119},{8,121},{10,123},{12,125},{14,127}... | collective-permute-start | bytes 1327112 | tf_op jit(solution)/shard_map/ppermute | solution.py:62
  51.8 2.1 %shard_map.70 = (f32[192,1152]{1,0:T(8,128)S(1)}, f32[192,1152]{1,0:T(8,128)S(1)}, f32[192,1152]{1,0:T(8,128)S(1)}) custom-call(bf16[384,768]{1,0:T(8,128)(2,1)S(1)} %get-tuple-element.54.w0, bf16[768,768]{1,0:T(8,128)(2,1)S(1)} %get-tuple-element.49.weights, bf16[384,1152]{1,0:T(8,128)(2,1)S(1)} %get-tuple-element.46.t0, ...), custom_call_target="tpu_custom_call" | custom-call | flops 1528823808 | bytes 1048576 | tf_op jit(solution)/shard_map/pallas_call | solution.py:74
  55.7 7.4 %all-to-all-start = ((f32[64,1,128]{2,1,0:T(1,128)}), f32[64,1,128]{2,1,0:T(1,128)}, u32[]{:S(2)}, u32[]{:S(2)}) async-start(f32[64,1,128]{2,1,0:T(1,128)} %shard_map.71), calls=%async_computation | async-start | bytes 65536 | tf_op jit(solution)/shard_map/all_to_all | solution.py:274
  63.1 2.8 %collective-permute-start.14 = (f16[192,1152]{1,0:T(8,128)(2,1)}, f16[192,1152]{1,0:T(8,128)(2,1)S(1)}, u32[]{:S(2)}, u32[]{:S(2)}) collective-permute-start(f16[192,1152]{1,0:T(8,128)(2,1)} %multiply_convert_fusion.3), channel_id=1, source_target_pairs={{0,6},{2,0},{4,2},{6,4},{8,10},{10,12},{12,14},{14,8},{16,22},{18,... | collective-permute-start | bytes 1327112 | tf_op jit(solution)/shard_map/ppermute | solution.py:62
  65.9 5.1 %collective-permute-done.11 = f16[192,1152]{1,0:T(8,128)(2,1)S(1)} collective-permute-done((f16[192,1152]{1,0:T(8,128)(2,1)}, f16[192,1152]{1,0:T(8,128)(2,1)S(1)}, u32[]{:S(2)}, u32[]{:S(2)}) %collective-permute-start.11) | collective-permute-done | bytes 442400 | tf_op jit(solution)/shard_map/ppermute | solution.py:62
  70.9 2.0 %collective-permute-done.13 = f16[192,1152]{1,0:T(8,128)(2,1)S(1)} collective-permute-done((f16[192,1152]{1,0:T(8,128)(2,1)}, f16[192,1152]{1,0:T(8,128)(2,1)S(1)}, u32[]{:S(2)}, u32[]{:S(2)}) %collective-permute-start.13) | collective-permute-done | bytes 442400 | tf_op jit(solution)/shard_map/ppermute | solution.py:62
  72.9 1.2 %add_multiply_fusion.1 = f32[192,1152]{1,0:T(8,128)} fusion(f16[192,1152]{1,0:T(8,128)(2,1)S(1)} %collective-permute-done.13, f16[192,1152]{1,0:T(8,128)(2,1)S(1)} %collective-permute-done.12, f32[192,1152]{1,0:T(8,128)S(1)} %get-tuple-element.63, f16[192,1152]{1,0:T(8,128)(2,1)S(1)} %collective-permute-done.11, f32[]{:T(128)} %bitcast.2), kind=kLoop, calls=%fused_computation.14 | loop fusion | flops 2211840 | bytes 3096580 | tf_op jit(solution)/shard_map/mul | solution.py:275
  75.4 1.1 %add_multiply_fusion = f32[192,1152]{1,0:T(8,128)} fusion(f16[192,1152]{1,0:T(8,128)(2,1)S(1)} %collective-permute-done.15, f32[192,1152]{1,0:T(8,128)S(1)} %get-tuple-element.67, f16[192,1152]{1,0:T(8,128)(2,1)S(1)} %collective-permute-done.14, f32[]{:T(128)} %bitcast.3), kind=kLoop, calls=%fused_computation.13 | loop fusion | flops 1548288 | bytes 2654212 | tf_op jit(solution)/shard_map/mul | solution.py:277
  76.5 1.4 %shard_map.72 = f32[1]{0:T(128)} custom-call(f32[64,1,128]{2,1,0:T(1,128)} %all-to-all-done.parts), custom_call_target="tpu_custom_call" | custom-call | tf_op jit(solution)/shard_map/pallas_call | solution.py:280
  (30 shorter events, 5.5 us)
Async XLA Ops:
  0.6 9.1 %copy-start = (f32[192,1152]{1,0:T(8,128)S(1)}, f32[192,1152]{1,0:T(8,128)}, u32[]{:S(2)}) copy-start(f32[192,1152]{1,0:T(8,128)} %param.4) | copy-start | bytes 2654212
  1.9 1.9 %collective-permute-start = (bf16[192,1152]{1,0:T(8,128)(2,1)S(1)}, bf16[192,1152]{1,0:T(8,128)(2,1)S(1)}, u32[]{:S(2)}, u32[]{:S(2)}) collective-permute-start(bf16[192,1152]{1,0:T(8,128)(2,1)S(1)} %convert_element_type.48.ta), channel_id=1, source_target_pairs={{0,8},{2,10},{4,12},{6,14},{8,0},{10,2},{12,4},{14,6},{16,24},{18,... | collective-permute-start | bytes 1327112 | tf_op jit(solution)/shard_map/ppermute | solution.py:62
  4.1 28.5 %collective-permute-start.1 = (bf16[384,1152]{1,0:T(8,128)(2,1)S(1)}, bf16[384,1152]{1,0:T(8,128)(2,1)S(1)}, u32[]{:S(2)}, u32[]{:S(2)}) collective-permute-start(bf16[384,1152]{1,0:T(8,128)(2,1)S(1)} %maximum_select_fusion), channel_id=1, source_target_pairs={{0,16},{2,18},{4,20},{6,22},{8,25},{10,27},{12,29},{14,31},{16,32}... | collective-permute-start | bytes 2654216 | tf_op jit(solution)/shard_map/ppermute | solution.py:62
  6.1 26.4 %collective-permute-start.2 = (bf16[192,1152]{1,0:T(8,128)(2,1)S(1)}, bf16[192,1152]{1,0:T(8,128)(2,1)S(1)}, u32[]{:S(2)}, u32[]{:S(2)}) collective-permute-start(bf16[192,1152]{1,0:T(8,128)(2,1)S(1)} %convert_element_type.48.ta), channel_id=1, source_target_pairs={{0,1},{2,3},{4,5},{6,7},{8,9},{10,11},{12,13},{14,15},{16,17},{18,... | collective-permute-start | bytes 1327112 | tf_op jit(solution)/shard_map/ppermute | solution.py:62
  9.8 22.8 %collective-permute-start.5 = (bf16[192,1152]{1,0:T(8,128)(2,1)S(1)}, bf16[192,1152]{1,0:T(8,128)(2,1)S(1)}, u32[]{:S(2)}, u32[]{:S(2)}) collective-permute-start(bf16[192,1152]{1,0:T(8,128)(2,1)S(1)} %convert_element_type.49.i0), channel_id=1, source_target_pairs={{0,4},{2,6},{4,0},{6,2},{8,12},{10,14},{12,8},{14,10},{16,20},{18,... | collective-permute-start | bytes 1327112 | tf_op jit(solution)/shard_map/ppermute | solution.py:62
  12.9 19.7 %collective-permute-start.4 = (bf16[192,1152]{1,0:T(8,128)(2,1)S(1)}, bf16[192,1152]{1,0:T(8,128)(2,1)S(1)}, u32[]{:S(2)}, u32[]{:S(2)}) collective-permute-start(bf16[192,1152]{1,0:T(8,128)(2,1)S(1)} %convert_element_type.49.i0), channel_id=1, source_target_pairs={{0,6},{2,0},{4,2},{6,4},{8,10},{10,12},{12,14},{14,8},{16,22},{18,... | collective-permute-start | bytes 1327112 | tf_op jit(solution)/shard_map/ppermute | solution.py:62
  14.0 18.5 %collective-permute-start.3 = (bf16[192,1152]{1,0:T(8,128)(2,1)S(1)}, bf16[192,1152]{1,0:T(8,128)(2,1)S(1)}, u32[]{:S(2)}, u32[]{:S(2)}) collective-permute-start(bf16[192,1152]{1,0:T(8,128)(2,1)S(1)} %convert_element_type.49.i0), channel_id=1, source_target_pairs={{0,2},{2,4},{4,6},{6,0},{8,14},{10,8},{12,10},{14,12},{16,18},{18,... | collective-permute-start | bytes 1327112 | tf_op jit(solution)/shard_map/ppermute | solution.py:62
  32.6 3.1 %collective-permute-start.7 = (bf16[384,1152]{1,0:T(8,128)(2,1)S(1)}, bf16[384,1152]{1,0:T(8,128)(2,1)S(1)}, u32[]{:S(2)}, u32[]{:S(2)}) collective-permute-start(bf16[384,1152]{1,0:T(8,128)(2,1)S(1)} %collective-permute-done.1.far), channel_id=1, source_target_pairs={{0,8},{2,10},{4,12},{6,14},{8,0},{10,2},{12,4},{14,6},{16,24},{18,... | collective-permute-start | bytes 2654216 | tf_op jit(solution)/shard_map/ppermute | solution.py:62
  32.7 3.0 %collective-permute-start.6 = (bf16[192,1152]{1,0:T(8,128)(2,1)S(1)}, bf16[192,1152]{1,0:T(8,128)(2,1)S(1)}, u32[]{:S(2)}, u32[]{:S(2)}) collective-permute-start(bf16[192,1152]{1,0:T(8,128)(2,1)S(1)} %collective-permute-done.2.tb), channel_id=1, source_target_pairs={{0,8},{2,10},{4,12},{6,14},{8,0},{10,2},{12,4},{14,6},{16,24},{18,... | collective-permute-start | bytes 1327112 | tf_op jit(solution)/shard_map/ppermute | solution.py:62
  41.0 3.9 %collective-permute-start.8 = (f16[384,1152]{1,0:T(8,128)(2,1)S(1)}, f16[384,1152]{1,0:T(8,128)(2,1)S(1)}, u32[]{:S(2)}, u32[]{:S(2)}) collective-permute-start(f16[384,1152]{1,0:T(8,128)(2,1)S(1)} %multiply_convert_fusion), channel_id=1, source_target_pairs={{0,8},{2,10},{4,12},{6,14},{8,0},{10,2},{12,4},{14,6},{16,24},{18,... | collective-permute-start | bytes 2654216 | tf_op jit(solution)/shard_map/ppermute | solution.py:62
  41.2 13.7 %collective-permute-start.10 = (f32[8,128]{1,0:T(8,128)S(1)}, f32[8,128]{1,0:T(8,128)S(1)}, u32[]{:S(2)}, u32[]{:S(2)}) collective-permute-start(f32[8,128]{1,0:T(8,128)S(1)} %get-tuple-element.60.mine), channel_id=1, source_target_pairs={{0,8},{2,10},{4,12},{6,14},{8,0},{10,2},{12,4},{14,6},{16,24},{18,... | collective-permute-start | bytes 12296 | tf_op jit(solution)/shard_map/ppermute | solution.py:62
  41.7 12.2 %collective-permute-start.9 = (f16[192,1152]{1,0:T(8,128)(2,1)S(1)}, f16[192,1152]{1,0:T(8,128)(2,1)S(1)}, u32[]{:S(2)}, u32[]{:S(2)}) collective-permute-start(f16[192,1152]{1,0:T(8,128)(2,1)S(1)} %multiply_convert_fusion.2), channel_id=1, source_target_pairs={{0,2},{2,4},{4,6},{6,0},{8,14},{10,8},{12,10},{14,12},{16,18},{18,... | collective-permute-start | bytes 1327112 | tf_op jit(solution)/shard_map/ppermute | solution.py:62
  46.5 24.4 %collective-permute-start.11 = (f16[192,1152]{1,0:T(8,128)(2,1)}, f16[192,1152]{1,0:T(8,128)(2,1)S(1)}, u32[]{:S(2)}, u32[]{:S(2)}) collective-permute-start(f16[192,1152]{1,0:T(8,128)(2,1)} %get-tuple-element.64), channel_id=1, source_target_pairs={{0,1},{2,3},{4,5},{6,7},{8,9},{10,11},{12,13},{14,15},{16,17},{18,... | collective-permute-start | bytes 1327112 | tf_op jit(solution)/shard_map/ppermute | solution.py:62
  47.7 23.2 %collective-permute-start.12 = (f16[192,1152]{1,0:T(8,128)(2,1)}, f16[192,1152]{1,0:T(8,128)(2,1)S(1)}, u32[]{:S(2)}, u32[]{:S(2)}) collective-permute-start(f16[192,1152]{1,0:T(8,128)(2,1)} %get-tuple-element.65), channel_id=1, source_target_pairs={{0,112},{2,114},{4,116},{6,118},{8,120},{10,122},{12,124},{14,126}... | collective-permute-start | bytes 1327112 | tf_op jit(solution)/shard_map/ppermute | solution.py:62
  50.2 22.7 %collective-permute-start.13 = (f16[192,1152]{1,0:T(8,128)(2,1)}, f16[192,1152]{1,0:T(8,128)(2,1)S(1)}, u32[]{:S(2)}, u32[]{:S(2)}) collective-permute-start(f16[192,1152]{1,0:T(8,128)(2,1)} %get-tuple-element.66), channel_id=1, source_target_pairs={{0,113},{2,115},{4,117},{6,119},{8,121},{10,123},{12,125},{14,127}... | collective-permute-start | bytes 1327112 | tf_op jit(solution)/shard_map/ppermute | solution.py:62
  55.7 20.8 %all-to-all-start = ((f32[64,1,128]{2,1,0:T(1,128)}), f32[64,1,128]{2,1,0:T(1,128)}, u32[]{:S(2)}, u32[]{:S(2)}) async-start(f32[64,1,128]{2,1,0:T(1,128)} %shard_map.71), calls=%async_computation | async-start | bytes 65536 | tf_op jit(solution)/shard_map/all_to_all | solution.py:274
  63.1 11.4 %collective-permute-start.14 = (f16[192,1152]{1,0:T(8,128)(2,1)}, f16[192,1152]{1,0:T(8,128)(2,1)S(1)}, u32[]{:S(2)}, u32[]{:S(2)}) collective-permute-start(f16[192,1152]{1,0:T(8,128)(2,1)} %multiply_convert_fusion.3), channel_id=1, source_target_pairs={{0,6},{2,0},{4,2},{6,4},{8,10},{10,12},{12,14},{14,8},{16,22},{18,... | collective-permute-start | bytes 1327112 | tf_op jit(solution)/shard_map/ppermute | solution.py:62
  65.9 9.5 %collective-permute-start.15 = (f16[192,1152]{1,0:T(8,128)(2,1)S(1)}, f16[192,1152]{1,0:T(8,128)(2,1)S(1)}, u32[]{:S(2)}, u32[]{:S(2)}) collective-permute-start(f16[192,1152]{1,0:T(8,128)(2,1)S(1)} %multiply_convert_fusion.1), channel_id=1, source_target_pairs={{0,2},{2,4},{4,6},{6,0},{8,14},{10,8},{12,10},{14,12},{16,18},{18,... | collective-permute-start | bytes 1327112 | tf_op jit(solution)/shard_map/ppermute | solution.py:62

commit v6 on v5

--- a/solution.py
+++ b/solution.py
@@ -18,7 +18,7 @@
 LAST = (((1,), (1,)), ((), ()))
 FIRST = (((0,), (0,)), ((), ()))
 PLAIN = (((1,), (0,)), ((), ()))
-VMEM_BYTES = 16 * 1024 * 1024
+VMEM_BYTES = 12 * 1024 * 1024
 
 
 def place(y, z, core, x):
@@ -164,17 +164,13 @@
     sum_2[...] = dot(weights[pl.ds(2 * n, 2 * n), :], images[...], PLAIN)
 
 
-def image_body(w0, weights, t0, text, *outs):
+def image_body(w0, weights, t0, text, loss, loss_o, spread, *outs):
+    spread[...] = jnp.full(spread.shape, jnp.sum(loss[...] + loss_o[...]), jnp.float32)
     n = outs[0].shape[0]
     cut = pl.ds(0, len(outs) * n)
     out = dot(w0[:, cut], t0[...], FIRST) + dot(weights[:, cut], text[...], FIRST)
     for k, ref in enumerate(outs):
         ref[...] = out[k * n : (k + 1) * n]
-
-
-def spread_body(mine, other, out):
-    total = jnp.sum(mine[...] + other[...])
-    out[...] = jnp.full(out.shape, total, jnp.float32)
 
 
 def mean_body(pairs, parts, out):
@@ -258,13 +254,15 @@
     )
     sum_a, w0 = out[3:]
     out = out[:3]
-    own, left, right = call(
-        image_body, [((n, width), f32)] * 3, (w0, weights, t0, text), 9 * unit // 2, scalars=0
+    loss, own, left, right = call(
+        image_body,
+        [((CHIP_COUNT, 1, 128), f32)] + [((n, width), f32)] * 3,
+        (w0, weights, t0, text, loss, loss_o),
+        9 * unit // 2,
+        scalars=0,
     )
     right = right + passed
-    out = out + lax.optimization_barrier((narrow(left), narrow(right), loss, loss_o))
-    (loss,) = call(spread_body, [((CHIP_COUNT, 1, 128), f32)], out[5:], 4, scalars=0)
-    out = out[:5] + (loss,)
+    out = out + lax.optimization_barrier((narrow(left), narrow(right), loss))
     back_z = send(out[0], along_z(2))
     back_a = send(out[1], next_column(-1, lambda core: 0))
     back_b = send(out[2], next_column(-1, lambda core: 1))

time: 78.3 us -> 78.2 us (level)
    pallas_call x5 -> x4, Pallas kernels: 12 us -> 11.8 us  [call(): pl.pallas_call(body, out_shape=tuple((jax.ShapeDtypeStruct(s, t) for s, t...]
where the time goes in v6:
time: 78.2 us; the launch traced here: 77.9 us
  starting transfers between devices  29.1 us (37%)
  waiting for transfers between devices  26.6 us (34%)
  Pallas kernels  13.3 us (17%)
  other arithmetic  6.78 us (9%)
  between operations  2.21 us (3%)
    ppermute x16, waiting for transfers between devices, send(): return lax.ppermute(value, AXES, pairs)  26.6 us
    ppermute x16, starting transfers between devices, send(): return lax.ppermute(value, AXES, pairs)  21.7 us
    pallas_call x4, Pallas kernels, call(): pl.pallas_call(body, out_shape=tuple((jax.ShapeDtypeStruct(s, t) for s, t...  11.8 us
    all_to_all x1, starting transfers between devices, local(): losses = lax.all_to_all(out[5], CHIPS, 0, 0, tiled=True)  7.4 us
  transfers between devices with their start and end apart: 17, of which 7 were waited for; matrix products, arithmetic and copies ran while one was open for 7% of the time, Pallas kernels for 9%

profile of v6, /device:TPU:0, one launch (start us, length us, event | category | flops | bytes accessed | tf_op | source)
XLA Modules:
  0.0 77.9 jit_solution(17673481184850553030)
XLA Ops:
  0.6 1.3 %convert_element_type.48.ta = bf16[192,1152]{1,0:T(8,128)(2,1)S(1)} convert(f32[192,1152]{1,0:T(8,128)} %param.5) | non-fusion elementwise | flops 221184 | bytes 1327104 | tf_op jit(solution)/shard_map/convert_element_type | solution.py:197
  2.0 1.8 %collective-permute-done.own_o = bf16[192,1152]{1,0:T(8,128)(2,1)S(1)} collective-permute-done((bf16[192,1152]{1,0:T(8,128)(2,1)S(1)}, bf16[192,1152]{1,0:T(8,128)(2,1)S(1)}, u32[]{:S(2)}, u32[]{:S(2)}) %collective-permute-start) | collective-permute-done | bytes 442400 | tf_op jit(solution)/shard_map/ppermute | solution.py:62
  4.1 2.1 %collective-permute-start.1 = (bf16[384,1152]{1,0:T(8,128)(2,1)S(1)}, bf16[384,1152]{1,0:T(8,128)(2,1)S(1)}, u32[]{:S(2)}, u32[]{:S(2)}) collective-permute-start(bf16[384,1152]{1,0:T(8,128)(2,1)S(1)} %maximum_select_fusion), channel_id=1, source_target_pairs={{0,16},{2,18},{4,20},{6,22},{8,25},{10,27},{12,29},{14,31},{16,32}... | collective-permute-start | bytes 2654216 | tf_op jit(solution)/shard_map/ppermute | solution.py:62
  6.1 3.6 %collective-permute-start.2 = (bf16[192,1152]{1,0:T(8,128)(2,1)S(1)}, bf16[192,1152]{1,0:T(8,128)(2,1)S(1)}, u32[]{:S(2)}, u32[]{:S(2)}) collective-permute-start(bf16[192,1152]{1,0:T(8,128)(2,1)S(1)} %convert_element_type.48.ta), channel_id=1, source_target_pairs={{0,1},{2,3},{4,5},{6,7},{8,9},{10,11},{12,13},{14,15},{16,17},{18,... | collective-permute-start | bytes 1327112 | tf_op jit(solution)/shard_map/ppermute | solution.py:62
  9.8 3.1 %collective-permute-start.5 = (bf16[192,1152]{1,0:T(8,128)(2,1)S(1)}, bf16[192,1152]{1,0:T(8,128)(2,1)S(1)}, u32[]{:S(2)}, u32[]{:S(2)}) collective-permute-start(bf16[192,1152]{1,0:T(8,128)(2,1)S(1)} %convert_element_type.49.i0), channel_id=1, source_target_pairs={{0,4},{2,6},{4,0},{6,2},{8,12},{10,14},{12,8},{14,10},{16,20},{18,... | collective-permute-start | bytes 1327112 | tf_op jit(solution)/shard_map/ppermute | solution.py:62
  12.9 1.1 %collective-permute-start.4 = (bf16[192,1152]{1,0:T(8,128)(2,1)S(1)}, bf16[192,1152]{1,0:T(8,128)(2,1)S(1)}, u32[]{:S(2)}, u32[]{:S(2)}) collective-permute-start(bf16[192,1152]{1,0:T(8,128)(2,1)S(1)} %convert_element_type.49.i0), channel_id=1, source_target_pairs={{0,6},{2,0},{4,2},{6,4},{8,10},{10,12},{12,14},{14,8},{16,22},{18,... | collective-permute-start | bytes 1327112 | tf_op jit(solution)/shard_map/ppermute | solution.py:62
  14.0 0.9 %collective-permute-start.3 = (bf16[192,1152]{1,0:T(8,128)(2,1)S(1)}, bf16[192,1152]{1,0:T(8,128)(2,1)S(1)}, u32[]{:S(2)}, u32[]{:S(2)}) collective-permute-start(bf16[192,1152]{1,0:T(8,128)(2,1)S(1)} %convert_element_type.49.i0), channel_id=1, source_target_pairs={{0,2},{2,4},{4,6},{6,0},{8,14},{10,8},{12,10},{14,12},{16,18},{18,... | collective-permute-start | bytes 1327112 | tf_op jit(solution)/shard_map/ppermute | solution.py:62
  16.3 16.2 %collective-permute-done.2.tb = bf16[192,1152]{1,0:T(8,128)(2,1)S(1)} collective-permute-done((bf16[192,1152]{1,0:T(8,128)(2,1)S(1)}, bf16[192,1152]{1,0:T(8,128)(2,1)S(1)}, u32[]{:S(2)}, u32[]{:S(2)}) %collective-permute-start.2) | collective-permute-done | bytes 442400 | tf_op jit(solution)/shard_map/ppermute | solution.py:62
  33.1 2.3 %shard_map.67 = (bf16[768,1152]{1,0:T(8,128)(2,1)S(1)}, bf16[384,1152]{1,0:T(8,128)(2,1)S(1)}, bf16[384,768]{1,0:T(8,128)(2,1)S(1)}, f32[8,128]{1,0:T(8,128)S(1)}) custom-call(f32[2]{0:T(128)S(1)} %pad_maximum_fusion.scalars, bf16[192,1152]{1,0:T(8,128)(2,1)S(1)} %convert_element_type.49.i0, bf16[192,1152]{1,0:T(8,128)(2,1)S(1)} %collective-permute-done.3.i1, ...), custom_call_target="tpu_custom_call" | custom-call | flops 679477248 | bytes 1048576 | tf_op jit(solution)/shard_map/pallas_call | solution.py:74
  35.7 5.2 %shard_map.68 = (bf16[768,1152]{1,0:T(8,128)(2,1)S(1)}, bf16[768,768]{1,0:T(8,128)(2,1)S(1)}, f32[192,1152]{1,0:T(8,128)S(1)}, f32[384,1152]{1,0:T(8,128)S(1)}, f32[8,128]{1,0:T(8,128)S(1)}) custom-call(f32[2]{0:T(128)S(1)} %pad_maximum_fusion.scalars, s32[1]{0:T(128)} %bitcast.core, bf16[768,1152]{1,0:T(8,128)(2,1)S(1)} %get-tuple-element.43.images, ...), custom_call_target="tpu_custom_call" | custom-call | flops 2717908992 | bytes 1048576 | tf_op jit(solution)/shard_map/pallas_call | solution.py:74
  41.7 1.6 %collective-permute-start.10 = (f16[192,1152]{1,0:T(8,128)(2,1)S(1)}, f16[192,1152]{1,0:T(8,128)(2,1)S(1)}, u32[]{:S(2)}, u32[]{:S(2)}) collective-permute-start(f16[192,1152]{1,0:T(8,128)(2,1)S(1)} %multiply_convert_fusion.2), channel_id=1, source_target_pairs={{0,2},{2,4},{4,6},{6,0},{8,14},{10,8},{12,10},{14,12},{16,18},{18,... | collective-permute-start | bytes 1327112 | tf_op jit(solution)/shard_map/ppermute | solution.py:62
  43.3 1.7 %shard_map.69 = (f32[192,1152]{1,0:T(8,128)S(1)}, f32[192,1152]{1,0:T(8,128)S(1)}, f32[384,1152]{1,0:T(8,128)S(1)}) custom-call(bf16[768,1152]{1,0:T(8,128)(2,1)S(1)} %get-tuple-element.43.images, bf16[384,768]{1,0:T(8,128)(2,1)S(1)} %get-tuple-element.54.w0, bf16[768,768]{1,0:T(8,128)(2,1)S(1)} %get-tuple-element.49.weights), custom_call_target="tpu_custom_call" | custom-call | flops 1358954496 | bytes 1048576 | tf_op jit(solution)/shard_map/pallas_call | solution.py:74
  45.3 1.2 %slice_add_fusion = (f32[192,1152]{1,0:T(8,128)S(1)}, f16[192,1152]{1,0:T(8,128)(2,1)}, f16[192,1152]{1,0:T(8,128)(2,1)}, f16[192,1152]{1,0:T(8,128)(2,1)}) fusion(f32[192,1152]{1,0:T(8,128)S(1)} %get-tuple-element.53, f32[384,1152]{1,0:T(8,128)S(1)} %get-tuple-element.78, f32[192,1152]{1,0:T(8,128)S(1)} %get-tuple-element.50, ...), kind=kLoop, calls=%fused_computation.4 | loop fusion | flops 1769472 | bytes 7520256 | tf_op jit(solution)/shard_map/add | solution.py:253
  46.5 1.2 %collective-permute-start.11 = (f16[192,1152]{1,0:T(8,128)(2,1)}, f16[192,1152]{1,0:T(8,128)(2,1)S(1)}, u32[]{:S(2)}, u32[]{:S(2)}) collective-permute-start(f16[192,1152]{1,0:T(8,128)(2,1)} %get-tuple-element.64), channel_id=1, source_target_pairs={{0,1},{2,3},{4,5},{6,7},{8,9},{10,11},{12,13},{14,15},{16,17},{18,... | collective-permute-start | bytes 1327112 | tf_op jit(solution)/shard_map/ppermute | solution.py:62
  47.8 2.5 %collective-permute-start.12 = (f16[192,1152]{1,0:T(8,128)(2,1)}, f16[192,1152]{1,0:T(8,128)(2,1)S(1)}, u32[]{:S(2)}, u32[]{:S(2)}) collective-permute-start(f16[192,1152]{1,0:T(8,128)(2,1)} %get-tuple-element.65), channel_id=1, source_target_pairs={{0,112},{2,114},{4,116},{6,118},{8,120},{10,122},{12,124},{14,126}... | collective-permute-start | bytes 1327112 | tf_op jit(solution)/shard_map/ppermute | solution.py:62
  50.3 1.5 %collective-permute-start.13 = (f16[192,1152]{1,0:T(8,128)(2,1)}, f16[192,1152]{1,0:T(8,128)(2,1)S(1)}, u32[]{:S(2)}, u32[]{:S(2)}) collective-permute-start(f16[192,1152]{1,0:T(8,128)(2,1)} %get-tuple-element.66), channel_id=1, source_target_pairs={{0,113},{2,115},{4,117},{6,119},{8,121},{10,123},{12,125},{14,127}... | collective-permute-start | bytes 1327112 | tf_op jit(solution)/shard_map/ppermute | solution.py:62
  51.8 2.7 %shard_map.70 = (f32[64,1,128]{2,1,0:T(1,128)}, f32[192,1152]{1,0:T(8,128)S(1)}, f32[192,1152]{1,0:T(8,128)S(1)}, f32[192,1152]{1,0:T(8,128)S(1)}) custom-call(bf16[384,768]{1,0:T(8,128)(2,1)S(1)} %get-tuple-element.54.w0, bf16[768,768]{1,0:T(8,128)(2,1)S(1)} %get-tuple-element.49.weights, bf16[384,1152]{1,0:T(8,128)(2,1)S(1)} %get-tuple-element.46.t0, ...), custom_call_target="tpu_custom_call" | custom-call | flops 1528823808 | bytes 1048576 | tf_op jit(solution)/shard_map/pallas_call | solution.py:74
  55.5 7.4 %all-to-all-start = ((f32[64,1,128]{2,1,0:T(1,128)}), f32[64,1,128]{2,1,0:T(1,128)}, u32[]{:S(2)}, u32[]{:S(2)}) async-start(f32[64,1,128]{2,1,0:T(1,128)} %get-tuple-element.61), calls=%async_computation | async-start | bytes 65536 | tf_op jit(solution)/shard_map/all_to_all | solution.py:272
  62.9 2.8 %collective-permute-start.14 = (f16[192,1152]{1,0:T(8,128)(2,1)}, f16[192,1152]{1,0:T(8,128)(2,1)S(1)}, u32[]{:S(2)}, u32[]{:S(2)}) collective-permute-start(f16[192,1152]{1,0:T(8,128)(2,1)} %multiply_convert_fusion.3), channel_id=1, source_target_pairs={{0,6},{2,0},{4,2},{6,4},{8,10},{10,12},{12,14},{14,8},{16,22},{18,... | collective-permute-start | bytes 1327112 | tf_op jit(solution)/shard_map/ppermute | solution.py:62
  65.7 5.3 %collective-permute-done.11 = f16[192,1152]{1,0:T(8,128)(2,1)S(1)} collective-permute-done((f16[192,1152]{1,0:T(8,128)(2,1)}, f16[192,1152]{1,0:T(8,128)(2,1)S(1)}, u32[]{:S(2)}, u32[]{:S(2)}) %collective-permute-start.11) | collective-permute-done | bytes 442400 | tf_op jit(solution)/shard_map/ppermute | solution.py:62
  71.0 2.0 %collective-permute-done.13 = f16[192,1152]{1,0:T(8,128)(2,1)S(1)} collective-permute-done((f16[192,1152]{1,0:T(8,128)(2,1)}, f16[192,1152]{1,0:T(8,128)(2,1)S(1)}, u32[]{:S(2)}, u32[]{:S(2)}) %collective-permute-start.13) | collective-permute-done | bytes 442400 | tf_op jit(solution)/shard_map/ppermute | solution.py:62
  73.0 1.2 %add_multiply_fusion.1 = f32[192,1152]{1,0:T(8,128)} fusion(f16[192,1152]{1,0:T(8,128)(2,1)S(1)} %collective-permute-done.13, f16[192,1152]{1,0:T(8,128)(2,1)S(1)} %collective-permute-done.12, f32[192,1152]{1,0:T(8,128)S(1)} %get-tuple-element.63, f16[192,1152]{1,0:T(8,128)(2,1)S(1)} %collective-permute-done.11, f32[]{:T(128)} %bitcast.2), kind=kLoop, calls=%fused_computation.14 | loop fusion | flops 2211840 | bytes 3096580 | tf_op jit(solution)/shard_map/mul | solution.py:273
  75.2 1.1 %add_multiply_fusion = f32[192,1152]{1,0:T(8,128)} fusion(f16[192,1152]{1,0:T(8,128)(2,1)S(1)} %collective-permute-done.15, f32[192,1152]{1,0:T(8,128)S(1)} %get-tuple-element.67, f16[192,1152]{1,0:T(8,128)(2,1)S(1)} %collective-permute-done.14, f32[]{:T(128)} %bitcast.3), kind=kLoop, calls=%fused_computation.13 | loop fusion | flops 1548288 | bytes 2654212 | tf_op jit(solution)/shard_map/mul | solution.py:275
  76.3 1.4 %shard_map.71 = f32[1]{0:T(128)} custom-call(f32[64,1,128]{2,1,0:T(1,128)} %all-to-all-done.parts), custom_call_target="tpu_custom_call" | custom-call | tf_op jit(solution)/shard_map/pallas_call | solution.py:278
  (29 shorter events, 4.5 us)
Async XLA Ops:
  0.6 9.1 %copy-start = (f32[192,1152]{1,0:T(8,128)S(1)}, f32[192,1152]{1,0:T(8,128)}, u32[]{:S(2)}) copy-start(f32[192,1152]{1,0:T(8,128)} %param.4) | copy-start | bytes 2654212
  1.9 1.9 %collective-permute-start = (bf16[192,1152]{1,0:T(8,128)(2,1)S(1)}, bf16[192,1152]{1,0:T(8,128)(2,1)S(1)}, u32[]{:S(2)}, u32[]{:S(2)}) collective-permute-start(bf16[192,1152]{1,0:T(8,128)(2,1)S(1)} %convert_element_type.48.ta), channel_id=1, source_target_pairs={{0,8},{2,10},{4,12},{6,14},{8,0},{10,2},{12,4},{14,6},{16,24},{18,... | collective-permute-start | bytes 1327112 | tf_op jit(solution)/shard_map/ppermute | solution.py:62
  4.1 28.5 %collective-permute-start.1 = (bf16[384,1152]{1,0:T(8,128)(2,1)S(1)}, bf16[384,1152]{1,0:T(8,128)(2,1)S(1)}, u32[]{:S(2)}, u32[]{:S(2)}) collective-permute-start(bf16[384,1152]{1,0:T(8,128)(2,1)S(1)} %maximum_select_fusion), channel_id=1, source_target_pairs={{0,16},{2,18},{4,20},{6,22},{8,25},{10,27},{12,29},{14,31},{16,32}... | collective-permute-start | bytes 2654216 | tf_op jit(solution)/shard_map/ppermute | solution.py:62
  6.1 26.4 %collective-permute-start.2 = (bf16[192,1152]{1,0:T(8,128)(2,1)S(1)}, bf16[192,1152]{1,0:T(8,128)(2,1)S(1)}, u32[]{:S(2)}, u32[]{:S(2)}) collective-permute-start(bf16[192,1152]{1,0:T(8,128)(2,1)S(1)} %convert_element_type.48.ta), channel_id=1, source_target_pairs={{0,1},{2,3},{4,5},{6,7},{8,9},{10,11},{12,13},{14,15},{16,17},{18,... | collective-permute-start | bytes 1327112 | tf_op jit(solution)/shard_map/ppermute | solution.py:62
  9.8 22.8 %collective-permute-start.5 = (bf16[192,1152]{1,0:T(8,128)(2,1)S(1)}, bf16[192,1152]{1,0:T(8,128)(2,1)S(1)}, u32[]{:S(2)}, u32[]{:S(2)}) collective-permute-start(bf16[192,1152]{1,0:T(8,128)(2,1)S(1)} %convert_element_type.49.i0), channel_id=1, source_target_pairs={{0,4},{2,6},{4,0},{6,2},{8,12},{10,14},{12,8},{14,10},{16,20},{18,... | collective-permute-start | bytes 1327112 | tf_op jit(solution)/shard_map/ppermute | solution.py:62
  12.9 19.7 %collective-permute-start.4 = (bf16[192,1152]{1,0:T(8,128)(2,1)S(1)}, bf16[192,1152]{1,0:T(8,128)(2,1)S(1)}, u32[]{:S(2)}, u32[]{:S(2)}) collective-permute-start(bf16[192,1152]{1,0:T(8,128)(2,1)S(1)} %convert_element_type.49.i0), channel_id=1, source_target_pairs={{0,6},{2,0},{4,2},{6,4},{8,10},{10,12},{12,14},{14,8},{16,22},{18,... | collective-permute-start | bytes 1327112 | tf_op jit(solution)/shard_map/ppermute | solution.py:62
  14.0 18.5 %collective-permute-start.3 = (bf16[192,1152]{1,0:T(8,128)(2,1)S(1)}, bf16[192,1152]{1,0:T(8,128)(2,1)S(1)}, u32[]{:S(2)}, u32[]{:S(2)}) collective-permute-start(bf16[192,1152]{1,0:T(8,128)(2,1)S(1)} %convert_element_type.49.i0), channel_id=1, source_target_pairs={{0,2},{2,4},{4,6},{6,0},{8,14},{10,8},{12,10},{14,12},{16,18},{18,... | collective-permute-start | bytes 1327112 | tf_op jit(solution)/shard_map/ppermute | solution.py:62
  32.6 3.1 %collective-permute-start.7 = (bf16[384,1152]{1,0:T(8,128)(2,1)S(1)}, bf16[384,1152]{1,0:T(8,128)(2,1)S(1)}, u32[]{:S(2)}, u32[]{:S(2)}) collective-permute-start(bf16[384,1152]{1,0:T(8,128)(2,1)S(1)} %collective-permute-done.1.far), channel_id=1, source_target_pairs={{0,8},{2,10},{4,12},{6,14},{8,0},{10,2},{12,4},{14,6},{16,24},{18,... | collective-permute-start | bytes 2654216 | tf_op jit(solution)/shard_map/ppermute | solution.py:62
  32.7 3.0 %collective-permute-start.6 = (bf16[192,1152]{1,0:T(8,128)(2,1)S(1)}, bf16[192,1152]{1,0:T(8,128)(2,1)S(1)}, u32[]{:S(2)}, u32[]{:S(2)}) collective-permute-start(bf16[192,1152]{1,0:T(8,128)(2,1)S(1)} %collective-permute-done.2.tb), channel_id=1, source_target_pairs={{0,8},{2,10},{4,12},{6,14},{8,0},{10,2},{12,4},{14,6},{16,24},{18,... | collective-permute-start | bytes 1327112 | tf_op jit(solution)/shard_map/ppermute | solution.py:62
  41.0 3.9 %collective-permute-start.8 = (f16[384,1152]{1,0:T(8,128)(2,1)S(1)}, f16[384,1152]{1,0:T(8,128)(2,1)S(1)}, u32[]{:S(2)}, u32[]{:S(2)}) collective-permute-start(f16[384,1152]{1,0:T(8,128)(2,1)S(1)} %multiply_convert_fusion), channel_id=1, source_target_pairs={{0,8},{2,10},{4,12},{6,14},{8,0},{10,2},{12,4},{14,6},{16,24},{18,... | collective-permute-start | bytes 2654216 | tf_op jit(solution)/shard_map/ppermute | solution.py:62
  41.3 10.6 %collective-permute-start.9 = (f32[8,128]{1,0:T(8,128)S(1)}, f32[8,128]{1,0:T(8,128)S(1)}, u32[]{:S(2)}, u32[]{:S(2)}) collective-permute-start(f32[8,128]{1,0:T(8,128)S(1)} %get-tuple-element.56.loss), channel_id=1, source_target_pairs={{0,8},{2,10},{4,12},{6,14},{8,0},{10,2},{12,4},{14,6},{16,24},{18,... | collective-permute-start | bytes 12296 | tf_op jit(solution)/shard_map/ppermute | solution.py:62
  41.7 12.8 %collective-permute-start.10 = (f16[192,1152]{1,0:T(8,128)(2,1)S(1)}, f16[192,1152]{1,0:T(8,128)(2,1)S(1)}, u32[]{:S(2)}, u32[]{:S(2)}) collective-permute-start(f16[192,1152]{1,0:T(8,128)(2,1)S(1)} %multiply_convert_fusion.2), channel_id=1, source_target_pairs={{0,2},{2,4},{4,6},{6,0},{8,14},{10,8},{12,10},{14,12},{16,18},{18,... | collective-permute-start | bytes 1327112 | tf_op jit(solution)/shard_map/ppermute | solution.py:62
  46.5 24.4 %collective-permute-start.11 = (f16[192,1152]{1,0:T(8,128)(2,1)}, f16[192,1152]{1,0:T(8,128)(2,1)S(1)}, u32[]{:S(2)}, u32[]{:S(2)}) collective-permute-start(f16[192,1152]{1,0:T(8,128)(2,1)} %get-tuple-element.64), channel_id=1, source_target_pairs={{0,1},{2,3},{4,5},{6,7},{8,9},{10,11},{12,13},{14,15},{16,17},{18,... | collective-permute-start | bytes 1327112 | tf_op jit(solution)/shard_map/ppermute | solution.py:62
  47.8 23.2 %collective-permute-start.12 = (f16[192,1152]{1,0:T(8,128)(2,1)}, f16[192,1152]{1,0:T(8,128)(2,1)S(1)}, u32[]{:S(2)}, u32[]{:S(2)}) collective-permute-start(f16[192,1152]{1,0:T(8,128)(2,1)} %get-tuple-element.65), channel_id=1, source_target_pairs={{0,112},{2,114},{4,116},{6,118},{8,120},{10,122},{12,124},{14,126}... | collective-permute-start | bytes 1327112 | tf_op jit(solution)/shard_map/ppermute | solution.py:62
  50.3 22.7 %collective-permute-start.13 = (f16[192,1152]{1,0:T(8,128)(2,1)}, f16[192,1152]{1,0:T(8,128)(2,1)S(1)}, u32[]{:S(2)}, u32[]{:S(2)}) collective-permute-start(f16[192,1152]{1,0:T(8,128)(2,1)} %get-tuple-element.66), channel_id=1, source_target_pairs={{0,113},{2,115},{4,117},{6,119},{8,121},{10,123},{12,125},{14,127}... | collective-permute-start | bytes 1327112 | tf_op jit(solution)/shard_map/ppermute | solution.py:62
  55.5 20.8 %all-to-all-start = ((f32[64,1,128]{2,1,0:T(1,128)}), f32[64,1,128]{2,1,0:T(1,128)}, u32[]{:S(2)}, u32[]{:S(2)}) async-start(f32[64,1,128]{2,1,0:T(1,128)} %get-tuple-element.61), calls=%async_computation | async-start | bytes 65536 | tf_op jit(solution)/shard_map/all_to_all | solution.py:272
  62.9 11.4 %collective-permute-start.14 = (f16[192,1152]{1,0:T(8,128)(2,1)}, f16[192,1152]{1,0:T(8,128)(2,1)S(1)}, u32[]{:S(2)}, u32[]{:S(2)}) collective-permute-start(f16[192,1152]{1,0:T(8,128)(2,1)} %multiply_convert_fusion.3), channel_id=1, source_target_pairs={{0,6},{2,0},{4,2},{6,4},{8,10},{10,12},{12,14},{14,8},{16,22},{18,... | collective-permute-start | bytes 1327112 | tf_op jit(solution)/shard_map/ppermute | solution.py:62
  65.7 9.5 %collective-permute-start.15 = (f16[192,1152]{1,0:T(8,128)(2,1)S(1)}, f16[192,1152]{1,0:T(8,128)(2,1)S(1)}, u32[]{:S(2)}, u32[]{:S(2)}) collective-permute-start(f16[192,1152]{1,0:T(8,128)(2,1)S(1)} %multiply_convert_fusion.1), channel_id=1, source_target_pairs={{0,2},{2,4},{4,6},{6,0},{8,14},{10,8},{12,10},{14,12},{16,18},{18,... | collective-permute-start | bytes 1327112 | tf_op jit(solution)/shard_map/ppermute | solution.py:62

commit v7 on v6

--- a/solution.py
+++ b/solution.py
@@ -218,7 +218,7 @@
         [((4 * n, width), bf16), ((2 * n, width), bf16), ((2 * n, 4 * n), bf16), ((8, 128), f32)],
         (scalars, image_b, image_l, image_r, image_f, text_b, text_z),
         2 * unit,
-        scratch=[pltpu.VMEM((2, 2 * n, 2 * n), f32)],
+        scratch=[pltpu.VMEM((1, 2 * n, 4 * n), f32)],
     )
     text, weights, across, sum_1, loss = call(
         far_body,

time: 78.2 us -> 78.2 us (level)
  transfers between devices with their start and end apart: 17 -> 17, of which waited for: 7 -> 7; matrix products, arithmetic and copies ran while one was open for 7% -> 7% of each run, Pallas kernels for 9% -> 8%
where the time goes in v7:
time: 78.2 us; the launch traced here: 77.9 us
  starting transfers between devices  29.1 us (37%)
  waiting for transfers between devices  26.8 us (34%)
  Pallas kernels  13.1 us (17%)
  other arithmetic  6.78 us (9%)
  between operations  2.21 us (3%)
    ppermute x16, waiting for transfers between devices, send(): return lax.ppermute(value, AXES, pairs)  26.8 us
    ppermute x16, starting transfers between devices, send(): return lax.ppermute(value, AXES, pairs)  21.7 us
    pallas_call x4, Pallas kernels, call(): pl.pallas_call(body, out_shape=tuple((jax.ShapeDtypeStruct(s, t) for s, t...  11.6 us
    all_to_all x1, starting transfers between devices, local(): losses = lax.all_to_all(out[5], CHIPS, 0, 0, tiled=True)  7.4 us
  transfers between devices with their start and end apart: 17, of which 7 were waited for; matrix products, arithmetic and copies ran while one was open for 7% of the time, Pallas kernels for 8%

profile of v7, /device:TPU:0, one launch (start us, length us, event | category | flops | bytes accessed | tf_op | source)
XLA Modules:
  0.0 77.9 jit_solution(1796553020162568612)
XLA Ops:
  0.6 1.3 %convert_element_type.48.ta = bf16[192,1152]{1,0:T(8,128)(2,1)S(1)} convert(f32[192,1152]{1,0:T(8,128)} %param.5) | non-fusion elementwise | flops 221184 | bytes 1327104 | tf_op jit(solution)/shard_map/convert_element_type | solution.py:197
  2.0 1.8 %collective-permute-done.own_o = bf16[192,1152]{1,0:T(8,128)(2,1)S(1)} collective-permute-done((bf16[192,1152]{1,0:T(8,128)(2,1)S(1)}, bf16[192,1152]{1,0:T(8,128)(2,1)S(1)}, u32[]{:S(2)}, u32[]{:S(2)}) %collective-permute-start) | collective-permute-done | bytes 442400 | tf_op jit(solution)/shard_map/ppermute | solution.py:62
  4.1 2.1 %collective-permute-start.1 = (bf16[384,1152]{1,0:T(8,128)(2,1)S(1)}, bf16[384,1152]{1,0:T(8,128)(2,1)S(1)}, u32[]{:S(2)}, u32[]{:S(2)}) collective-permute-start(bf16[384,1152]{1,0:T(8,128)(2,1)S(1)} %maximum_select_fusion), channel_id=1, source_target_pairs={{0,16},{2,18},{4,20},{6,22},{8,25},{10,27},{12,29},{14,31},{16,32}... | collective-permute-start | bytes 2654216 | tf_op jit(solution)/shard_map/ppermute | solution.py:62
  6.1 3.6 %collective-permute-start.2 = (bf16[192,1152]{1,0:T(8,128)(2,1)S(1)}, bf16[192,1152]{1,0:T(8,128)(2,1)S(1)}, u32[]{:S(2)}, u32[]{:S(2)}) collective-permute-start(bf16[192,1152]{1,0:T(8,128)(2,1)S(1)} %convert_element_type.48.ta), channel_id=1, source_target_pairs={{0,1},{2,3},{4,5},{6,7},{8,9},{10,11},{12,13},{14,15},{16,17},{18,... | collective-permute-start | bytes 1327112 | tf_op jit(solution)/shard_map/ppermute | solution.py:62
  9.8 3.1 %collective-permute-start.5 = (bf16[192,1152]{1,0:T(8,128)(2,1)S(1)}, bf16[192,1152]{1,0:T(8,128)(2,1)S(1)}, u32[]{:S(2)}, u32[]{:S(2)}) collective-permute-start(bf16[192,1152]{1,0:T(8,128)(2,1)S(1)} %convert_element_type.49.i0), channel_id=1, source_target_pairs={{0,4},{2,6},{4,0},{6,2},{8,12},{10,14},{12,8},{14,10},{16,20},{18,... | collective-permute-start | bytes 1327112 | tf_op jit(solution)/shard_map/ppermute | solution.py:62
  12.9 1.1 %collective-permute-start.4 = (bf16[192,1152]{1,0:T(8,128)(2,1)S(1)}, bf16[192,1152]{1,0:T(8,128)(2,1)S(1)}, u32[]{:S(2)}, u32[]{:S(2)}) collective-permute-start(bf16[192,1152]{1,0:T(8,128)(2,1)S(1)} %convert_element_type.49.i0), channel_id=1, source_target_pairs={{0,6},{2,0},{4,2},{6,4},{8,10},{10,12},{12,14},{14,8},{16,22},{18,... | collective-permute-start | bytes 1327112 | tf_op jit(solution)/shard_map/ppermute | solution.py:62
  14.0 0.9 %collective-permute-start.3 = (bf16[192,1152]{1,0:T(8,128)(2,1)S(1)}, bf16[192,1152]{1,0:T(8,128)(2,1)S(1)}, u32[]{:S(2)}, u32[]{:S(2)}) collective-permute-start(bf16[192,1152]{1,0:T(8,128)(2,1)S(1)} %convert_element_type.49.i0), channel_id=1, source_target_pairs={{0,2},{2,4},{4,6},{6,0},{8,14},{10,8},{12,10},{14,12},{16,18},{18,... | collective-permute-start | bytes 1327112 | tf_op jit(solution)/shard_map/ppermute | solution.py:62
  16.3 16.2 %collective-permute-done.2.tb = bf16[192,1152]{1,0:T(8,128)(2,1)S(1)} collective-permute-done((bf16[192,1152]{1,0:T(8,128)(2,1)S(1)}, bf16[192,1152]{1,0:T(8,128)(2,1)S(1)}, u32[]{:S(2)}, u32[]{:S(2)}) %collective-permute-start.2) | collective-permute-done | bytes 442400 | tf_op jit(solution)/shard_map/ppermute | solution.py:62
  33.1 2.1 %shard_map.67 = (bf16[768,1152]{1,0:T(8,128)(2,1)S(1)}, bf16[384,1152]{1,0:T(8,128)(2,1)S(1)}, bf16[384,768]{1,0:T(8,128)(2,1)S(1)}, f32[8,128]{1,0:T(8,128)S(1)}) custom-call(f32[2]{0:T(128)S(1)} %pad_maximum_fusion.scalars, bf16[192,1152]{1,0:T(8,128)(2,1)S(1)} %convert_element_type.49.i0, bf16[192,1152]{1,0:T(8,128)(2,1)S(1)} %collective-permute-done.3.i1, ...), custom_call_target="tpu_custom_call" | custom-call | flops 679477248 | bytes 1048576 | tf_op jit(solution)/shard_map/pallas_call | solution.py:74
  35.7 5.2 %shard_map.68 = (bf16[768,1152]{1,0:T(8,128)(2,1)S(1)}, bf16[768,768]{1,0:T(8,128)(2,1)S(1)}, f32[192,1152]{1,0:T(8,128)S(1)}, f32[384,1152]{1,0:T(8,128)S(1)}, f32[8,128]{1,0:T(8,128)S(1)}) custom-call(f32[2]{0:T(128)S(1)} %pad_maximum_fusion.scalars, s32[1]{0:T(128)} %bitcast.core, bf16[768,1152]{1,0:T(8,128)(2,1)S(1)} %get-tuple-element.43.images, ...), custom_call_target="tpu_custom_call" | custom-call | flops 2717908992 | bytes 1048576 | tf_op jit(solution)/shard_map/pallas_call | solution.py:74
  41.7 1.6 %collective-permute-start.10 = (f16[192,1152]{1,0:T(8,128)(2,1)S(1)}, f16[192,1152]{1,0:T(8,128)(2,1)S(1)}, u32[]{:S(2)}, u32[]{:S(2)}) collective-permute-start(f16[192,1152]{1,0:T(8,128)(2,1)S(1)} %multiply_convert_fusion.2), channel_id=1, source_target_pairs={{0,2},{2,4},{4,6},{6,0},{8,14},{10,8},{12,10},{14,12},{16,18},{18,... | collective-permute-start | bytes 1327112 | tf_op jit(solution)/shard_map/ppermute | solution.py:62
  43.3 1.7 %shard_map.69 = (f32[192,1152]{1,0:T(8,128)S(1)}, f32[192,1152]{1,0:T(8,128)S(1)}, f32[384,1152]{1,0:T(8,128)S(1)}) custom-call(bf16[768,1152]{1,0:T(8,128)(2,1)S(1)} %get-tuple-element.43.images, bf16[384,768]{1,0:T(8,128)(2,1)S(1)} %get-tuple-element.54.w0, bf16[768,768]{1,0:T(8,128)(2,1)S(1)} %get-tuple-element.49.weights), custom_call_target="tpu_custom_call" | custom-call | flops 1358954496 | bytes 1048576 | tf_op jit(solution)/shard_map/pallas_call | solution.py:74
  45.3 1.2 %slice_add_fusion = (f32[192,1152]{1,0:T(8,128)S(1)}, f16[192,1152]{1,0:T(8,128)(2,1)}, f16[192,1152]{1,0:T(8,128)(2,1)}, f16[192,1152]{1,0:T(8,128)(2,1)}) fusion(f32[192,1152]{1,0:T(8,128)S(1)} %get-tuple-element.53, f32[384,1152]{1,0:T(8,128)S(1)} %get-tuple-element.78, f32[192,1152]{1,0:T(8,128)S(1)} %get-tuple-element.50, ...), kind=kLoop, calls=%fused_computation.4 | loop fusion | flops 1769472 | bytes 7520256 | tf_op jit(solution)/shard_map/add | solution.py:253
  46.5 1.2 %collective-permute-start.11 = (f16[192,1152]{1,0:T(8,128)(2,1)}, f16[192,1152]{1,0:T(8,128)(2,1)S(1)}, u32[]{:S(2)}, u32[]{:S(2)}) collective-permute-start(f16[192,1152]{1,0:T(8,128)(2,1)} %get-tuple-element.64), channel_id=1, source_target_pairs={{0,1},{2,3},{4,5},{6,7},{8,9},{10,11},{12,13},{14,15},{16,17},{18,... | collective-permute-start | bytes 1327112 | tf_op jit(solution)/shard_map/ppermute | solution.py:62
  47.8 2.5 %collective-permute-start.12 = (f16[192,1152]{1,0:T(8,128)(2,1)}, f16[192,1152]{1,0:T(8,128)(2,1)S(1)}, u32[]{:S(2)}, u32[]{:S(2)}) collective-permute-start(f16[192,1152]{1,0:T(8,128)(2,1)} %get-tuple-element.65), channel_id=1, source_target_pairs={{0,112},{2,114},{4,116},{6,118},{8,120},{10,122},{12,124},{14,126}... | collective-permute-start | bytes 1327112 | tf_op jit(solution)/shard_map/ppermute | solution.py:62
  50.3 1.5 %collective-permute-start.13 = (f16[192,1152]{1,0:T(8,128)(2,1)}, f16[192,1152]{1,0:T(8,128)(2,1)S(1)}, u32[]{:S(2)}, u32[]{:S(2)}) collective-permute-start(f16[192,1152]{1,0:T(8,128)(2,1)} %get-tuple-element.66), channel_id=1, source_target_pairs={{0,113},{2,115},{4,117},{6,119},{8,121},{10,123},{12,125},{14,127}... | collective-permute-start | bytes 1327112 | tf_op jit(solution)/shard_map/ppermute | solution.py:62
  51.8 2.7 %shard_map.70 = (f32[64,1,128]{2,1,0:T(1,128)}, f32[192,1152]{1,0:T(8,128)S(1)}, f32[192,1152]{1,0:T(8,128)S(1)}, f32[192,1152]{1,0:T(8,128)S(1)}) custom-call(bf16[384,768]{1,0:T(8,128)(2,1)S(1)} %get-tuple-element.54.w0, bf16[768,768]{1,0:T(8,128)(2,1)S(1)} %get-tuple-element.49.weights, bf16[384,1152]{1,0:T(8,128)(2,1)S(1)} %get-tuple-element.46.t0, ...), custom_call_target="tpu_custom_call" | custom-call | flops 1528823808 | bytes 1048576 | tf_op jit(solution)/shard_map/pallas_call | solution.py:74
  55.5 7.4 %all-to-all-start = ((f32[64,1,128]{2,1,0:T(1,128)}), f32[64,1,128]{2,1,0:T(1,128)}, u32[]{:S(2)}, u32[]{:S(2)}) async-start(f32[64,1,128]{2,1,0:T(1,128)} %get-tuple-element.61), calls=%async_computation | async-start | bytes 65536 | tf_op jit(solution)/shard_map/all_to_all | solution.py:272
  62.9 2.8 %collective-permute-start.14 = (f16[192,1152]{1,0:T(8,128)(2,1)}, f16[192,1152]{1,0:T(8,128)(2,1)S(1)}, u32[]{:S(2)}, u32[]{:S(2)}) collective-permute-start(f16[192,1152]{1,0:T(8,128)(2,1)} %multiply_convert_fusion.3), channel_id=1, source_target_pairs={{0,6},{2,0},{4,2},{6,4},{8,10},{10,12},{12,14},{14,8},{16,22},{18,... | collective-permute-start | bytes 1327112 | tf_op jit(solution)/shard_map/ppermute | solution.py:62
  65.7 5.3 %collective-permute-done.11 = f16[192,1152]{1,0:T(8,128)(2,1)S(1)} collective-permute-done((f16[192,1152]{1,0:T(8,128)(2,1)}, f16[192,1152]{1,0:T(8,128)(2,1)S(1)}, u32[]{:S(2)}, u32[]{:S(2)}) %collective-permute-start.11) | collective-permute-done | bytes 442400 | tf_op jit(solution)/shard_map/ppermute | solution.py:62
  71.0 2.0 %collective-permute-done.13 = f16[192,1152]{1,0:T(8,128)(2,1)S(1)} collective-permute-done((f16[192,1152]{1,0:T(8,128)(2,1)}, f16[192,1152]{1,0:T(8,128)(2,1)S(1)}, u32[]{:S(2)}, u32[]{:S(2)}) %collective-permute-start.13) | collective-permute-done | bytes 442400 | tf_op jit(solution)/shard_map/ppermute | solution.py:62
  73.0 1.2 %add_multiply_fusion.1 = f32[192,1152]{1,0:T(8,128)} fusion(f16[192,1152]{1,0:T(8,128)(2,1)S(1)} %collective-permute-done.13, f16[192,1152]{1,0:T(8,128)(2,1)S(1)} %collective-permute-done.12, f32[192,1152]{1,0:T(8,128)S(1)} %get-tuple-element.63, f16[192,1152]{1,0:T(8,128)(2,1)S(1)} %collective-permute-done.11, f32[]{:T(128)} %bitcast.2), kind=kLoop, calls=%fused_computation.14 | loop fusion | flops 2211840 | bytes 3096580 | tf_op jit(solution)/shard_map/mul | solution.py:273
  75.2 1.1 %add_multiply_fusion = f32[192,1152]{1,0:T(8,128)} fusion(f16[192,1152]{1,0:T(8,128)(2,1)S(1)} %collective-permute-done.15, f32[192,1152]{1,0:T(8,128)S(1)} %get-tuple-element.67, f16[192,1152]{1,0:T(8,128)(2,1)S(1)} %collective-permute-done.14, f32[]{:T(128)} %bitcast.3), kind=kLoop, calls=%fused_computation.13 | loop fusion | flops 1548288 | bytes 2654212 | tf_op jit(solution)/shard_map/mul | solution.py:275
  76.3 1.4 %shard_map.71 = f32[1]{0:T(128)} custom-call(f32[64,1,128]{2,1,0:T(1,128)} %all-to-all-done.parts), custom_call_target="tpu_custom_call" | custom-call | tf_op jit(solution)/shard_map/pallas_call | solution.py:278
  (29 shorter events, 4.7 us)
Async XLA Ops:
  0.6 9.1 %copy-start = (f32[192,1152]{1,0:T(8,128)S(1)}, f32[192,1152]{1,0:T(8,128)}, u32[]{:S(2)}) copy-start(f32[192,1152]{1,0:T(8,128)} %param.4) | copy-start | bytes 2654212
  1.9 1.9 %collective-permute-start = (bf16[192,1152]{1,0:T(8,128)(2,1)S(1)}, bf16[192,1152]{1,0:T(8,128)(2,1)S(1)}, u32[]{:S(2)}, u32[]{:S(2)}) collective-permute-start(bf16[192,1152]{1,0:T(8,128)(2,1)S(1)} %convert_element_type.48.ta), channel_id=1, source_target_pairs={{0,8},{2,10},{4,12},{6,14},{8,0},{10,2},{12,4},{14,6},{16,24},{18,... | collective-permute-start | bytes 1327112 | tf_op jit(solution)/shard_map/ppermute | solution.py:62
  4.1 28.5 %collective-permute-start.1 = (bf16[384,1152]{1,0:T(8,128)(2,1)S(1)}, bf16[384,1152]{1,0:T(8,128)(2,1)S(1)}, u32[]{:S(2)}, u32[]{:S(2)}) collective-permute-start(bf16[384,1152]{1,0:T(8,128)(2,1)S(1)} %maximum_select_fusion), channel_id=1, source_target_pairs={{0,16},{2,18},{4,20},{6,22},{8,25},{10,27},{12,29},{14,31},{16,32}... | collective-permute-start | bytes 2654216 | tf_op jit(solution)/shard_map/ppermute | solution.py:62
  6.1 26.4 %collective-permute-start.2 = (bf16[192,1152]{1,0:T(8,128)(2,1)S(1)}, bf16[192,1152]{1,0:T(8,128)(2,1)S(1)}, u32[]{:S(2)}, u32[]{:S(2)}) collective-permute-start(bf16[192,1152]{1,0:T(8,128)(2,1)S(1)} %convert_element_type.48.ta), channel_id=1, source_target_pairs={{0,1},{2,3},{4,5},{6,7},{8,9},{10,11},{12,13},{14,15},{16,17},{18,... | collective-permute-start | bytes 1327112 | tf_op jit(solution)/shard_map/ppermute | solution.py:62
  9.8 22.8 %collective-permute-start.5 = (bf16[192,1152]{1,0:T(8,128)(2,1)S(1)}, bf16[192,1152]{1,0:T(8,128)(2,1)S(1)}, u32[]{:S(2)}, u32[]{:S(2)}) collective-permute-start(bf16[192,1152]{1,0:T(8,128)(2,1)S(1)} %convert_element_type.49.i0), channel_id=1, source_target_pairs={{0,4},{2,6},{4,0},{6,2},{8,12},{10,14},{12,8},{14,10},{16,20},{18,... | collective-permute-start | bytes 1327112 | tf_op jit(solution)/shard_map/ppermute | solution.py:62
  12.9 19.7 %collective-permute-start.4 = (bf16[192,1152]{1,0:T(8,128)(2,1)S(1)}, bf16[192,1152]{1,0:T(8,128)(2,1)S(1)}, u32[]{:S(2)}, u32[]{:S(2)}) collective-permute-start(bf16[192,1152]{1,0:T(8,128)(2,1)S(1)} %convert_element_type.49.i0), channel_id=1, source_target_pairs={{0,6},{2,0},{4,2},{6,4},{8,10},{10,12},{12,14},{14,8},{16,22},{18,... | collective-permute-start | bytes 1327112 | tf_op jit(solution)/shard_map/ppermute | solution.py:62
  14.0 18.5 %collective-permute-start.3 = (bf16[192,1152]{1,0:T(8,128)(2,1)S(1)}, bf16[192,1152]{1,0:T(8,128)(2,1)S(1)}, u32[]{:S(2)}, u32[]{:S(2)}) collective-permute-start(bf16[192,1152]{1,0:T(8,128)(2,1)S(1)} %convert_element_type.49.i0), channel_id=1, source_target_pairs={{0,2},{2,4},{4,6},{6,0},{8,14},{10,8},{12,10},{14,12},{16,18},{18,... | collective-permute-start | bytes 1327112 | tf_op jit(solution)/shard_map/ppermute | solution.py:62
  32.6 3.1 %collective-permute-start.7 = (bf16[384,1152]{1,0:T(8,128)(2,1)S(1)}, bf16[384,1152]{1,0:T(8,128)(2,1)S(1)}, u32[]{:S(2)}, u32[]{:S(2)}) collective-permute-start(bf16[384,1152]{1,0:T(8,128)(2,1)S(1)} %collective-permute-done.1.far), channel_id=1, source_target_pairs={{0,8},{2,10},{4,12},{6,14},{8,0},{10,2},{12,4},{14,6},{16,24},{18,... | collective-permute-start | bytes 2654216 | tf_op jit(solution)/shard_map/ppermute | solution.py:62
  32.7 3.0 %collective-permute-start.6 = (bf16[192,1152]{1,0:T(8,128)(2,1)S(1)}, bf16[192,1152]{1,0:T(8,128)(2,1)S(1)}, u32[]{:S(2)}, u32[]{:S(2)}) collective-permute-start(bf16[192,1152]{1,0:T(8,128)(2,1)S(1)} %collective-permute-done.2.tb), channel_id=1, source_target_pairs={{0,8},{2,10},{4,12},{6,14},{8,0},{10,2},{12,4},{14,6},{16,24},{18,... | collective-permute-start | bytes 1327112 | tf_op jit(solution)/shard_map/ppermute | solution.py:62
  41.0 3.9 %collective-permute-start.8 = (f16[384,1152]{1,0:T(8,128)(2,1)S(1)}, f16[384,1152]{1,0:T(8,128)(2,1)S(1)}, u32[]{:S(2)}, u32[]{:S(2)}) collective-permute-start(f16[384,1152]{1,0:T(8,128)(2,1)S(1)} %multiply_convert_fusion), channel_id=1, source_target_pairs={{0,8},{2,10},{4,12},{6,14},{8,0},{10,2},{12,4},{14,6},{16,24},{18,... | collective-permute-start | bytes 2654216 | tf_op jit(solution)/shard_map/ppermute | solution.py:62
  41.3 10.6 %collective-permute-start.9 = (f32[8,128]{1,0:T(8,128)S(1)}, f32[8,128]{1,0:T(8,128)S(1)}, u32[]{:S(2)}, u32[]{:S(2)}) collective-permute-start(f32[8,128]{1,0:T(8,128)S(1)} %get-tuple-element.56.loss), channel_id=1, source_target_pairs={{0,8},{2,10},{4,12},{6,14},{8,0},{10,2},{12,4},{14,6},{16,24},{18,... | collective-permute-start | bytes 12296 | tf_op jit(solution)/shard_map/ppermute | solution.py:62
  41.7 12.8 %collective-permute-start.10 = (f16[192,1152]{1,0:T(8,128)(2,1)S(1)}, f16[192,1152]{1,0:T(8,128)(2,1)S(1)}, u32[]{:S(2)}, u32[]{:S(2)}) collective-permute-start(f16[192,1152]{1,0:T(8,128)(2,1)S(1)} %multiply_convert_fusion.2), channel_id=1, source_target_pairs={{0,2},{2,4},{4,6},{6,0},{8,14},{10,8},{12,10},{14,12},{16,18},{18,... | collective-permute-start | bytes 1327112 | tf_op jit(solution)/shard_map/ppermute | solution.py:62
  46.5 24.4 %collective-permute-start.11 = (f16[192,1152]{1,0:T(8,128)(2,1)}, f16[192,1152]{1,0:T(8,128)(2,1)S(1)}, u32[]{:S(2)}, u32[]{:S(2)}) collective-permute-start(f16[192,1152]{1,0:T(8,128)(2,1)} %get-tuple-element.64), channel_id=1, source_target_pairs={{0,1},{2,3},{4,5},{6,7},{8,9},{10,11},{12,13},{14,15},{16,17},{18,... | collective-permute-start | bytes 1327112 | tf_op jit(solution)/shard_map/ppermute | solution.py:62
  47.8 23.2 %collective-permute-start.12 = (f16[192,1152]{1,0:T(8,128)(2,1)}, f16[192,1152]{1,0:T(8,128)(2,1)S(1)}, u32[]{:S(2)}, u32[]{:S(2)}) collective-permute-start(f16[192,1152]{1,0:T(8,128)(2,1)} %get-tuple-element.65), channel_id=1, source_target_pairs={{0,112},{2,114},{4,116},{6,118},{8,120},{10,122},{12,124},{14,126}... | collective-permute-start | bytes 1327112 | tf_op jit(solution)/shard_map/ppermute | solution.py:62
  50.3 22.7 %collective-permute-start.13 = (f16[192,1152]{1,0:T(8,128)(2,1)}, f16[192,1152]{1,0:T(8,128)(2,1)S(1)}, u32[]{:S(2)}, u32[]{:S(2)}) collective-permute-start(f16[192,1152]{1,0:T(8,128)(2,1)} %get-tuple-element.66), channel_id=1, source_target_pairs={{0,113},{2,115},{4,117},{6,119},{8,121},{10,123},{12,125},{14,127}... | collective-permute-start | bytes 1327112 | tf_op jit(solution)/shard_map/ppermute | solution.py:62
  55.5 20.8 %all-to-all-start = ((f32[64,1,128]{2,1,0:T(1,128)}), f32[64,1,128]{2,1,0:T(1,128)}, u32[]{:S(2)}, u32[]{:S(2)}) async-start(f32[64,1,128]{2,1,0:T(1,128)} %get-tuple-element.61), calls=%async_computation | async-start | bytes 65536 | tf_op jit(solution)/shard_map/all_to_all | solution.py:272
  62.9 11.4 %collective-permute-start.14 = (f16[192,1152]{1,0:T(8,128)(2,1)}, f16[192,1152]{1,0:T(8,128)(2,1)S(1)}, u32[]{:S(2)}, u32[]{:S(2)}) collective-permute-start(f16[192,1152]{1,0:T(8,128)(2,1)} %multiply_convert_fusion.3), channel_id=1, source_target_pairs={{0,6},{2,0},{4,2},{6,4},{8,10},{10,12},{12,14},{14,8},{16,22},{18,... | collective-permute-start | bytes 1327112 | tf_op jit(solution)/shard_map/ppermute | solution.py:62
  65.7 9.5 %collective-permute-start.15 = (f16[192,1152]{1,0:T(8,128)(2,1)S(1)}, f16[192,1152]{1,0:T(8,128)(2,1)S(1)}, u32[]{:S(2)}, u32[]{:S(2)}) collective-permute-start(f16[192,1152]{1,0:T(8,128)(2,1)S(1)} %multiply_convert_fusion.1), channel_id=1, source_target_pairs={{0,2},{2,4},{4,6},{6,0},{8,14},{10,8},{12,10},{14,12},{16,18},{18,... | collective-permute-start | bytes 1327112 | tf_op jit(solution)/shard_map/ppermute | solution.py:62
